TPU v7x, 128 devices: a whole 4x4x4 slice. The times are simulated.
128 devices in a mesh: grp: 4 (over z_hi, core), wide: 32 (over y, z_lo, x).
Axes of the slice: x: 4, y: 4, z: 4 (z_hi: 2, z_lo: 2; z = z_hi * 2 + z_lo), core: 2. Of those that a mesh axis runs over, the one named last changes fastest.
Arguments:
- queries: bfloat16 [256, 32, 128], P(('grp', 'wide')), may hold values from -6 to 6
- centroids: bfloat16 [131072, 128], P('grp'), may hold values from -6 to 6
- codebook: bfloat16 [256, 128], replicated, may hold values from -4 to 4
- slot_codes: int32 [512, 4096], P('wide', 'grp'), may hold values from 0 to 255
- slot_centroid: int32 [512, 128], P('wide', 'grp'), may hold values from 0 to 131071, as said below
- lengths: int32 [512], P('wide'), may hold values from 1 to 128, 40960 in all
- candidates: int32 [256, 256], P(('grp', 'wide')), may hold values from 0 to 511, all different within a row
Outputs:
- scores: float32 [256, 256], P(('grp', 'wide'))
Inputs may be any that keep to these rules, and one draw needn't show every extreme that they name: `slot_centroid`: the centroid of slot j of any passage lies in [(j // 32) * 32768, (j // 32 + 1) * 32768). `candidates`: each row names 256 different passages.
All inputs are finite; a program needn't handle non-finite values. No bound on the sum of `lengths` on one device may be relied on, other than what follows from the above.
Results may differ from a plain program's by a relative error of at most 0.00034.
Values may be sent and summed in bfloat16 or wider, within the bound.
No kernel may reach another device: no remote copies, remote signals or barrier semaphores. Data moves between devices by JAX's collectives and lax.ppermute only.
A program may use at most 64 MiB of HBM per device.

v0:
```python
import math

import jax
import jax.numpy as jnp
from jax import lax
from jax.sharding import PartitionSpec as P


def unit_rows(values):
    wide32 = values.astype(jnp.float32)
    scale = lax.rsqrt(jnp.sum(wide32 * wide32, axis=-1, keepdims=True) + 1e-06)
    return (wide32 * scale).astype(jnp.bfloat16)


def decode_slots(slot_codes, slot_centroid, centroids, codebook, first_centroid):
    passages, slots = slot_centroid.shape
    count_codes, feature = codebook.shape
    subvecs = feature // 4
    total_rows = passages * slots
    code_rows = slot_codes.reshape(total_rows, subvecs)
    code_ids = jnp.arange(count_codes, dtype=jnp.int32)
    one_hot = (code_rows[:, :, None] == code_ids[None, None, :]).astype(jnp.bfloat16)
    code_parts = codebook.reshape(count_codes, subvecs, 4)
    residual = jnp.einsum(
        "rsk,ksc->rsc", one_hot, code_parts, preferred_element_type=jnp.float32
    ).reshape(total_rows, feature)
    row_ids = slot_centroid.reshape(total_rows) - first_centroid
    centre = jnp.take(centroids, row_ids, axis=0).astype(jnp.float32)
    return unit_rows(centre + residual).reshape(passages, slots, feature)


def token_maxima(passage_vecs, live_lengths, query_piece):
    count_rows, query_len, feature = query_piece.shape
    passages, slots, _ = passage_vecs.shape
    flat_tokens = passage_vecs.reshape(passages * slots, feature)
    live_mask = jnp.arange(slots, dtype=jnp.int32)[None, :] < live_lengths[:, None]
    group = math.gcd(count_rows, max(1, 65536 // (passages * slots)))

    def score_group(block):
        similar = lax.dot_general(
            block.reshape(group * query_len, feature),
            flat_tokens,
            (((1,), (1,)), ((), ())),
            preferred_element_type=jnp.float32,
        )
        similar = similar.reshape(group * query_len, passages, slots)
        best = jnp.max(jnp.where(live_mask[None], similar, -1e30), axis=2)
        return jnp.sum(best.reshape(group, query_len, passages), axis=1)

    grouped = query_piece.reshape(count_rows // group, group, query_len, feature)
    return lax.map(score_group, grouped).reshape(count_rows, passages)


def shards(queries, centroids, codebook, slot_codes, slot_centroid, lengths, candidates):
    grp_index = lax.axis_index("grp")
    first_centroid = grp_index * centroids.shape[0]
    query_vecs = unit_rows(queries)
    local_vecs = decode_slots(slot_codes, slot_centroid, centroids, codebook, first_centroid)
    wide_passages = lengths.shape[0]
    grp_count = lax.axis_size("grp")
    wide_count = lax.axis_size("wide")
    own_count = wide_passages // grp_count
    whole_vecs = lax.all_to_all(local_vecs, "grp", split_axis=0, concat_axis=1, tiled=True)
    own_lengths = lax.dynamic_slice_in_dim(lengths, grp_index * own_count, own_count)
    table = token_maxima(
        whole_vecs, own_lengths, lax.all_gather(query_vecs, ("grp", "wide"), axis=0, tiled=True)
    )
    owned = lax.all_to_all(table, ("grp", "wide"), split_axis=0, concat_axis=1, tiled=True)
    wide_part = candidates // wide_passages
    within = candidates % wide_passages
    grp_part = within // own_count
    position = (grp_part * wide_count + wide_part) * own_count + within % own_count
    return jnp.take_along_axis(owned, position, axis=1)


def solution(mesh):
    placed = (
        P(("grp", "wide"), None, None),
        P("grp", None),
        P(),
        P("wide", "grp"),
        P("wide", "grp"),
        P("wide"),
        P(("grp", "wide"), None),
    )
    return jax.shard_map(
        shards, mesh=mesh, in_specs=placed, out_specs=P(("grp", "wide"), None), check_vma=False
    )
```

profile of v0, /device:TPU:0, one launch (start us, length us, event | category | flops | bytes accessed | tf_op | source)
XLA Modules:
  0.0 350.3 jit_solution(7950720793716734927)
XLA Ops:
  6.5 0.0 all-gather.2.cloned.1.call-start
  6.5 0.8 fusion.5
  7.3 1.4 fusion.6
  8.8 0.0 all-gather.2.cloned.1.call-update
  8.8 0.7 compare_and_fusion
  9.5 0.1 sub.36
  9.6 0.1 sub.37
  9.7 5.5 %gather_fusion = bf16[512,128]{1,0:T(8,128)(2,1)S(1)} fusion(bf16[32768,128]{1,0:T(8,128)(2,1)} %param.10, s32[1024]{0:T(1024)S(1)} %pad_clamp_fusion), kind=kCustom, calls=%fused_computation | custom fusion | bytes 264192 | tf_op jit(solution)/shard_map/jit(_take)/gather | solution.py:28
  15.2 0.1 copy.31
  15.3 1.0 eq.18
  16.3 0.1 copy.29
  16.4 0.9 copy.30
  17.4 0.0 copy-start.1
  17.4 4.2 %multiply_reduce_fusion = (f32[512]{0:T(512)S(1)}, f32[512,32,4]{0,2,1:T(4,128)S(1)}) fusion(bf16[512,32,4]{0,2,1:T(4,128)(2,1)S(1)} %gather.14, pred[512]{0:T(512)(128)(4,1)S(1)} %compare_and_fusion.1, bf16[256,32,4]{0,2,1:T(4,128)(2,1)S(1)} %reshape.103, s32[512,32]{0,1:T(8,128)S(1)} %copy.29), kind=kOutput, calls=%fused_computation.12 | convolution fusion | flops 38075904 | bytes 526848 | tf_op jit(solution)/shard_map/rsk,ksc->rsc/dot_general | solution.py:24
  21.6 0.3 reshape.104
  21.9 0.1 rsqrt.21
  22.0 0.4 copy.28
  22.5 0.2 multiply_convert_fusion
  22.6 1.1 copy.32
  23.7 5.2 %all-to-all-start = ((bf16[16,32,128]{2,1,0:T(8,128)(2,1)}), bf16[16,32,128]{2,1,0:T(8,128)(2,1)S(1)}, u32[]{:S(2)}, u32[]{:S(2)}) async-start(bf16[16,32,128]{2,1,0:T(8,128)(2,1)} %copy.32), calls=%async_computation | async-start | bytes 262144 | tf_op jit(solution)/shard_map/all_to_all | solution.py:63
  29.0 0.0 copy-done.1
  29.0 0.1 dynamic_slice.7
  29.0 6.1 %all-to-all-done = bf16[16,32,128]{2,1,0:T(8,128)(2,1)S(1)} async-done(((bf16[16,32,128]{2,1,0:T(8,128)(2,1)}), bf16[16,32,128]{2,1,0:T(8,128)(2,1)S(1)}, u32[]{:S(2)}, u32[]{:S(2)}) %all-to-all-start) | async-done | bytes 131104 | tf_op jit(solution)/shard_map/all_to_all | solution.py:63
  35.2 276.3 %all-gather.2.cloned.1.call-done = bf16[256,32,128]{2,1,0:T(8,128)(2,1)} async-done(((bf16[2,32,128]{2,1,0:T(8,128)(2,1)}), bf16[256,32,128]{2,1,0:T(8,128)(2,1)}) %all-gather.2.cloned.1.call-update) | async-done | bytes 2097168 | tf_op jit(solution)/shard_map/all_gather | solution.py:66
  311.4 0.0 copy-start
  311.4 6.0 %while.11 = (s32[]{:T(128)}, f32[2,128,4]{1,2,0:T(4,128)S(1)}, bf16[2,128,32,128]{3,2,1,0:T(8,128)(2,1)}, bf16[512,128]{1,0:T(8,128)(2,1)S(1)}, s32[4]{0:T(128)S(1)}, /*index=5*/s32[]{:T(128)}, f32[]{:T(128)}) while((s32[]{:T(128)}, f32[2,128,4]{1,2,0:T(4,128)S(1)}, bf16[2,128,32,128]{3,2,1,0:T(8,128)(2,1)}, ...), condition=%wide.region_5.6_spmd.clone, body=%wide.region_2.0_spmd.clone.sunk | while | flops 541065216 | bytes 3546217 | solution.py:51
  311.4 1.3 constant_dynamic-slice_fusion.2
  312.8 0.1 iota_compare_fusion.6
  312.8 1.3 select_reduce_fusion.2
  314.1 0.1 reshape.130
  314.3 0.1 reduce_sum.33
  314.4 1.3 constant_dynamic-slice_fusion.2
  315.7 0.1 iota_compare_fusion.6
  315.8 1.3 select_reduce_fusion.2
  317.1 0.1 reshape.130
  317.2 0.1 reduce_sum.33
  317.4 0.8 copy.34
  318.2 10.0 %all-to-all-start.1 = ((f32[128,2,4]{2,1,0:T(2,128)}), f32[128,2,4]{2,1,0:T(2,128)S(1)}, u32[]{:S(2)}, u32[]{:S(2)}) async-start(f32[128,2,4]{2,1,0:T(2,128)} %bitcast.7), calls=%async_computation.1 | async-start | bytes 262144 | tf_op jit(solution)/shard_map/all_to_all | solution.py:68
  328.2 0.0 copy-done
  328.3 9.6 %all-to-all-done.1 = f32[128,2,4]{2,1,0:T(2,128)S(1)} async-done(((f32[128,2,4]{2,1,0:T(2,128)}), f32[128,2,4]{2,1,0:T(2,128)S(1)}, u32[]{:S(2)}, u32[]{:S(2)}) %all-to-all-start.1) | async-done | bytes 4128 | tf_op jit(solution)/shard_map/all_to_all | solution.py:68
  337.9 0.1 all_to_all.31
  338.0 4.8 %gather_fusion.1 = f32[512]{0:T(512)S(1)} fusion(f32[2,512]{1,0:T(2,128)S(1)} %all_to_all.31, s32[512]{0:T(512)S(1)} %bitcast.46), kind=kCustom, calls=%fused_computation.1 | custom fusion | bytes 8192 | tf_op jit(solution)/shard_map/jit(take_along_axis)/gather | solution.py:73
  342.8 0.6 and_select_fusion
  (15 shorter events, 0.2 us)
Async XLA Ops:
  6.5 304.9 %all-gather.2.cloned.1.call-start = ((), (), s32[]{:S(2)}) async-start(), calls=%async_computation.2 | async-start | bytes 2113536 | tf_op jit(solution)/shard_map/all_gather | solution.py:66
  17.4 11.6 %copy-start.1 = (s32[16]{0:T(128)S(1)}, s32[16]{0:T(128)}, u32[]{:S(2)}) copy-start(s32[16]{0:T(128)} %param.14) | copy-start | bytes 196
  23.7 11.4 %all-to-all-start = ((bf16[16,32,128]{2,1,0:T(8,128)(2,1)}), bf16[16,32,128]{2,1,0:T(8,128)(2,1)S(1)}, u32[]{:S(2)}, u32[]{:S(2)}) async-start(bf16[16,32,128]{2,1,0:T(8,128)(2,1)} %copy.32), calls=%async_computation | async-start | bytes 262144 | tf_op jit(solution)/shard_map/all_to_all | solution.py:63
  311.4 16.8 %copy-start = (s32[2,256]{1,0:T(2,128)S(1)}, s32[2,256]{1,0:T(2,128)}, u32[]{:S(2)}) copy-start(s32[2,256]{1,0:T(2,128)} %param.15) | copy-start | bytes 6148
  318.2 19.7 %all-to-all-start.1 = ((f32[128,2,4]{2,1,0:T(2,128)}), f32[128,2,4]{2,1,0:T(2,128)S(1)}, u32[]{:S(2)}, u32[]{:S(2)}) async-start(f32[128,2,4]{2,1,0:T(2,128)} %bitcast.7), calls=%async_computation.1 | async-start | bytes 262144 | tf_op jit(solution)/shard_map/all_to_all | solution.py:68
Sparse Core Ops, SparseCore 0:
  9.0 302.3 all-gather.1
where the time goes:
time: 351 us; the launch traced here: 350 us
  waiting for transfers between devices  292 us (83%)
  local copies, waits for them, and re-layouts  18.5 us (5%)
  starting transfers between devices  15.3 us (4%)
  between operations  13.5 us (4%)
  matrix products  6.79 us (2%)
  other arithmetic  4.16 us (1%)
    all_gather x1, waiting for transfers between devices, shards(): lax.all_gather(query_vecs, ('grp', 'wide'), axis=0, tiled=True)  276 us
    all_to_all x1, starting transfers between devices, shards(): lax.all_to_all(table, ('grp', 'wide'), split_axis=0, concat_axis=1, tiled...  10 us
    all_to_all x1, waiting for transfers between devices, shards(): lax.all_to_all(table, ('grp', 'wide'), split_axis=0, concat_axis=1, tiled...  9.55 us
  transfers between devices with their start and end apart: 3, of which 3 were waited for; matrix products, arithmetic and copies ran while one was open for 4% of the time, Pallas kernels for 0%

commit v1 on v0

v1 whole, which is shorter than its diff:
```python
import functools

import jax
import jax.numpy as jnp
from jax import lax
from jax.experimental import pallas as pl
from jax.experimental.pallas import tpu as pltpu
from jax.sharding import PartitionSpec as P

SLAB = 16
LANES = 128
NT = (((1,), (1,)), ((), ()))


def unit(values):
    scale = lax.rsqrt(jnp.sum(values * values, axis=-1, keepdims=True) + 1e-06)
    return (values * scale).astype(jnp.bfloat16)


def decode_kernel(ids_smem, ids_ref, codes_ref, codebook_ref, centroids_ref, out_ref, slabs, sem):
    passages, slots = ids_ref.shape
    rows = passages * slots
    per_tile = 4
    tiles = slots // per_tile
    count = centroids_ref.shape[0]

    def start_passage(p, carry):
        for j in range(slots):
            row = (j % per_tile) * tiles * passages + (j // per_tile) * passages + p
            local = ids_smem[p, j] & (count - 1)
            base = pl.multiple_of(local & ~(SLAB - 1), SLAB)
            pltpu.make_async_copy(
                centroids_ref.at[pl.ds(base, SLAB), :], slabs.at[pl.ds(row * SLAB, SLAB), :], sem
            ).start()
        return carry

    lax.fori_loop(0, passages, start_passage, 0)

    table = codebook_ref[...].astype(jnp.float32)
    low, high = table[:LANES].T, table[LANES:].T
    codes = codes_ref[...].astype(jnp.float32).astype(jnp.bfloat16)
    stacked = jnp.concatenate(
        [codes[:, c * LANES : (c + 1) * LANES] for c in range(tiles)], axis=0
    )
    feature = lax.broadcasted_iota(jnp.int32, (LANES, LANES), 0)
    lane = lax.broadcasted_iota(jnp.int32, (LANES, LANES), 1)
    residuals = []
    for jj in range(per_tile):
        spread = (lane == jj * 32 + feature // 4).astype(jnp.float32).astype(jnp.bfloat16)
        index = lax.dot_general(spread, stacked, NT, preferred_element_type=jnp.float32)
        index = index.astype(jnp.int32)
        within = index & (LANES - 1)
        parts = []
        for s in range(0, LANES, 8):
            w = within[s : s + 8]
            first = jnp.take_along_axis(low[s : s + 8], w, axis=1)
            second = jnp.take_along_axis(high[s : s + 8], w, axis=1)
            parts.append(jnp.where(index[s : s + 8] < LANES, first, second))
        residuals.append(jnp.concatenate(parts, axis=0).T)

    pltpu.make_async_copy(centroids_ref.at[pl.ds(0, rows * SLAB), :], slabs, sem).wait()

    span = passages * SLAB
    column = lax.broadcasted_iota(jnp.int32, (passages, span), 1)
    first_row = lax.broadcasted_iota(jnp.int32, (passages, span), 0) * SLAB
    ids = ids_ref[...] & (SLAB - 1)
    for jj in range(per_tile):
        for c in range(tiles):
            j = c * per_tile + jj
            block = jj * tiles + c
            pick = (column == first_row + ids[:, j : j + 1]).astype(jnp.float32).astype(jnp.bfloat16)
            centre = jnp.dot(
                pick, slabs[block * span : (block + 1) * span, :], preferred_element_type=jnp.float32
            )
            raw = centre + residuals[jj][c * passages : (c + 1) * passages]
            out_ref[block * passages : (block + 1) * passages, :] = unit(raw)


def decode(slot_centroid, slot_codes, codebook, centroids):
    passages, slots = slot_centroid.shape
    rows, feature = passages * slots, codebook.shape[1]
    vmem = pl.BlockSpec(memory_space=pltpu.VMEM)
    return pl.pallas_call(
        decode_kernel,
        out_shape=jax.ShapeDtypeStruct((rows, feature), jnp.bfloat16),
        in_specs=[
            pl.BlockSpec(memory_space=pltpu.SMEM),
            vmem,
            vmem,
            vmem,
            pl.BlockSpec(memory_space=pl.ANY),
        ],
        out_specs=vmem,
        scratch_shapes=[
            pltpu.VMEM((rows * SLAB, feature), jnp.bfloat16),
            pltpu.SemaphoreType.DMA,
        ],
        compiler_params=pltpu.CompilerParams(vmem_limit_bytes=16 << 20),
        cost_estimate=pl.CostEstimate(
            flops=2 * rows * 256 * feature, bytes_accessed=rows * SLAB * 256, transcendentals=rows
        ),
        name="decode",
    )(slot_centroid, slot_centroid, slot_codes, codebook, centroids)


def score_kernel(per_tile, lengths_ref, queries_ref, vecs_ref, out_ref, unit_queries, live):
    blocks, rows, feature = vecs_ref.shape
    passages = lengths_ref.shape[0]
    slots = rows // passages
    tiles = slots // per_tile
    tokens = queries_ref.shape[0]
    owners = out_ref.shape[0]
    query_len = 32
    own = tokens // query_len // owners

    unit_queries[...] = unit(queries_ref[...].astype(jnp.float32))
    lengths = lengths_ref[...]
    first = vecs_ref[0, 0:passages, :]
    for b in range(blocks):
        for m in range(slots):
            j = b * slots + (m % tiles) * per_tile + m // tiles
            rows_here = vecs_ref[b, m * passages : (m + 1) * passages, :]
            if j:
                rows_here = jnp.where(lengths > j, rows_here, first)
            at = b * rows + m * passages
            live[at : at + passages, :] = rows_here

    chunk, span = 256, 256
    total = blocks * rows
    here = chunk // query_len
    segment = (
        lax.broadcasted_iota(jnp.int32, (here, chunk), 1) // query_len
        == lax.broadcasted_iota(jnp.int32, (here, chunk), 0)
    ).astype(jnp.float32)
    for k in range(tokens // chunk):
        wanted = unit_queries[k * chunk : (k + 1) * chunk, :]
        best = None
        for s in range(0, total, span):
            similar = lax.dot_general(
                live[s : s + span, :], wanted, NT, preferred_element_type=jnp.float32
            )
            top = jnp.max(similar.reshape(span // passages, passages, chunk), axis=0)
            best = top if best is None else jnp.maximum(best, top)
        scored = lax.dot_general(
            segment, best, NT, preferred_element_type=jnp.float32, precision=lax.Precision.HIGHEST
        )
        for i in range(here // own):
            out_ref[k * (here // own) + i, 0:own, 0:passages] = scored[i * own : (i + 1) * own]


def score(lengths, queries, vecs, owners, per_tile):
    blocks, rows, feature = vecs.shape
    tokens = queries.shape[0]
    vmem = pl.BlockSpec(memory_space=pltpu.VMEM)
    return pl.pallas_call(
        functools.partial(score_kernel, per_tile),
        out_shape=jax.ShapeDtypeStruct((owners, 8, LANES), jnp.float32),
        in_specs=[vmem, vmem, vmem],
        out_specs=vmem,
        scratch_shapes=[
            pltpu.VMEM((tokens, feature), jnp.bfloat16),
            pltpu.VMEM((blocks * rows, feature), jnp.bfloat16),
        ],
        compiler_params=pltpu.CompilerParams(vmem_limit_bytes=32 << 20),
        cost_estimate=pl.CostEstimate(
            flops=2 * tokens * blocks * rows * feature,
            bytes_accessed=(tokens + blocks * rows) * feature * 2,
            transcendentals=tokens,
        ),
        name="score",
    )(lengths, queries, vecs)


def pick_kernel(passages, owned_ref, candidates_ref, out_ref):
    owners = owned_ref.shape[0]
    count, wanted = candidates_ref.shape
    rows = lax.broadcasted_iota(jnp.int32, (owners, LANES), 0)
    for q in range(count):
        held = owned_ref[:, q, :]
        for c in range(0, wanted, LANES):
            ids = candidates_ref[q : q + 1, c : c + LANES]
            lane = jnp.broadcast_to(ids % passages, (owners, LANES))
            part = jnp.broadcast_to(ids // passages, (owners, LANES))
            found = jnp.take_along_axis(held, lane, axis=1)
            out_ref[q : q + 1, c : c + LANES] = jnp.sum(
                jnp.where(rows == part, found, 0.0), axis=0, keepdims=True
            )


def pick(owned, candidates, passages):
    vmem = pl.BlockSpec(memory_space=pltpu.VMEM)
    return pl.pallas_call(
        functools.partial(pick_kernel, passages),
        out_shape=jax.ShapeDtypeStruct(candidates.shape, jnp.float32),
        in_specs=[vmem, vmem],
        out_specs=vmem,
        name="pick",
    )(owned, candidates)


def shards(queries, centroids, codebook, slot_codes, slot_centroid, lengths, candidates):
    own, query_len, feature = queries.shape
    owners = lax.axis_size("wide")
    passages = lengths.shape[0]
    sent = jnp.broadcast_to(queries.reshape(1, own * query_len, feature), (owners, own * query_len, feature))
    gathered = lax.all_to_all(sent, "wide", split_axis=0, concat_axis=0, tiled=True)
    vecs = decode(slot_centroid, slot_codes, codebook, centroids)
    whole = lax.all_gather(vecs, "grp")
    table = score(
        lengths.reshape(passages, 1), gathered.reshape(owners * own * query_len, feature), whole, owners, 4
    )
    owned = lax.all_to_all(table, "wide", split_axis=0, concat_axis=0, tiled=True)
    return pick(owned, candidates, passages)


def solution(mesh):
    placed = (
        P(("grp", "wide"), None, None),
        P("grp", None),
        P(),
        P("wide", "grp"),
        P("wide", "grp"),
        P("wide"),
        P(("grp", "wide"), None),
    )
    return jax.shard_map(
        shards, mesh=mesh, in_specs=placed, out_specs=P(("grp", "wide"), None), check_vma=False
    )
```

time: 351 us -> 57.7 us (0.16)
  waiting for transfers between devices: 292 us -> 0.01 us
  blocking collectives: 0 us -> 25.6 us
  Pallas kernels: 0 us -> 14.7 us
  between operations: 13.5 us -> 0.02 us
  local copies, waits for them, and re-layouts: 18.5 us -> 8.11 us
  matrix products: 6.79 us -> 0 us
  starting transfers between devices: 15.3 us -> 8.76 us
  other arithmetic: 4.16 us -> 0 us
    all_gather x1 -> x0, waiting for transfers between devices: 276 us -> none  [shards(): lax.all_gather(query_vecs, ('grp', 'wide'), axis=0, tiled=True)]
    all_to_all x0 -> x1, blocking collectives: none -> 16.3 us  [shards(): lax.all_to_all(table, 'wide', split_axis=0, concat_axis=0, tiled=True)]
    all_to_all x2 -> x1, waiting for transfers between devices: 15.7 us -> 0.01 us  [shards(): lax.all_to_all(sent, 'wide', split_axis=0, concat_axis=0, tiled=True)]
    pallas_call x0 -> x3, Pallas kernels: none -> 14.7 us  [the longest x1 9.1 us: decode(): pl.pallas_call(decode_kernel, out_shape=jax.ShapeDtypeStruct((rows, featu...]
    gather x6 -> x0, local copies, waits for them, and re-layouts: 11 us -> none  [the longest x4 6.11 us: decode_slots(): centre = jnp.take(centroids, row_ids, axis=0).astype(jnp.float32)]
    all_gather x0 -> x1, blocking collectives: none -> 9.26 us  [shards(): whole = lax.all_gather(vecs, 'grp')]
    dot_general x3 -> x0, matrix products: 6.79 us -> none  [the longest x1 4.2 us: decode_slots(): jnp.einsum('rsk,ksc->rsc', one_hot, code_parts, preferred_element_type=jn...]
    all_to_all x2 -> x1, starting transfers between devices: 15.3 us -> 8.76 us  [shards(): lax.all_to_all(sent, 'wide', split_axis=0, concat_axis=0, tiled=True)]
  transfers between devices with their start and end apart: 3 -> 1, of which waited for: 3 -> 0; matrix products, arithmetic and copies ran while one was open for 4% -> 1% of each run, Pallas kernels for 0% -> 16%
where the time goes in v1:
time: 57.7 us; the launch traced here: 57.2 us
  blocking collectives  25.6 us (44%)
  Pallas kernels  14.7 us (25%)
  starting transfers between devices  8.76 us (15%)
  local copies, waits for them, and re-layouts  8.11 us (14%)
    all_to_all x1, blocking collectives, shards(): lax.all_to_all(table, 'wide', split_axis=0, concat_axis=0, tiled=True)  16.3 us
    all_gather x1, blocking collectives, shards(): whole = lax.all_gather(vecs, 'grp')  9.26 us
    pallas_call x1, Pallas kernels, decode(): pl.pallas_call(decode_kernel, out_shape=jax.ShapeDtypeStruct((rows, featu...  9.1 us
    all_to_all x1, starting transfers between devices, shards(): lax.all_to_all(sent, 'wide', split_axis=0, concat_axis=0, tiled=True)  8.76 us
    unnamed x8, local copies, waits for them, and re-layouts  5.76 us
    pallas_call x1, Pallas kernels, score(): pl.pallas_call(functools.partial(score_kernel, per_tile), out_shape=jax.S...  3.99 us
    broadcast_in_dim x1, local copies, waits for them, and re-layouts, shards(): jnp.broadcast_to(queries.reshape(1, own * query_len, feature), (owners, o...  1.62 us
    pallas_call x1, Pallas kernels, pick(): pl.pallas_call(functools.partial(pick_kernel, passages), out_shape=jax.Sh...  1.61 us
  transfers between devices with their start and end apart: 1, of which 0 were waited for; matrix products, arithmetic and copies ran while one was open for 1% of the time, Pallas kernels for 16%

profile of v1, /device:TPU:0, one launch (start us, length us, event | category | flops | bytes accessed | tf_op | source)
XLA Modules:
  0.0 57.2 jit_solution(8613178142865169821)
XLA Ops:
  0.0 1.6 %broadcast_in_dim.8 = bf16[32,64,128]{2,1,0:T(8,128)(2,1)} broadcast(bf16[64,128]{1,0:T(8,128)(2,1)} %bitcast.6), dimensions={1,2} | broadcast | bytes 540672 | tf_op jit(solution)/shard_map/broadcast_in_dim | solution.py:205
  1.6 8.8 %all-to-all-start = ((bf16[32,64,128]{2,1,0:T(8,128)(2,1)}), bf16[32,64,128]{2,1,0:T(8,128)(2,1)S(1)}, u32[]{:S(2)}, u32[]{:S(2)}) async-start(bf16[32,64,128]{2,1,0:T(8,128)(2,1)} %broadcast_in_dim.8), calls=%async_computation | async-start | bytes 1048576 | tf_op jit(solution)/shard_map/all_to_all | solution.py:206
  10.4 0.7 %copy.8.lengths_ref = s32[16,1]{1,0:T(8,128)S(1)} copy(s32[16,1]{0,1:T(1,128)} %bitcast.7) | data formatting | bytes 128 | tf_op jit(solution)/shard_map/reshape | solution.py:210
  11.1 0.0 copy-start
  11.1 3.4 %copy-done = bf16[32768,128]{1,0:T(8,128)(2,1)S(1)} copy-done((bf16[32768,128]{1,0:T(8,128)(2,1)S(1)}, bf16[32768,128]{1,0:T(8,128)(2,1)}, u32[]{:S(2)}) %copy-start) | copy-done | bytes 8388632
  14.5 0.0 copy-start.1
  14.5 0.8 %copy-done.1 = s32[16,1024]{1,0:T(8,128)S(1)} copy-done((s32[16,1024]{1,0:T(8,128)S(1)}, s32[16,1024]{1,0:T(8,128)}, u32[]{:S(2)}) %copy-start.1) | copy-done | bytes 65560
  15.3 0.0 copy-start.2
  15.3 0.8 %copy-done.2 = bf16[256,128]{1,0:T(8,128)(2,1)S(1)} copy-done((bf16[256,128]{1,0:T(8,128)(2,1)S(1)}, bf16[256,128]{1,0:T(8,128)(2,1)}, u32[]{:S(2)}) %copy-start.2) | copy-done | bytes 65560
  16.2 0.0 copy-start.3
  16.2 0.7 %copy-done.3 = s32[16,32]{1,0:T(8,128)S(1)} copy-done((s32[16,32]{1,0:T(8,128)S(1)}, s32[16,32]{1,0:T(8,128)}, u32[]{:S(2)}) %copy-start.3) | copy-done | bytes 2072
  16.9 9.1 %decode.1 = bf16[512,128]{1,0:T(8,128)(2,1)S(1)} custom-call(s32[16,32]{1,0:T(8,128)S(1)} %copy-done.3, s32[16,32]{1,0:T(8,128)S(1)} %copy-done.3, s32[16,1024]{1,0:T(8,128)S(1)} %copy-done.1, bf16[256,128]{1,0:T(8,128)(2,1)S(1)} %copy-done.2, bf16[32768,128]{1,0:T(8,128)(2,1)S(1)} %copy-done), custom_call_target="tpu_custom_call" | custom-call | flops 33554432 | bytes 2097152 | tf_op jit(solution)/shard_map/decode/pallas_call | solution.py:83
  26.0 9.3 %all-gather = bf16[2048,128]{1,0:T(8,128)(2,1)S(1)} all-gather(bf16[512,128]{1,0:T(8,128)(2,1)S(1)} %decode.1), channel_id=2, replica_groups=mesh['grp'=4,'wide'=32] {'grp'}, dimensions={0}, use_global_device_ids=true | all-gather | bytes 655360 | tf_op jit(solution)/shard_map/all_gather | solution.py:208
  35.3 0.0 all-to-all-done
  35.3 4.0 %score.1 = f32[32,8,128]{2,1,0:T(8,128)S(1)} custom-call(s32[16,1]{1,0:T(8,128)S(1)} %copy.8.lengths_ref, bf16[2048,128]{1,0:T(8,128)(2,1)S(1)} %bitcast.5, bf16[4,512,128]{2,1,0:T(8,128)(2,1)S(1)} %bitcast.4), custom_call_target="tpu_custom_call" | custom-call | flops 1073741824 | bytes 1048576 | tf_op jit(solution)/shard_map/score/pallas_call | solution.py:155
  39.3 16.3 %all_to_all.10.owned_ref = f32[32,8,128]{2,1,0:T(8,128)} all-to-all(f32[32,8,128]{2,1,0:T(8,128)S(1)} %score.1), channel_id=1, replica_groups=mesh['grp'=4,'wide'=32] {'wide'}, dimensions={0} | all-to-all | bytes 262144 | tf_op jit(solution)/shard_map/all_to_all | solution.py:212
  55.6 1.6 %pick.1 = f32[2,256]{1,0:T(2,128)} custom-call(f32[32,8,128]{2,1,0:T(8,128)} %all_to_all.10.owned_ref, s32[2,256]{1,0:T(2,128)} %candidates_ref.1), custom_call_target="tpu_custom_call" | custom-call | tf_op jit(solution)/shard_map/pick/pallas_call | solution.py:192
Async XLA Ops:
  1.6 33.6 %all-to-all-start = ((bf16[32,64,128]{2,1,0:T(8,128)(2,1)}), bf16[32,64,128]{2,1,0:T(8,128)(2,1)S(1)}, u32[]{:S(2)}, u32[]{:S(2)}) async-start(bf16[32,64,128]{2,1,0:T(8,128)(2,1)} %broadcast_in_dim.8), calls=%async_computation | async-start | bytes 1048576 | tf_op jit(solution)/shard_map/all_to_all | solution.py:206
  11.1 3.4 %copy-start = (bf16[32768,128]{1,0:T(8,128)(2,1)S(1)}, bf16[32768,128]{1,0:T(8,128)(2,1)}, u32[]{:S(2)}) copy-start(bf16[32768,128]{1,0:T(8,128)(2,1)} %centroids_ref.1) | copy-start | bytes 25165828
  14.5 0.8 %copy-start.1 = (s32[16,1024]{1,0:T(8,128)S(1)}, s32[16,1024]{1,0:T(8,128)}, u32[]{:S(2)}) copy-start(s32[16,1024]{1,0:T(8,128)} %codes_ref.1) | copy-start | bytes 196612
  15.3 0.8 %copy-start.2 = (bf16[256,128]{1,0:T(8,128)(2,1)S(1)}, bf16[256,128]{1,0:T(8,128)(2,1)}, u32[]{:S(2)}) copy-start(bf16[256,128]{1,0:T(8,128)(2,1)} %codebook_ref.1) | copy-start | bytes 196612
  16.2 0.7 %copy-start.3 = (s32[16,32]{1,0:T(8,128)S(1)}, s32[16,32]{1,0:T(8,128)}, u32[]{:S(2)}) copy-start(s32[16,32]{1,0:T(8,128)} %ids_ref.1) | copy-start | bytes 6148

commit v2 on v0

v2 whole, which is shorter than its diff:
```python
import functools

import jax
import jax.numpy as jnp
from jax import lax
from jax.experimental import pallas as pl
from jax.experimental.pallas import tpu as pltpu
from jax.sharding import PartitionSpec as P

SLAB = 16
LANES = 128
PER_TILE = 4
PIECES = 4
LOWEST = -1e30
NT = (((1,), (1,)), ((), ()))
VMEM = pl.BlockSpec(memory_space=pltpu.VMEM)
ANY = pl.BlockSpec(memory_space=pl.ANY)


def unit(values):
    scale = lax.rsqrt(jnp.sum(values * values, axis=-1, keepdims=True) + 1e-06)
    return (values * scale).astype(jnp.bfloat16)


def spread_kernel(queries_ref, out_ref):
    held = queries_ref[...]
    for i in range(out_ref.shape[0]):
        out_ref[i] = held


def spread(queries, owners):
    return pl.pallas_call(
        spread_kernel,
        out_shape=jax.ShapeDtypeStruct((owners, *queries.shape), queries.dtype),
        in_specs=[VMEM],
        out_specs=VMEM,
        compiler_params=params(4),
        cost_estimate=pl.CostEstimate(flops=20000000000, bytes_accessed=1000000, transcendentals=0),
        name="spread",
    )(queries)


def residual_rows(codes, codebook, store):
    tiles = codes.shape[1] // LANES
    table = codebook.astype(jnp.float32)
    low, high = table[:LANES].T, table[LANES:].T
    codes = codes.astype(jnp.float32).astype(jnp.bfloat16)
    stacked = jnp.concatenate(
        [codes[:, c * LANES : (c + 1) * LANES] for c in range(tiles)], axis=0
    )
    feature = lax.broadcasted_iota(jnp.int32, (LANES, LANES), 0)
    lane = lax.broadcasted_iota(jnp.int32, (LANES, LANES), 1)
    for jj in range(PER_TILE):
        pattern = (lane == jj * 32 + feature // 4).astype(jnp.float32).astype(jnp.bfloat16)
        index = lax.dot_general(pattern, stacked, NT, preferred_element_type=jnp.float32)
        index = index.astype(jnp.int32)
        within = index & (LANES - 1)
        parts = []
        for s in range(0, LANES, 8):
            w = within[s : s + 8]
            first = jnp.take_along_axis(low[s : s + 8], w, axis=1)
            second = jnp.take_along_axis(high[s : s + 8], w, axis=1)
            parts.append(jnp.where(index[s : s + 8] < LANES, first, second))
        store(jj, jnp.concatenate(parts, axis=0).T)


def decode_kernel(
    ids_hbm, lengths_hbm, codes_hbm, book_hbm, cent_hbm, out_ref, live_ref,
    ids, lengths, codes, book, table, residual, sems,
):
    passages, slots = ids.shape
    tiles = slots // PER_TILE
    count = table.shape[0]
    copies = [
        pltpu.make_async_copy(source, target, sems.at[i])
        for i, (source, target) in enumerate(
            [(codes_hbm, codes), (book_hbm, book), (ids_hbm, ids), (lengths_hbm, lengths)]
        )
    ]
    piece = count // PIECES
    for i in range(PIECES):
        part = pl.ds(i * piece, piece)
        copies.append(pltpu.make_async_copy(cent_hbm.at[part, :], table.at[part, :], sems.at[4 + i]))
    for copy in copies:
        copy.start()
    for copy in copies[:4]:
        copy.wait()

    row = lax.broadcasted_iota(jnp.int32, (passages, LANES), 0)
    live = jnp.zeros((passages, LANES), jnp.int32)
    for p in range(passages):
        live = jnp.where(row == p, lengths[p], live)
    live_ref[...] = live

    def store(jj, rows):
        residual[jj * LANES : (jj + 1) * LANES, :] = rows

    residual_rows(codes[...], book[...], store)
    for copy in copies[4:]:
        copy.wait()

    sublane = lax.broadcasted_iota(jnp.int32, (8, LANES), 0)

    def gather(m, carry):
        j = (m % tiles) * PER_TILE + m // tiles
        halves = []
        for h in range(0, passages, 8):
            held = jnp.zeros((8, LANES), jnp.float32)
            for q in range(8):
                local = ids[h + q, j] & (count - 1)
                base = pl.multiple_of(local & ~(SLAB - 1), SLAB)
                slab = table[pl.ds(base, SLAB), :].astype(jnp.float32)
                within = local & (SLAB - 1)
                half = jnp.where(within >= 8, slab[8:], slab[:8])
                held = jnp.where(sublane == q, pltpu.roll(half, (q - within) & 7, 0), held)
            halves.append(held)
        at = pl.multiple_of(m * passages, passages)
        raw = jnp.concatenate(halves, axis=0) + residual[pl.ds(at, passages), :]
        out_ref[pl.ds(at, passages), :] = unit(raw)
        return carry

    lax.fori_loop(0, slots, gather, 0, unroll=8)


def decode(slot_centroid, lengths, slot_codes, codebook, centroids):
    passages, slots = slot_centroid.shape
    rows, feature = passages * slots, codebook.shape[1]
    return pl.pallas_call(
        decode_kernel,
        out_shape=(
            jax.ShapeDtypeStruct((rows, feature), jnp.bfloat16),
            jax.ShapeDtypeStruct((passages, LANES), jnp.int32),
        ),
        in_specs=[ANY] * 5,
        out_specs=(VMEM, VMEM),
        scratch_shapes=[
            pltpu.SMEM(slot_centroid.shape, jnp.int32),
            pltpu.SMEM(lengths.shape, jnp.int32),
            pltpu.VMEM(slot_codes.shape, jnp.int32),
            pltpu.VMEM(codebook.shape, jnp.bfloat16),
            pltpu.VMEM(centroids.shape, jnp.bfloat16),
            pltpu.VMEM((rows, feature), jnp.float32),
            pltpu.SemaphoreType.DMA((4 + PIECES,)),
        ],
        compiler_params=pltpu.CompilerParams(vmem_limit_bytes=57 << 20),
        cost_estimate=pl.CostEstimate(
            flops=2 * rows * 256 * feature, bytes_accessed=centroids.size * 2, transcendentals=rows
        ),
        name="decode",
    )(slot_centroid, lengths, slot_codes, codebook, centroids)


def maxima(live, tokens, blocks, scratch, store):
    passages = live.shape[0]
    rows = scratch.shape[0] // len(blocks)
    slots = rows // passages
    tiles = slots // PER_TILE
    for b, (begin, vecs) in enumerate(blocks):
        first = vecs[0:passages, :]
        for m in range(slots):
            j = (m % tiles) * PER_TILE + m // tiles
            held = vecs[m * passages : (m + 1) * passages, :]
            if j:
                held = jnp.where(live > begin + j, held, first)
            at = b * rows + m * passages
            scratch[at : at + passages, :] = held

    chunk, span = 1024, 128
    for k in range(0, tokens.shape[0], chunk):
        wanted = tokens[k : k + chunk, :]
        best = None
        for b, (begin, _) in enumerate(blocks):
            top = None
            for s in range(b * rows, (b + 1) * rows, span):
                similar = lax.dot_general(
                    scratch[s : s + span, :], wanted, NT, preferred_element_type=jnp.float32
                )
                here = jnp.max(similar.reshape(span // passages, passages, chunk), axis=0)
                top = here if top is None else jnp.maximum(top, here)
            top = jnp.where(live[:, :1] > begin, top, LOWEST)
            best = top if best is None else jnp.maximum(best, top)
        store(k, best)


def score_kernel(live, queries, vecs, out_ref, scratch, whole, tokens):
    passages, count = live.shape[0], queries.shape[0]
    owners = out_ref.shape[0]
    own = 2
    query_len = count // owners // own
    slots = vecs.shape[1] // passages
    tokens[...] = unit(queries[...].astype(jnp.float32))

    def store(k, best):
        high = best.astype(jnp.bfloat16)
        rest = best - high.astype(jnp.float32)
        mid = rest.astype(jnp.bfloat16)
        low = (rest - mid.astype(jnp.float32)).astype(jnp.bfloat16)
        for i, part in enumerate((high, mid, low)):
            whole[i * passages : (i + 1) * passages, k : k + best.shape[1]] = part

    maxima(live[...], tokens, [(b * slots, vecs.at[b]) for b in range(4)], scratch, store)
    token = lax.broadcasted_iota(jnp.int32, (owners, count), 1) // query_len
    owner = lax.broadcasted_iota(jnp.int32, (owners, count), 0)
    for q in range(own):
        members = (token == owner * own + q).astype(jnp.float32).astype(jnp.bfloat16)
        sums = lax.dot_general(members, whole[...], NT, preferred_element_type=jnp.float32)
        total = sums[:, 2 * passages : 3 * passages] + sums[:, passages : 2 * passages]
        out_ref[:, q * passages : (q + 1) * passages] = total + sums[:, :passages]


def params(mebibytes):
    return pltpu.CompilerParams(vmem_limit_bytes=mebibytes << 20)


def cost(tokens, rows, feature):
    return pl.CostEstimate(
        flops=2 * tokens * rows * feature,
        bytes_accessed=(tokens + rows) * feature * 2,
        transcendentals=tokens,
    )


def shards(queries, centroids, codebook, slot_codes, slot_centroid, lengths, candidates):
    own, query_len, feature = queries.shape
    owners = lax.axis_size("wide")
    passages = lengths.shape[0]
    tokens = owners * own * query_len
    rows = slot_centroid.size
    sent = spread(queries.reshape(own * query_len, feature), owners)
    gathered = lax.all_to_all(sent, "wide", split_axis=0, concat_axis=0, tiled=True)
    gathered = gathered.reshape(tokens, feature)
    vecs, live = decode(slot_centroid, lengths, slot_codes, codebook, centroids)

    whole = lax.all_gather(vecs, "grp")
    table = pl.pallas_call(
        score_kernel,
        out_shape=jax.ShapeDtypeStruct((owners, LANES), jnp.float32),
        in_specs=[VMEM] * 3,
        out_specs=VMEM,
        scratch_shapes=[
            pltpu.VMEM((4 * rows, feature), jnp.bfloat16),
            pltpu.VMEM((3 * passages, tokens), jnp.bfloat16),
            pltpu.VMEM((tokens, feature), jnp.bfloat16),
        ],
        compiler_params=params(24),
        cost_estimate=cost(tokens, 4 * rows, feature),
        name="score",
    )(live, gathered, whole)
    owned = lax.all_to_all(table, "wide", split_axis=0, concat_axis=0, tiled=True)
    return pick(owned, candidates, passages)


def pick_kernel(passages, owned_ref, candidates_ref, out_ref):
    owners = owned_ref.shape[0]
    count, wanted = candidates_ref.shape
    rows = lax.broadcasted_iota(jnp.int32, (owners, LANES), 0)
    held = owned_ref[...]
    for q in range(count):
        for c in range(0, wanted, LANES):
            ids = candidates_ref[q : q + 1, c : c + LANES]
            lane = jnp.broadcast_to(q * passages + ids % passages, (owners, LANES))
            part = jnp.broadcast_to(ids // passages, (owners, LANES))
            found = jnp.take_along_axis(held, lane, axis=1)
            out_ref[q : q + 1, c : c + LANES] = jnp.sum(
                jnp.where(rows == part, found, 0.0), axis=0, keepdims=True
            )


def pick(owned, candidates, passages):
    return pl.pallas_call(
        functools.partial(pick_kernel, passages),
        out_shape=jax.ShapeDtypeStruct(candidates.shape, jnp.float32),
        in_specs=[VMEM, VMEM],
        out_specs=VMEM,
        compiler_params=params(2),
        cost_estimate=pl.CostEstimate(
            flops=candidates.size * owned.shape[0] * 2, bytes_accessed=owned.size * 4, transcendentals=0
        ),
        name="pick",
    )(owned, candidates)


def solution(mesh):
    placed = (
        P(("grp", "wide"), None, None),
        P("grp", None),
        P(),
        P("wide", "grp"),
        P("wide", "grp"),
        P("wide"),
        P(("grp", "wide"), None),
    )
    return jax.shard_map(
        shards, mesh=mesh, in_specs=placed, out_specs=P(("grp", "wide"), None), check_vma=False
    )
```

time: 351 us -> 47.1 us (0.13)
  waiting for transfers between devices: 292 us -> 0.01 us
  blocking collectives: 0 us -> 25.2 us
  local copies, waits for them, and re-layouts: 18.5 us -> 1.42 us
  between operations: 13.5 us -> 0.02 us
  Pallas kernels: 0 us -> 11.1 us
  matrix products: 6.79 us -> 0 us
  starting transfers between devices: 15.3 us -> 8.89 us
  other arithmetic: 4.16 us -> 0 us
    all_gather x1 -> x0, waiting for transfers between devices: 276 us -> none  [shards(): lax.all_gather(query_vecs, ('grp', 'wide'), axis=0, tiled=True)]
    all_to_all x2 -> x1, waiting for transfers between devices: 15.7 us -> 0.01 us  [shards(): lax.all_to_all(sent, 'wide', split_axis=0, concat_axis=0, tiled=True)]
    all_to_all x0 -> x1, blocking collectives: none -> 15.2 us  [shards(): lax.all_to_all(table, 'wide', split_axis=0, concat_axis=0, tiled=True)]
    pallas_call x0 -> x4, Pallas kernels: none -> 11.1 us  [the longest x1 6.66 us: decode(): pl.pallas_call(decode_kernel, out_shape=(jax.ShapeDtypeStruct((rows, feat...]
    gather x6 -> x0, local copies, waits for them, and re-layouts: 11 us -> none  [the longest x4 6.11 us: decode_slots(): centre = jnp.take(centroids, row_ids, axis=0).astype(jnp.float32)]
    all_gather x0 -> x1, blocking collectives: none -> 10.1 us  [shards(): whole = lax.all_gather(vecs, 'grp')]
    dot_general x3 -> x0, matrix products: 6.79 us -> none  [the longest x1 4.2 us: decode_slots(): jnp.einsum('rsk,ksc->rsc', one_hot, code_parts, preferred_element_type=jn...]
    all_to_all x2 -> x1, starting transfers between devices: 15.3 us -> 8.89 us  [shards(): lax.all_to_all(sent, 'wide', split_axis=0, concat_axis=0, tiled=True)]
  transfers between devices with their start and end apart: 3 -> 1, of which waited for: 3 -> 0; matrix products, arithmetic and copies ran while one was open for 4% -> 0% of each run, Pallas kernels for 0% -> 14%
where the time goes in v2:
time: 47.1 us; the launch traced here: 46.7 us
  blocking collectives  25.2 us (54%)
  Pallas kernels  11.1 us (24%)
  starting transfers between devices  8.89 us (19%)
  local copies, waits for them, and re-layouts  1.42 us (3%)
    all_to_all x1, blocking collectives, shards(): lax.all_to_all(table, 'wide', split_axis=0, concat_axis=0, tiled=True)  15.2 us
    all_gather x1, blocking collectives, shards(): whole = lax.all_gather(vecs, 'grp')  10.1 us
    all_to_all x1, starting transfers between devices, shards(): lax.all_to_all(sent, 'wide', split_axis=0, concat_axis=0, tiled=True)  8.89 us
    pallas_call x1, Pallas kernels, decode(): pl.pallas_call(decode_kernel, out_shape=(jax.ShapeDtypeStruct((rows, feat...  6.66 us
    pallas_call x1, Pallas kernels, shards(): pl.pallas_call(score_kernel, out_shape=jax.ShapeDtypeStruct((owners, LANE...  2.85 us
    unnamed x6, local copies, waits for them, and re-layouts  1.42 us
  transfers between devices with their start and end apart: 1, of which 0 were waited for; matrix products, arithmetic and copies ran while one was open for 0% of the time, Pallas kernels for 14%

profile of v2, /device:TPU:0, one launch (start us, length us, event | category | flops | bytes accessed | tf_op | source)
XLA Modules:
  0.0 46.7 jit_solution(8857028489767315948)
XLA Ops:
  0.0 0.0 copy-start.1
  0.0 0.7 %copy-done.1 = bf16[2,32,128]{2,1,0:T(8,128)(2,1)S(1)} copy-done((bf16[2,32,128]{2,1,0:T(8,128)(2,1)S(1)}, bf16[2,32,128]{2,1,0:T(8,128)(2,1)}, u32[]{:S(2)}) %copy-start.1) | copy-done | bytes 16408
  0.7 0.9 %spread.1 = bf16[32,64,128]{2,1,0:T(8,128)(2,1)} custom-call(bf16[64,128]{1,0:T(8,128)(2,1)S(1)} %bitcast.11), custom_call_target="tpu_custom_call" | custom-call | flops 20000000000 | bytes 1000000 | tf_op jit(solution)/shard_map/spread/pallas_call | solution.py:32
  1.6 0.0 copy-start
  1.6 8.9 %all-to-all-start = ((bf16[32,64,128]{2,1,0:T(8,128)(2,1)}), bf16[32,64,128]{2,1,0:T(8,128)(2,1)S(1)}, u32[]{:S(2)}, u32[]{:S(2)}) async-start(bf16[32,64,128]{2,1,0:T(8,128)(2,1)} %spread.1), calls=%async_computation | async-start | bytes 1048576 | tf_op jit(solution)/shard_map/all_to_all | solution.py:230
  10.5 6.7 %decode.1 = (bf16[512,128]{1,0:T(8,128)(2,1)}, s32[16,128]{1,0:T(8,128)}) custom-call(s32[16,32]{1,0:T(8,128)} %ids_hbm.1, s32[16]{0:T(128)} %lengths_hbm.1, s32[16,1024]{1,0:T(8,128)} %codes_hbm.1, bf16[256,128]{1,0:T(8,128)(2,1)} %book_hbm.1, bf16[32768,128]{1,0:T(8,128)(2,1)} %cent_hbm.1), custom_call_target="tpu_custom_call" | custom-call | flops 33554432 | bytes 8388608 | tf_op jit(solution)/shard_map/decode/pallas_call | solution.py:128
  17.2 10.1 %all-gather = bf16[2048,128]{1,0:T(8,128)(2,1)S(1)} all-gather(bf16[512,128]{1,0:T(8,128)(2,1)} %get-tuple-element.8), channel_id=2, replica_groups=mesh['grp'=4,'wide'=32] {'grp'}, dimensions={0}, use_global_device_ids=true | all-gather | bytes 655360 | tf_op jit(solution)/shard_map/all_gather | solution.py:234
  27.2 0.0 all-to-all-done
  27.2 0.0 copy-start.2
  27.2 0.7 %copy-done.2 = s32[16,128]{1,0:T(8,128)S(1)} copy-done((s32[16,128]{1,0:T(8,128)S(1)}, s32[16,128]{1,0:T(8,128)}, u32[]{:S(2)}) %copy-start.2) | copy-done | bytes 8216
  27.9 2.8 %score.1 = f32[32,128]{1,0:T(8,128)S(1)} custom-call(s32[16,128]{1,0:T(8,128)S(1)} %copy-done.2, bf16[2048,128]{1,0:T(8,128)(2,1)S(1)} %bitcast.8, bf16[4,512,128]{2,1,0:T(8,128)(2,1)S(1)} %bitcast.7), custom_call_target="tpu_custom_call" | custom-call | flops 1073741824 | bytes 1048576 | tf_op jit(solution)/shard_map/score/pallas_call | solution.py:235
  30.8 15.2 %all_to_all.16 = f32[32,1,128]{2,1,0:T(1,128)S(1)} all-to-all(f32[32,1,128]{2,1,0:T(1,128)S(1)} %bitcast.10), channel_id=1, replica_groups=mesh['grp'=4,'wide'=32] {'wide'}, dimensions={0} | all-to-all | bytes 32768 | tf_op jit(solution)/shard_map/all_to_all | solution.py:249
  46.0 0.0 copy-done
  46.0 0.7 %pick.1 = f32[2,256]{1,0:T(2,128)} custom-call(f32[32,128]{1,0:T(8,128)S(1)} %bitcast.9, s32[2,256]{1,0:T(2,128)S(1)} %copy-done), custom_call_target="tpu_custom_call" | custom-call | flops 32768 | bytes 16384 | tf_op jit(solution)/shard_map/pick/pallas_call | solution.py:270
Async XLA Ops:
  0.0 0.7 %copy-start.1 = (bf16[2,32,128]{2,1,0:T(8,128)(2,1)S(1)}, bf16[2,32,128]{2,1,0:T(8,128)(2,1)}, u32[]{:S(2)}) copy-start(bf16[2,32,128]{2,1,0:T(8,128)(2,1)} %param.7) | copy-start | bytes 49156
  1.6 44.4 %copy-start = (s32[2,256]{1,0:T(2,128)S(1)}, s32[2,256]{1,0:T(2,128)}, u32[]{:S(2)}) copy-start(s32[2,256]{1,0:T(2,128)} %candidates_ref.1) | copy-start | bytes 6148
  1.6 25.6 %all-to-all-start = ((bf16[32,64,128]{2,1,0:T(8,128)(2,1)}), bf16[32,64,128]{2,1,0:T(8,128)(2,1)S(1)}, u32[]{:S(2)}, u32[]{:S(2)}) async-start(bf16[32,64,128]{2,1,0:T(8,128)(2,1)} %spread.1), calls=%async_computation | async-start | bytes 1048576 | tf_op jit(solution)/shard_map/all_to_all | solution.py:230
  27.2 0.7 %copy-start.2 = (s32[16,128]{1,0:T(8,128)S(1)}, s32[16,128]{1,0:T(8,128)}, u32[]{:S(2)}) copy-start(s32[16,128]{1,0:T(8,128)} %get-tuple-element.7.live) | copy-start | bytes 24580

commit v3 on v2

--- a/solution.py
+++ b/solution.py
@@ -12,6 +12,7 @@
 PER_TILE = 4
 PIECES = 4
 LOWEST = -1e30
+PAIR = 4
 NT = (((1,), (1,)), ((), ()))
 VMEM = pl.BlockSpec(memory_space=pltpu.VMEM)
 ANY = pl.BlockSpec(memory_space=pl.ANY)
@@ -22,22 +23,43 @@
     return (values * scale).astype(jnp.bfloat16)
 
 
-def spread_kernel(queries_ref, out_ref):
-    held = queries_ref[...]
+def unit_kernel(queries, out):
+    out[...] = unit(queries[...].astype(jnp.float32))
+
+
+def unit_queries(queries):
+    return pl.pallas_call(
+        unit_kernel,
+        out_shape=jax.ShapeDtypeStruct(queries.shape, jnp.bfloat16),
+        in_specs=[VMEM],
+        out_specs=VMEM,
+        compiler_params=params(2),
+        cost_estimate=pl.CostEstimate(flops=20000000000, bytes_accessed=queries.size * 2, transcendentals=0),
+        name="unit_queries",
+    )(queries)
+
+
+def spread_kernel(queries_ref, partner_ref, after_ref, out_ref):
+    rows = queries_ref.shape[0]
+    low = (lax.axis_index("wide") & PAIR) == 0
+    own, partner = queries_ref[...], partner_ref[...]
+    first, second = jnp.where(low, own, partner), jnp.where(low, partner, own)
     for i in range(out_ref.shape[0]):
-        out_ref[i] = held
-
-
-def spread(queries, owners):
+        out_ref[i, 0:rows, :] = first
+        out_ref[i, rows : 2 * rows, :] = second
+
+
+def spread(queries, partner, after, count):
+    rows, feature = queries.shape
     return pl.pallas_call(
         spread_kernel,
-        out_shape=jax.ShapeDtypeStruct((owners, *queries.shape), queries.dtype),
-        in_specs=[VMEM],
+        out_shape=jax.ShapeDtypeStruct((count, 2 * rows, feature), queries.dtype),
+        in_specs=[VMEM, VMEM, ANY],
         out_specs=VMEM,
         compiler_params=params(4),
-        cost_estimate=pl.CostEstimate(flops=20000000000, bytes_accessed=1000000, transcendentals=0),
+        cost_estimate=pl.CostEstimate(flops=0, bytes_accessed=count * rows * feature * 4, transcendentals=0),
         name="spread",
-    )(queries)
+    )(queries, partner, after)
 
 
 def residual_rows(codes, codebook, store):
@@ -64,41 +86,22 @@
         store(jj, jnp.concatenate(parts, axis=0).T)
 
 
-def decode_kernel(
-    ids_hbm, lengths_hbm, codes_hbm, book_hbm, cent_hbm, out_ref, live_ref,
-    ids, lengths, codes, book, table, residual, sems,
-):
+def residual_kernel(codes, book, out):
+    def store(jj, rows):
+        out[jj * LANES : (jj + 1) * LANES, :] = rows
+
+    residual_rows(codes[...], book[...], store)
+
+
+def gather_kernel(ids, lengths, residual, table, out_ref, live_ref):
     passages, slots = ids.shape
     tiles = slots // PER_TILE
     count = table.shape[0]
-    copies = [
-        pltpu.make_async_copy(source, target, sems.at[i])
-        for i, (source, target) in enumerate(
-            [(codes_hbm, codes), (book_hbm, book), (ids_hbm, ids), (lengths_hbm, lengths)]
-        )
-    ]
-    piece = count // PIECES
-    for i in range(PIECES):
-        part = pl.ds(i * piece, piece)
-        copies.append(pltpu.make_async_copy(cent_hbm.at[part, :], table.at[part, :], sems.at[4 + i]))
-    for copy in copies:
-        copy.start()
-    for copy in copies[:4]:
-        copy.wait()
-
     row = lax.broadcasted_iota(jnp.int32, (passages, LANES), 0)
     live = jnp.zeros((passages, LANES), jnp.int32)
     for p in range(passages):
         live = jnp.where(row == p, lengths[p], live)
     live_ref[...] = live
-
-    def store(jj, rows):
-        residual[jj * LANES : (jj + 1) * LANES, :] = rows
-
-    residual_rows(codes[...], book[...], store)
-    for copy in copies[4:]:
-        copy.wait()
-
     sublane = lax.broadcasted_iota(jnp.int32, (8, LANES), 0)
 
     def gather(m, carry):
@@ -125,29 +128,30 @@
 def decode(slot_centroid, lengths, slot_codes, codebook, centroids):
     passages, slots = slot_centroid.shape
     rows, feature = passages * slots, codebook.shape[1]
+    smem = pl.BlockSpec(memory_space=pltpu.SMEM)
+    residual = pl.pallas_call(
+        residual_kernel,
+        out_shape=jax.ShapeDtypeStruct((rows, feature), jnp.float32),
+        in_specs=[VMEM, VMEM],
+        out_specs=VMEM,
+        compiler_params=params(4),
+        cost_estimate=pl.CostEstimate(flops=rows * 256 * feature, bytes_accessed=rows * 256, transcendentals=0),
+        name="residual",
+    )(slot_codes, codebook)
     return pl.pallas_call(
-        decode_kernel,
+        gather_kernel,
         out_shape=(
             jax.ShapeDtypeStruct((rows, feature), jnp.bfloat16),
             jax.ShapeDtypeStruct((passages, LANES), jnp.int32),
         ),
-        in_specs=[ANY] * 5,
+        in_specs=[smem, smem, VMEM, VMEM],
         out_specs=(VMEM, VMEM),
-        scratch_shapes=[
-            pltpu.SMEM(slot_centroid.shape, jnp.int32),
-            pltpu.SMEM(lengths.shape, jnp.int32),
-            pltpu.VMEM(slot_codes.shape, jnp.int32),
-            pltpu.VMEM(codebook.shape, jnp.bfloat16),
-            pltpu.VMEM(centroids.shape, jnp.bfloat16),
-            pltpu.VMEM((rows, feature), jnp.float32),
-            pltpu.SemaphoreType.DMA((4 + PIECES,)),
-        ],
-        compiler_params=pltpu.CompilerParams(vmem_limit_bytes=57 << 20),
+        compiler_params=params(4 + centroids.size * 2 // (1 << 20)),
         cost_estimate=pl.CostEstimate(
-            flops=2 * rows * 256 * feature, bytes_accessed=centroids.size * 2, transcendentals=rows
+            flops=rows * feature * 8, bytes_accessed=centroids.size * 2, transcendentals=rows
         ),
-        name="decode",
-    )(slot_centroid, lengths, slot_codes, codebook, centroids)
+        name="gather",
+    )(slot_centroid, lengths, residual, centroids)
 
 
 def maxima(live, tokens, blocks, scratch, store):
@@ -182,13 +186,12 @@
         store(k, best)
 
 
-def score_kernel(live, queries, vecs, out_ref, scratch, whole, tokens):
-    passages, count = live.shape[0], queries.shape[0]
+def score_kernel(live, tokens, vecs, out_ref, scratch, whole):
+    passages, count = live.shape[0], tokens.shape[0]
     owners = out_ref.shape[0]
     own = 2
     query_len = count // owners // own
     slots = vecs.shape[1] // passages
-    tokens[...] = unit(queries[...].astype(jnp.float32))
 
     def store(k, best):
         high = best.astype(jnp.bfloat16)
@@ -199,10 +202,12 @@
             whole[i * passages : (i + 1) * passages, k : k + best.shape[1]] = part
 
     maxima(live[...], tokens, [(b * slots, vecs.at[b]) for b in range(4)], scratch, store)
-    token = lax.broadcasted_iota(jnp.int32, (owners, count), 1) // query_len
+    query = lax.broadcasted_iota(jnp.int32, (owners, count), 1) // query_len
     owner = lax.broadcasted_iota(jnp.int32, (owners, count), 0)
+    pair = (owner // (2 * PAIR)) * PAIR + owner % PAIR
+    place = pair * 2 + (owner // PAIR) % 2
     for q in range(own):
-        members = (token == owner * own + q).astype(jnp.float32).astype(jnp.bfloat16)
+        members = (query == place * own + q).astype(jnp.float32).astype(jnp.bfloat16)
         sums = lax.dot_general(members, whole[...], NT, preferred_element_type=jnp.float32)
         total = sums[:, 2 * passages : 3 * passages] + sums[:, passages : 2 * passages]
         out_ref[:, q * passages : (q + 1) * passages] = total + sums[:, :passages]
@@ -226,10 +231,14 @@
     passages = lengths.shape[0]
     tokens = owners * own * query_len
     rows = slot_centroid.size
-    sent = spread(queries.reshape(own * query_len, feature), owners)
-    gathered = lax.all_to_all(sent, "wide", split_axis=0, concat_axis=0, tiled=True)
-    gathered = gathered.reshape(tokens, feature)
+    plain = unit_queries(queries.reshape(own * query_len, feature))
+    partner = lax.ppermute(plain, "wide", [(i, i ^ PAIR) for i in range(owners)])
     vecs, live = decode(slot_centroid, lengths, slot_codes, codebook, centroids)
+    sent = spread(plain, partner, live, owners // 2)
+    groups = [[i + z for i in range(owners) if not i & PAIR] for z in (0, PAIR)]
+    gathered = lax.all_to_all(
+        sent, "wide", split_axis=0, concat_axis=0, axis_index_groups=groups, tiled=True
+    ).reshape(tokens, feature)
 
     whole = lax.all_gather(vecs, "grp")
     table = pl.pallas_call(
@@ -240,7 +249,6 @@
         scratch_shapes=[
             pltpu.VMEM((4 * rows, feature), jnp.bfloat16),
             pltpu.VMEM((3 * passages, tokens), jnp.bfloat16),
-            pltpu.VMEM((tokens, feature), jnp.bfloat16),
         ],
         compiler_params=params(24),
         cost_estimate=cost(tokens, 4 * rows, feature),

time: 47.1 us -> 44.6 us (0.947)
  Pallas kernels: 11.1 us -> 8.04 us
  waiting for transfers between devices: 0.01 us -> 1.98 us
  blocking collectives: 25.2 us -> 23.6 us
    pallas_call x2 -> x4, Pallas kernels: 7.56 us -> 4.68 us  [the longest x1 3.09 us: decode(): pl.pallas_call(gather_kernel, out_shape=(jax.ShapeDtypeStruct((rows, feat...]
    ppermute x0 -> x1, starting transfers between devices: none -> 2.08 us  [shards(): lax.ppermute(plain, 'wide', [(i, i ^ PAIR) for i in range(owners)])]
    all_to_all x1, waiting for transfers between devices: 0.01 us -> 1.98 us  [shards(): lax.all_to_all(sent, 'wide', split_axis=0, concat_axis=0, axis_index_grou...]
    all_to_all x1, starting transfers between devices: 8.89 us -> 7.12 us  [shards(): lax.all_to_all(sent, 'wide', split_axis=0, concat_axis=0, axis_index_grou...]
    all_to_all x1, blocking collectives: 15.2 us -> 14.1 us  [shards(): lax.all_to_all(table, 'wide', split_axis=0, concat_axis=0, tiled=True)]
    all_gather x1, blocking collectives: 10.1 us -> 9.56 us  [shards(): whole = lax.all_gather(vecs, 'grp')]
    unnamed x6 -> x14, local copies, waits for them, and re-layouts: 1.42 us -> 1.4 us
  transfers between devices with their start and end apart: 1 -> 2, of which waited for: 0 -> 1; matrix products, arithmetic and copies ran while one was open for 0% -> 0% of each run, Pallas kernels for 14% -> 8%
where the time goes in v3:
time: 44.6 us; the launch traced here: 44.3 us
  blocking collectives  23.6 us (53%)
  starting transfers between devices  9.2 us (21%)
  Pallas kernels  8.04 us (18%)
  waiting for transfers between devices  1.98 us (4%)
  local copies, waits for them, and re-layouts  1.4 us (3%)
    all_to_all x1, blocking collectives, shards(): lax.all_to_all(table, 'wide', split_axis=0, concat_axis=0, tiled=True)  14.1 us
    all_gather x1, blocking collectives, shards(): whole = lax.all_gather(vecs, 'grp')  9.56 us
    all_to_all x1, starting transfers between devices, shards(): lax.all_to_all(sent, 'wide', split_axis=0, concat_axis=0, axis_index_grou...  7.12 us
    pallas_call x1, Pallas kernels, decode(): pl.pallas_call(gather_kernel, out_shape=(jax.ShapeDtypeStruct((rows, feat...  3.09 us
    pallas_call x1, Pallas kernels, shards(): pl.pallas_call(score_kernel, out_shape=jax.ShapeDtypeStruct((owners, LANE...  2.66 us
    ppermute x1, starting transfers between devices, shards(): lax.ppermute(plain, 'wide', [(i, i ^ PAIR) for i in range(owners)])  2.08 us
    all_to_all x1, waiting for transfers between devices, shards(): lax.all_to_all(sent, 'wide', split_axis=0, concat_axis=0, axis_index_grou...  1.98 us
    unnamed x14, local copies, waits for them, and re-layouts  1.4 us
  transfers between devices with their start and end apart: 2, of which 1 were waited for; matrix products, arithmetic and copies ran while one was open for 0% of the time, Pallas kernels for 8%

profile of v3, /device:TPU:0, one launch (start us, length us, event | category | flops | bytes accessed | tf_op | source)
XLA Modules:
  0.0 44.3 jit_solution(6638374911300596482)
XLA Ops:
  0.0 0.0 copy-start.6
  0.0 0.7 %copy-done.6 = bf16[2,32,128]{2,1,0:T(8,128)(2,1)S(1)} copy-done((bf16[2,32,128]{2,1,0:T(8,128)(2,1)S(1)}, bf16[2,32,128]{2,1,0:T(8,128)(2,1)}, u32[]{:S(2)}) %copy-start.6) | copy-done | bytes 16408
  0.7 0.0 copy-start.1
  0.7 0.0 copy-start.2
  0.7 0.0 copy-start
  0.7 0.0 copy-start.3
  0.7 0.0 copy-start.5
  0.7 0.1 unit_queries.1.queries_ref
  0.8 0.0 copy-start.4
  0.8 2.1 %collective-permute-start = (bf16[64,128]{1,0:T(8,128)(2,1)S(1)}, bf16[64,128]{1,0:T(8,128)(2,1)S(1)}, u32[]{:S(2)}, u32[]{:S(2)}) collective-permute-start(bf16[64,128]{1,0:T(8,128)(2,1)S(1)} %unit_queries.1.queries_ref), channel_id=1, source_target_pairs={{0,4},{1,5},{2,6},{3,7},{4,0},{5,1},{6,2},{7,3},{8,12},{9,13},{10,... | collective-permute-start | bytes 49160 | tf_op jit(solution)/shard_map/ppermute | solution.py:235
  2.9 0.0 copy-done.1
  2.9 0.0 copy-done.2
  2.9 0.6 %residual.1 = f32[512,128]{1,0:T(8,128)S(1)} custom-call(s32[16,1024]{1,0:T(8,128)S(1)} %copy-done.1, bf16[256,128]{1,0:T(8,128)(2,1)S(1)} %copy-done.2), custom_call_target="tpu_custom_call" | custom-call | flops 16777216 | bytes 131072 | tf_op jit(solution)/shard_map/residual/pallas_call | solution.py:132
  3.5 0.7 %copy-done = bf16[32768,128]{1,0:T(8,128)(2,1)S(1)} copy-done((bf16[32768,128]{1,0:T(8,128)(2,1)S(1)}, bf16[32768,128]{1,0:T(8,128)(2,1)}, u32[]{:S(2)}) %copy-start) | copy-done | bytes 8388632
  4.2 0.0 copy-done.3
  4.2 0.0 copy-done.5
  4.2 3.1 %gather.1 = (bf16[512,128]{1,0:T(8,128)(2,1)S(1)}, s32[16,128]{1,0:T(8,128)S(1)}) custom-call(s32[16,32]{1,0:T(8,128)S(1)} %copy-done.3, s32[16]{0:T(128)S(1)} %copy-done.5, f32[512,128]{1,0:T(8,128)S(1)} %residual.1, bf16[32768,128]{1,0:T(8,128)(2,1)S(1)} %copy-done), custom_call_target="tpu_custom_call" | custom-call | flops 524288 | bytes 8388608 | tf_op jit(solution)/shard_map/gather/pallas_call | solution.py:141
  7.3 0.0 collective-permute-done.partner_ref
  7.3 0.9 %spread.1 = bf16[16,128,128]{2,1,0:T(8,128)(2,1)} custom-call(bf16[64,128]{1,0:T(8,128)(2,1)S(1)} %unit_queries.1.queries_ref, bf16[64,128]{1,0:T(8,128)(2,1)S(1)} %collective-permute-done.partner_ref, s32[16,128]{1,0:T(8,128)S(1)} %get-tuple-element.7.after_ref.live), custom_call_target="tpu_custom_call" | custom-call | bytes 524288 | tf_op jit(solution)/shard_map/spread/pallas_call | solution.py:54
  8.2 7.1 %all-to-all-start = ((bf16[16,128,128]{2,1,0:T(8,128)(2,1)}), bf16[16,128,128]{2,1,0:T(8,128)(2,1)S(1)}, u32[]{:S(2)}, u32[]{:S(2)}) async-start(bf16[16,128,128]{2,1,0:T(8,128)(2,1)} %spread.1), calls=%async_computation | async-start | bytes 1048576 | tf_op jit(solution)/shard_map/all_to_all | solution.py:239
  15.3 9.6 %all-gather = bf16[2048,128]{1,0:T(8,128)(2,1)S(1)} all-gather(bf16[512,128]{1,0:T(8,128)(2,1)S(1)} %get-tuple-element.8), channel_id=2, replica_groups=mesh['grp'=4,'wide'=32] {'grp'}, dimensions={0}, use_global_device_ids=true | all-gather | bytes 655360 | tf_op jit(solution)/shard_map/all_gather | solution.py:243
  24.9 2.0 %all-to-all-done = bf16[16,128,128]{2,1,0:T(8,128)(2,1)S(1)} async-done(((bf16[16,128,128]{2,1,0:T(8,128)(2,1)}), bf16[16,128,128]{2,1,0:T(8,128)(2,1)S(1)}, u32[]{:S(2)}, u32[]{:S(2)}) %all-to-all-start) | async-done | bytes 524320 | tf_op jit(solution)/shard_map/all_to_all | solution.py:239
  26.9 2.7 %score.1 = f32[32,128]{1,0:T(8,128)S(1)} custom-call(s32[16,128]{1,0:T(8,128)S(1)} %get-tuple-element.7.after_ref.live, bf16[2048,128]{1,0:T(8,128)(2,1)S(1)} %bitcast.8, bf16[4,512,128]{2,1,0:T(8,128)(2,1)S(1)} %bitcast.7), custom_call_target="tpu_custom_call" | custom-call | flops 1073741824 | bytes 1048576 | tf_op jit(solution)/shard_map/score/pallas_call | solution.py:244
  29.5 14.1 %all_to_all.16 = f32[32,1,128]{2,1,0:T(1,128)S(1)} all-to-all(f32[32,1,128]{2,1,0:T(1,128)S(1)} %bitcast.10), channel_id=1, replica_groups=mesh['grp'=4,'wide'=32] {'wide'}, dimensions={0} | all-to-all | bytes 32768 | tf_op jit(solution)/shard_map/all_to_all | solution.py:257
  43.6 0.0 copy-done.4
  43.6 0.7 %pick.1 = f32[2,256]{1,0:T(2,128)} custom-call(f32[32,128]{1,0:T(8,128)S(1)} %bitcast.9, s32[2,256]{1,0:T(2,128)S(1)} %copy-done.4), custom_call_target="tpu_custom_call" | custom-call | flops 32768 | bytes 16384 | tf_op jit(solution)/shard_map/pick/pallas_call | solution.py:278
Async XLA Ops:
  0.0 0.7 %copy-start.6 = (bf16[2,32,128]{2,1,0:T(8,128)(2,1)S(1)}, bf16[2,32,128]{2,1,0:T(8,128)(2,1)}, u32[]{:S(2)}) copy-start(bf16[2,32,128]{2,1,0:T(8,128)(2,1)} %param.7) | copy-start | bytes 49156
  0.7 2.2 %copy-start.1 = (s32[16,1024]{1,0:T(8,128)S(1)}, s32[16,1024]{1,0:T(8,128)}, u32[]{:S(2)}) copy-start(s32[16,1024]{1,0:T(8,128)} %codes.1) | copy-start | bytes 196612
  0.7 2.2 %copy-start.2 = (bf16[256,128]{1,0:T(8,128)(2,1)S(1)}, bf16[256,128]{1,0:T(8,128)(2,1)}, u32[]{:S(2)}) copy-start(bf16[256,128]{1,0:T(8,128)(2,1)} %book.1) | copy-start | bytes 196612
  0.7 3.5 %copy-start = (bf16[32768,128]{1,0:T(8,128)(2,1)S(1)}, bf16[32768,128]{1,0:T(8,128)(2,1)}, u32[]{:S(2)}) copy-start(bf16[32768,128]{1,0:T(8,128)(2,1)} %table.1) | copy-start | bytes 25165828
  0.7 3.5 %copy-start.3 = (s32[16,32]{1,0:T(8,128)S(1)}, s32[16,32]{1,0:T(8,128)}, u32[]{:S(2)}) copy-start(s32[16,32]{1,0:T(8,128)} %ids.1) | copy-start | bytes 6148
  0.7 3.5 %copy-start.5 = (s32[16]{0:T(128)S(1)}, s32[16]{0:T(128)}, u32[]{:S(2)}) copy-start(s32[16]{0:T(128)} %lengths.1) | copy-start | bytes 196
  0.8 42.7 %copy-start.4 = (s32[2,256]{1,0:T(2,128)S(1)}, s32[2,256]{1,0:T(2,128)}, u32[]{:S(2)}) copy-start(s32[2,256]{1,0:T(2,128)} %candidates_ref.1) | copy-start | bytes 6148
  0.8 6.4 %collective-permute-start = (bf16[64,128]{1,0:T(8,128)(2,1)S(1)}, bf16[64,128]{1,0:T(8,128)(2,1)S(1)}, u32[]{:S(2)}, u32[]{:S(2)}) collective-permute-start(bf16[64,128]{1,0:T(8,128)(2,1)S(1)} %unit_queries.1.queries_ref), channel_id=1, source_target_pairs={{0,4},{1,5},{2,6},{3,7},{4,0},{5,1},{6,2},{7,3},{8,12},{9,13},{10,... | collective-permute-start | bytes 49160 | tf_op jit(solution)/shard_map/ppermute | solution.py:235
  8.2 18.7 %all-to-all-start = ((bf16[16,128,128]{2,1,0:T(8,128)(2,1)}), bf16[16,128,128]{2,1,0:T(8,128)(2,1)S(1)}, u32[]{:S(2)}, u32[]{:S(2)}) async-start(bf16[16,128,128]{2,1,0:T(8,128)(2,1)} %spread.1), calls=%async_computation | async-start | bytes 1048576 | tf_op jit(solution)/shard_map/all_to_all | solution.py:239

commit v4 on v3

--- a/solution.py
+++ b/solution.py
@@ -23,43 +23,49 @@
     return (values * scale).astype(jnp.bfloat16)
 
 
-def unit_kernel(queries, out):
-    out[...] = unit(queries[...].astype(jnp.float32))
-
-
-def unit_queries(queries):
+def members_kernel(query_len, out_ref):
+    own, owners, count = out_ref.shape
+    query = lax.broadcasted_iota(jnp.int32, (owners, count), 1) // query_len
+    owner = lax.broadcasted_iota(jnp.int32, (owners, count), 0)
+    pair = (owner // (2 * PAIR)) * PAIR + owner % PAIR
+    place = pair * 2 + (owner // PAIR) % 2
+    for q in range(own):
+        out_ref[q] = (query == place * own + q).astype(jnp.float32).astype(jnp.bfloat16)
+
+
+def members_of(own, owners, query_len):
     return pl.pallas_call(
-        unit_kernel,
-        out_shape=jax.ShapeDtypeStruct(queries.shape, jnp.bfloat16),
-        in_specs=[VMEM],
+        functools.partial(members_kernel, query_len),
+        out_shape=jax.ShapeDtypeStruct((own, owners, owners * own * query_len), jnp.bfloat16),
         out_specs=VMEM,
         compiler_params=params(2),
-        cost_estimate=pl.CostEstimate(flops=20000000000, bytes_accessed=queries.size * 2, transcendentals=0),
-        name="unit_queries",
-    )(queries)
-
-
-def spread_kernel(queries_ref, partner_ref, after_ref, out_ref):
+        cost_estimate=pl.CostEstimate(flops=20000000000, bytes_accessed=1000, transcendentals=0),
+        name="members",
+    )()
+
+
+def spread_kernel(queries_ref, partner_ref, out_ref):
     rows = queries_ref.shape[0]
     low = (lax.axis_index("wide") & PAIR) == 0
-    own, partner = queries_ref[...], partner_ref[...]
+    own = unit(queries_ref[...].astype(jnp.float32))
+    partner = unit(partner_ref[...].astype(jnp.float32))
     first, second = jnp.where(low, own, partner), jnp.where(low, partner, own)
     for i in range(out_ref.shape[0]):
         out_ref[i, 0:rows, :] = first
         out_ref[i, rows : 2 * rows, :] = second
 
 
-def spread(queries, partner, after, count):
+def spread(queries, partner, count):
     rows, feature = queries.shape
     return pl.pallas_call(
         spread_kernel,
         out_shape=jax.ShapeDtypeStruct((count, 2 * rows, feature), queries.dtype),
-        in_specs=[VMEM, VMEM, ANY],
+        in_specs=[VMEM, VMEM],
         out_specs=VMEM,
         compiler_params=params(4),
         cost_estimate=pl.CostEstimate(flops=0, bytes_accessed=count * rows * feature * 4, transcendentals=0),
         name="spread",
-    )(queries, partner, after)
+    )(queries, partner)
 
 
 def residual_rows(codes, codebook, store):
@@ -86,25 +92,25 @@
         store(jj, jnp.concatenate(parts, axis=0).T)
 
 
-def residual_kernel(codes, book, out):
+def residual_kernel(codes, book, lengths, out, live):
     def store(jj, rows):
         out[jj * LANES : (jj + 1) * LANES, :] = rows
 
     residual_rows(codes[...], book[...], store)
-
-
-def gather_kernel(ids, lengths, residual, table, out_ref, live_ref):
+    count = live.shape[0]
+    row = lax.broadcasted_iota(jnp.int32, (count, count), 0)
+    lane = lax.broadcasted_iota(jnp.int32, (count, count), 1)
+    held = jnp.where(row == lane, jnp.broadcast_to(lengths[...], (count, count)), 0)
+    live[...] = jnp.broadcast_to(jnp.sum(held, axis=1, keepdims=True), live.shape)
+
+
+def gather_kernel(ids, residual, table, out_ref):
     passages, slots = ids.shape
     tiles = slots // PER_TILE
     count = table.shape[0]
-    row = lax.broadcasted_iota(jnp.int32, (passages, LANES), 0)
-    live = jnp.zeros((passages, LANES), jnp.int32)
-    for p in range(passages):
-        live = jnp.where(row == p, lengths[p], live)
-    live_ref[...] = live
     sublane = lax.broadcasted_iota(jnp.int32, (8, LANES), 0)
 
-    def gather(m, carry):
+    for m in range(slots):
         j = (m % tiles) * PER_TILE + m // tiles
         halves = []
         for h in range(0, passages, 8):
@@ -117,41 +123,41 @@
                 half = jnp.where(within >= 8, slab[8:], slab[:8])
                 held = jnp.where(sublane == q, pltpu.roll(half, (q - within) & 7, 0), held)
             halves.append(held)
-        at = pl.multiple_of(m * passages, passages)
-        raw = jnp.concatenate(halves, axis=0) + residual[pl.ds(at, passages), :]
-        out_ref[pl.ds(at, passages), :] = unit(raw)
-        return carry
-
-    lax.fori_loop(0, slots, gather, 0, unroll=8)
-
-
-def decode(slot_centroid, lengths, slot_codes, codebook, centroids):
+        at = m * passages
+        raw = jnp.concatenate(halves, axis=0) + residual[at : at + passages, :]
+        out_ref[at : at + passages, :] = unit(raw)
+
+
+def decode(slot_centroid, lengths, slot_codes, codebook, centroids, sent):
     passages, slots = slot_centroid.shape
     rows, feature = passages * slots, codebook.shape[1]
     smem = pl.BlockSpec(memory_space=pltpu.SMEM)
-    residual = pl.pallas_call(
+    residual, live = pl.pallas_call(
         residual_kernel,
-        out_shape=jax.ShapeDtypeStruct((rows, feature), jnp.float32),
-        in_specs=[VMEM, VMEM],
-        out_specs=VMEM,
+        out_shape=(
+            jax.ShapeDtypeStruct((rows, feature), jnp.float32),
+            jax.ShapeDtypeStruct((passages, LANES), jnp.int32),
+        ),
+        in_specs=[VMEM] * 3,
+        out_specs=(VMEM, VMEM),
         compiler_params=params(4),
         cost_estimate=pl.CostEstimate(flops=rows * 256 * feature, bytes_accessed=rows * 256, transcendentals=0),
         name="residual",
-    )(slot_codes, codebook)
-    return pl.pallas_call(
+    )(slot_codes, codebook, lengths.reshape(1, passages))
+    residual, sent = lax.optimization_barrier((residual, sent))
+    vecs = pl.pallas_call(
         gather_kernel,
-        out_shape=(
-            jax.ShapeDtypeStruct((rows, feature), jnp.bfloat16),
-            jax.ShapeDtypeStruct((passages, LANES), jnp.int32),
-        ),
-        in_specs=[smem, smem, VMEM, VMEM],
-        out_specs=(VMEM, VMEM),
+        out_shape=jax.ShapeDtypeStruct((rows, feature), jnp.bfloat16),
+        in_specs=[smem, VMEM, VMEM],
+        out_specs=VMEM,
         compiler_params=params(4 + centroids.size * 2 // (1 << 20)),
         cost_estimate=pl.CostEstimate(
             flops=rows * feature * 8, bytes_accessed=centroids.size * 2, transcendentals=rows
         ),
         name="gather",
-    )(slot_centroid, lengths, residual, centroids)
+    )(slot_centroid, residual, centroids)
+    vecs, sent = lax.optimization_barrier((vecs, sent))
+    return vecs, live, sent
 
 
 def maxima(live, tokens, blocks, scratch, store):
@@ -186,14 +192,35 @@
         store(k, best)
 
 
-def score_kernel(live, tokens, vecs, out_ref, scratch, whole):
-    passages, count = live.shape[0], tokens.shape[0]
-    owners = out_ref.shape[0]
-    own = 2
-    query_len = count // owners // own
-    slots = vecs.shape[1] // passages
+def begins(slots):
+    own = lax.axis_index("grp")
+    return [jnp.bitwise_xor(own, s) * slots for s in range(4)]
+
+
+def near_kernel(live, tokens, own, other, best_out, scratch):
+    begin = begins(own.shape[0] // live.shape[0])
 
     def store(k, best):
+        best_out[:, k : k + best.shape[1]] = best
+
+    maxima(live[...], tokens, [(begin[0], own), (begin[1], other)], scratch, store)
+
+
+def far_kernel(live, tokens, vecs, before, best_out, scratch):
+    begin = begins(vecs.shape[0] // live.shape[0])
+
+    def store(k, best):
+        best_out[:, k : k + best.shape[1]] = jnp.maximum(best, before[:, k : k + best.shape[1]])
+
+    maxima(live[...], tokens, [(begin[2], vecs)], scratch, store)
+
+
+def last_kernel(live, tokens, vecs, before, members, out_ref, scratch, whole):
+    passages = live.shape[0]
+    begin = begins(vecs.shape[0] // passages)
+
+    def store(k, best):
+        best = jnp.maximum(best, before[:, k : k + best.shape[1]])
         high = best.astype(jnp.bfloat16)
         rest = best - high.astype(jnp.float32)
         mid = rest.astype(jnp.bfloat16)
@@ -201,14 +228,9 @@
         for i, part in enumerate((high, mid, low)):
             whole[i * passages : (i + 1) * passages, k : k + best.shape[1]] = part
 
-    maxima(live[...], tokens, [(b * slots, vecs.at[b]) for b in range(4)], scratch, store)
-    query = lax.broadcasted_iota(jnp.int32, (owners, count), 1) // query_len
-    owner = lax.broadcasted_iota(jnp.int32, (owners, count), 0)
-    pair = (owner // (2 * PAIR)) * PAIR + owner % PAIR
-    place = pair * 2 + (owner // PAIR) % 2
-    for q in range(own):
-        members = (query == place * own + q).astype(jnp.float32).astype(jnp.bfloat16)
-        sums = lax.dot_general(members, whole[...], NT, preferred_element_type=jnp.float32)
+    maxima(live[...], tokens, [(begin[3], vecs)], scratch, store)
+    for q in range(members.shape[0]):
+        sums = lax.dot_general(members[q], whole[...], NT, preferred_element_type=jnp.float32)
         total = sums[:, 2 * passages : 3 * passages] + sums[:, passages : 2 * passages]
         out_ref[:, q * passages : (q + 1) * passages] = total + sums[:, :passages]
 
@@ -231,29 +253,53 @@
     passages = lengths.shape[0]
     tokens = owners * own * query_len
     rows = slot_centroid.size
-    plain = unit_queries(queries.reshape(own * query_len, feature))
+    plain = queries.reshape(own * query_len, feature)
+    members = members_of(own, owners, query_len)
+    members, slot_codes = lax.optimization_barrier((members, slot_codes))
     partner = lax.ppermute(plain, "wide", [(i, i ^ PAIR) for i in range(owners)])
-    vecs, live = decode(slot_centroid, lengths, slot_codes, codebook, centroids)
-    sent = spread(plain, partner, live, owners // 2)
+    sent = spread(plain, partner, owners // 2)
+    vecs, live, sent = decode(slot_centroid, lengths, slot_codes, codebook, centroids, sent)
     groups = [[i + z for i in range(owners) if not i & PAIR] for z in (0, PAIR)]
     gathered = lax.all_to_all(
         sent, "wide", split_axis=0, concat_axis=0, axis_index_groups=groups, tiled=True
     ).reshape(tokens, feature)
 
-    whole = lax.all_gather(vecs, "grp")
+    core = [(i, i ^ 1) for i in range(4)]
+    other = lax.ppermute(vecs, "grp", core)
+    far = lax.ppermute(vecs, "grp", [(i, i ^ 2) for i in range(4)])
+    far_other = lax.ppermute(far, "grp", core)
+    best_shape = jax.ShapeDtypeStruct((passages, tokens), jnp.float32)
+    block = pltpu.VMEM((rows, feature), jnp.bfloat16)
+    best = pl.pallas_call(
+        near_kernel,
+        out_shape=best_shape,
+        in_specs=[VMEM] * 4,
+        out_specs=VMEM,
+        scratch_shapes=[pltpu.VMEM((2 * rows, feature), jnp.bfloat16)],
+        compiler_params=params(24),
+        cost_estimate=cost(tokens, 2 * rows, feature),
+        name="score_near",
+    )(live, gathered, vecs, other)
+    best = pl.pallas_call(
+        far_kernel,
+        out_shape=best_shape,
+        in_specs=[VMEM] * 4,
+        out_specs=VMEM,
+        scratch_shapes=[block],
+        compiler_params=params(24),
+        cost_estimate=cost(tokens, rows, feature),
+        name="score_far",
+    )(live, gathered, far, best)
     table = pl.pallas_call(
-        score_kernel,
+        last_kernel,
         out_shape=jax.ShapeDtypeStruct((owners, LANES), jnp.float32),
-        in_specs=[VMEM] * 3,
-        out_specs=VMEM,
-        scratch_shapes=[
-            pltpu.VMEM((4 * rows, feature), jnp.bfloat16),
-            pltpu.VMEM((3 * passages, tokens), jnp.bfloat16),
-        ],
+        in_specs=[VMEM] * 5,
+        out_specs=VMEM,
+        scratch_shapes=[block, pltpu.VMEM((3 * passages, tokens), jnp.bfloat16)],
         compiler_params=params(24),
-        cost_estimate=cost(tokens, 4 * rows, feature),
-        name="score",
-    )(live, gathered, whole)
+        cost_estimate=cost(tokens, rows, feature),
+        name="score_last",
+    )(live, gathered, far_other, best, members)
     owned = lax.all_to_all(table, "wide", split_axis=0, concat_axis=0, tiled=True)
     return pick(owned, candidates, passages)
 

time: 44.6 us -> 42 us (0.942)
  blocking collectives: 23.6 us -> 12.8 us
  waiting for transfers between devices: 1.98 us -> 7.86 us
  starting transfers between devices: 9.2 us -> 13.2 us
  local copies, waits for them, and re-layouts: 1.4 us -> 0.03 us
    all_gather x1 -> x0, blocking collectives: 9.56 us -> none  [shards(): whole = lax.all_gather(vecs, 'grp')]
    ppermute x0 -> x3, starting transfers between devices: none -> 3.96 us  [the longest x1 3.96 us: shards(): far = lax.ppermute(vecs, 'grp', [(i, i ^ 2) for i in range(4)])]
    ppermute x0 -> x3, waiting for transfers between devices: none -> 2.95 us  [the longest x1 2.94 us: shards(): far = lax.ppermute(vecs, 'grp', [(i, i ^ 2) for i in range(4)])]
    all_to_all x1, waiting for transfers between devices: 1.98 us -> 3.69 us  [shards(): lax.all_to_all(sent, 'wide', split_axis=0, concat_axis=0, axis_index_grou...]
    unnamed x14 -> x16, local copies, waits for them, and re-layouts: 1.4 us -> 0.03 us
    all_to_all x1, blocking collectives: 14.1 us -> 12.8 us  [shards(): lax.all_to_all(table, 'wide', split_axis=0, concat_axis=0, tiled=True)]
    ppermute x1, waiting for transfers between devices: 0.01 us -> 1.22 us  [shards(): lax.ppermute(plain, 'wide', [(i, i ^ PAIR) for i in range(owners)])]
    pallas_call x4 -> x6, Pallas kernels: 6.43 us -> 6.05 us  [the longest x1 2.38 us: decode(): pl.pallas_call(gather_kernel, out_shape=jax.ShapeDtypeStruct((rows, featu...]
  transfers between devices with their start and end apart: 2 -> 5, of which waited for: 1 -> 3; matrix products, arithmetic and copies ran while one was open for 0% -> 0% of each run, Pallas kernels for 8% -> 6%
where the time goes in v4:
time: 42 us; the launch traced here: 41.7 us
  starting transfers between devices  13.2 us (31%)
  blocking collectives  12.8 us (30%)
  waiting for transfers between devices  7.86 us (19%)
  Pallas kernels  7.71 us (18%)
    all_to_all x1, blocking collectives, shards(): lax.all_to_all(table, 'wide', split_axis=0, concat_axis=0, tiled=True)  12.8 us
    all_to_all x1, starting transfers between devices, shards(): lax.all_to_all(sent, 'wide', split_axis=0, concat_axis=0, axis_index_grou...  7.15 us
    ppermute x1, starting transfers between devices, shards(): far = lax.ppermute(vecs, 'grp', [(i, i ^ 2) for i in range(4)])  3.96 us
    all_to_all x1, waiting for transfers between devices, shards(): lax.all_to_all(sent, 'wide', split_axis=0, concat_axis=0, axis_index_grou...  3.69 us
    ppermute x1, waiting for transfers between devices, shards(): far = lax.ppermute(vecs, 'grp', [(i, i ^ 2) for i in range(4)])  2.94 us
    pallas_call x1, Pallas kernels, decode(): pl.pallas_call(gather_kernel, out_shape=jax.ShapeDtypeStruct((rows, featu...  2.38 us
    ppermute x1, starting transfers between devices, shards(): lax.ppermute(plain, 'wide', [(i, i ^ PAIR) for i in range(owners)])  2.1 us
    pallas_call x1, Pallas kernels, shards(): pl.pallas_call(near_kernel, out_shape=best_shape, in_specs=[VMEM] * 4, ou...  1.26 us
  transfers between devices with their start and end apart: 5, of which 3 were waited for; matrix products, arithmetic and copies ran while one was open for 0% of the time, Pallas kernels for 6%

profile of v4, /device:TPU:0, one launch (start us, length us, event | category | flops | bytes accessed | tf_op | source)
XLA Modules:
  0.0 41.7 jit_solution(14878019904687083521)
XLA Ops:
  0.0 0.0 slice-start
  0.0 0.0 copy-start
  0.0 0.0 copy-start.1
  0.0 0.0 copy-start.5
  0.0 0.0 copy-start.2
  0.0 0.0 slice-start.1
  0.0 0.0 copy-start.3
  0.0 2.1 %collective-permute-start = (bf16[64,128]{1,0:T(8,128)(2,1)}, bf16[64,128]{1,0:T(8,128)(2,1)S(1)}, u32[]{:S(2)}, u32[]{:S(2)}) collective-permute-start(bf16[64,128]{1,0:T(8,128)(2,1)} %bitcast.14), channel_id=1, source_target_pairs={{0,4},{1,5},{2,6},{3,7},{4,0},{5,1},{6,2},{7,3},{8,12},{9,13},{10,... | collective-permute-start | bytes 49160 | tf_op jit(solution)/shard_map/ppermute | solution.py:259
  2.1 0.1 members.1
  2.2 0.0 copy-start.4
  2.2 0.0 copy-done
  2.2 0.0 copy-done.1
  2.2 0.0 copy-done.5
  2.2 0.6 %residual.1 = (f32[512,128]{1,0:T(8,128)S(1)}, s32[16,128]{1,0:T(8,128)S(1)}) custom-call(s32[16,1024]{1,0:T(8,128)S(1)} %copy-done, bf16[256,128]{1,0:T(8,128)(2,1)S(1)} %copy-done.1, s32[1,16]{1,0:T(1,128)S(1)} %bitcast.16), custom_call_target="tpu_custom_call" | custom-call | flops 16777216 | bytes 131072 | tf_op jit(solution)/shard_map/residual/pallas_call | solution.py:135
  2.8 1.2 %collective-permute-done.partner_ref = bf16[64,128]{1,0:T(8,128)(2,1)S(1)} collective-permute-done((bf16[64,128]{1,0:T(8,128)(2,1)}, bf16[64,128]{1,0:T(8,128)(2,1)S(1)}, u32[]{:S(2)}, u32[]{:S(2)}) %collective-permute-start) | collective-permute-done | bytes 16416 | tf_op jit(solution)/shard_map/ppermute | solution.py:259
  4.1 0.0 copy-done.2
  4.1 1.0 %spread.1 = bf16[16,128,128]{2,1,0:T(8,128)(2,1)} custom-call(bf16[64,128]{1,0:T(8,128)(2,1)S(1)} %bitcast.15, bf16[64,128]{1,0:T(8,128)(2,1)S(1)} %collective-permute-done.partner_ref), custom_call_target="tpu_custom_call" | custom-call | bytes 524288 | tf_op jit(solution)/shard_map/spread/pallas_call | solution.py:60
  5.0 0.0 slice-done
  5.0 0.0 slice-done.1
  5.0 0.0 copy-done.3
  5.0 2.4 %gather.1.own = bf16[512,128]{1,0:T(8,128)(2,1)S(1)} custom-call(s32[16,32]{1,0:T(8,128)S(1)} %copy-done.3, f32[512,128]{1,0:T(8,128)S(1)} %get-tuple-element.16.residual, bf16[32768,128]{1,0:T(8,128)(2,1)S(1)} %bitcast.8), custom_call_target="tpu_custom_call" | custom-call | flops 524288 | bytes 8388608 | tf_op jit(solution)/shard_map/gather/pallas_call | solution.py:148
  7.4 7.1 %all-to-all-start = ((bf16[16,128,128]{2,1,0:T(8,128)(2,1)}), bf16[16,128,128]{2,1,0:T(8,128)(2,1)S(1)}, u32[]{:S(2)}, u32[]{:S(2)}) async-start(bf16[16,128,128]{2,1,0:T(8,128)(2,1)} %spread.1), calls=%async_computation | async-start | bytes 1048576 | tf_op jit(solution)/shard_map/all_to_all | solution.py:263
  14.6 4.0 %collective-permute-start.1 = (bf16[512,128]{1,0:T(8,128)(2,1)S(1)}, bf16[512,128]{1,0:T(8,128)(2,1)S(1)}, u32[]{:S(2)}, u32[]{:S(2)}) collective-permute-start(bf16[512,128]{1,0:T(8,128)(2,1)S(1)} %gather.1.own), channel_id=1, source_target_pairs={{0,64},{32,96},{64,0},{96,32},{1,65},{33,97},{65,1},{97,33},{2,66}... | collective-permute-start | bytes 393224 | tf_op jit(solution)/shard_map/ppermute | solution.py:269
  18.5 0.0 collective-permute-start.3
  18.5 2.9 %collective-permute-done.1.vecs = bf16[512,128]{1,0:T(8,128)(2,1)S(1)} collective-permute-done((bf16[512,128]{1,0:T(8,128)(2,1)S(1)}, bf16[512,128]{1,0:T(8,128)(2,1)S(1)}, u32[]{:S(2)}, u32[]{:S(2)}) %collective-permute-start.1) | collective-permute-done | bytes 131104 | tf_op jit(solution)/shard_map/ppermute | solution.py:269
  21.5 0.0 collective-permute-start.2
  21.5 0.0 collective-permute-done.3.other
  21.5 3.7 %all-to-all-done = bf16[16,128,128]{2,1,0:T(8,128)(2,1)S(1)} async-done(((bf16[16,128,128]{2,1,0:T(8,128)(2,1)}), bf16[16,128,128]{2,1,0:T(8,128)(2,1)S(1)}, u32[]{:S(2)}, u32[]{:S(2)}) %all-to-all-start) | async-done | bytes 524320 | tf_op jit(solution)/shard_map/all_to_all | solution.py:263
  25.2 1.3 %score_near.1.before = f32[16,2048]{1,0:T(8,128)S(1)} custom-call(s32[16,128]{1,0:T(8,128)S(1)} %get-tuple-element.14.live, bf16[2048,128]{1,0:T(8,128)(2,1)S(1)} %bitcast.9, bf16[512,128]{1,0:T(8,128)(2,1)S(1)} %gather.1.own, bf16[512,128]{1,0:T(8,128)(2,1)S(1)} %collective-permute-done.3.other), custom_call_target="tpu_custom_call" | custom-call | flops 536870912 | bytes 786432 | tf_op jit(solution)/shard_map/score_near/pallas_call | solution.py:273
  26.5 0.7 %score_far.1.before = f32[16,2048]{1,0:T(8,128)S(1)} custom-call(s32[16,128]{1,0:T(8,128)S(1)} %get-tuple-element.14.live, bf16[2048,128]{1,0:T(8,128)(2,1)S(1)} %bitcast.10, bf16[512,128]{1,0:T(8,128)(2,1)S(1)} %collective-permute-done.1.vecs, f32[16,2048]{1,0:T(8,128)S(1)} %score_near.1.before), custom_call_target="tpu_custom_call" | custom-call | flops 268435456 | bytes 655360 | tf_op jit(solution)/shard_map/score_far/pallas_call | solution.py:283
  27.2 0.0 collective-permute-done.2.vecs
  27.2 1.0 %score_last.1 = f32[32,128]{1,0:T(8,128)S(1)} custom-call(s32[16,128]{1,0:T(8,128)S(1)} %get-tuple-element.14.live, bf16[2048,128]{1,0:T(8,128)(2,1)S(1)} %bitcast.11, bf16[512,128]{1,0:T(8,128)(2,1)S(1)} %collective-permute-done.2.vecs, f32[16,2048]{1,0:T(8,128)S(1)} %score_far.1.before, bf16[2,32,2048]{2,1,0:T(8,128)(2,1)S(1)} %members.1), custom_call_target="tpu_custom_call" | custom-call | flops 268435456 | bytes 655360 | tf_op jit(solution)/shard_map/score_last/pallas_call | solution.py:293
  28.2 12.8 %all_to_all.16 = f32[32,1,128]{2,1,0:T(1,128)S(1)} all-to-all(f32[32,1,128]{2,1,0:T(1,128)S(1)} %bitcast.12), channel_id=1, replica_groups=mesh['grp'=4,'wide'=32] {'wide'}, dimensions={0} | all-to-all | bytes 32768 | tf_op jit(solution)/shard_map/all_to_all | solution.py:303
  41.0 0.0 copy-done.4
  41.0 0.7 %pick.1 = f32[2,256]{1,0:T(2,128)} custom-call(f32[32,128]{1,0:T(8,128)S(1)} %bitcast.13, s32[2,256]{1,0:T(2,128)S(1)} %copy-done.4), custom_call_target="tpu_custom_call" | custom-call | flops 32768 | bytes 16384 | tf_op jit(solution)/shard_map/pick/pallas_call | solution.py:324
  (1 shorter events, 0.0 us)
Async XLA Ops:
  0.0 5.0 %slice-start = ((s8[8388608]{0:T(1024)(128)(4,1)}), s8[4194304]{0:T(1024)(128)(4,1)S(1)}, s32[]{:S(2)}) async-start(s8[8388608]{0:T(1024)(128)(4,1)} %bitcast.7), calls=%async_computation.2 | async-start | bytes 8388608
  0.0 2.2 %copy-start = (s32[16,1024]{1,0:T(8,128)S(1)}, s32[16,1024]{1,0:T(8,128)}, u32[]{:S(2)}) copy-start(s32[16,1024]{1,0:T(8,128)} %codes) | copy-start | bytes 196612
  0.0 2.2 %copy-start.1 = (bf16[256,128]{1,0:T(8,128)(2,1)S(1)}, bf16[256,128]{1,0:T(8,128)(2,1)}, u32[]{:S(2)}) copy-start(bf16[256,128]{1,0:T(8,128)(2,1)} %book.1) | copy-start | bytes 196612
  0.0 2.2 %copy-start.5 = (s32[16]{0:T(128)S(1)}, s32[16]{0:T(128)}, u32[]{:S(2)}) copy-start(s32[16]{0:T(128)} %param.12) | copy-start | bytes 196
  0.0 4.1 %copy-start.2 = (bf16[2,32,128]{2,1,0:T(8,128)(2,1)S(1)}, bf16[2,32,128]{2,1,0:T(8,128)(2,1)}, u32[]{:S(2)}) copy-start(bf16[2,32,128]{2,1,0:T(8,128)(2,1)} %param.7) | copy-start | bytes 49156
  0.0 5.0 %slice-start.1 = ((s8[8388608]{0:T(1024)(128)(4,1)}), s8[4194304]{0:T(1024)(128)(4,1)S(1)}, s32[]{:S(2)}) async-start(s8[8388608]{0:T(1024)(128)(4,1)} %bitcast.7), calls=%async_computation.3 | async-start | bytes 8388608
  0.0 5.0 %copy-start.3 = (s32[16,32]{1,0:T(8,128)S(1)}, s32[16,32]{1,0:T(8,128)}, u32[]{:S(2)}) copy-start(s32[16,32]{1,0:T(8,128)} %ids.1) | copy-start | bytes 6148
  0.0 4.0 %collective-permute-start = (bf16[64,128]{1,0:T(8,128)(2,1)}, bf16[64,128]{1,0:T(8,128)(2,1)S(1)}, u32[]{:S(2)}, u32[]{:S(2)}) collective-permute-start(bf16[64,128]{1,0:T(8,128)(2,1)} %bitcast.14), channel_id=1, source_target_pairs={{0,4},{1,5},{2,6},{3,7},{4,0},{5,1},{6,2},{7,3},{8,12},{9,13},{10,... | collective-permute-start | bytes 49160 | tf_op jit(solution)/shard_map/ppermute | solution.py:259
  2.2 38.8 %copy-start.4 = (s32[2,256]{1,0:T(2,128)S(1)}, s32[2,256]{1,0:T(2,128)}, u32[]{:S(2)}) copy-start(s32[2,256]{1,0:T(2,128)} %candidates_ref.1) | copy-start | bytes 6148
  7.4 17.8 %all-to-all-start = ((bf16[16,128,128]{2,1,0:T(8,128)(2,1)}), bf16[16,128,128]{2,1,0:T(8,128)(2,1)S(1)}, u32[]{:S(2)}, u32[]{:S(2)}) async-start(bf16[16,128,128]{2,1,0:T(8,128)(2,1)} %spread.1), calls=%async_computation | async-start | bytes 1048576 | tf_op jit(solution)/shard_map/all_to_all | solution.py:263
  14.6 6.9 %collective-permute-start.1 = (bf16[512,128]{1,0:T(8,128)(2,1)S(1)}, bf16[512,128]{1,0:T(8,128)(2,1)S(1)}, u32[]{:S(2)}, u32[]{:S(2)}) collective-permute-start(bf16[512,128]{1,0:T(8,128)(2,1)S(1)} %gather.1.own), channel_id=1, source_target_pairs={{0,64},{32,96},{64,0},{96,32},{1,65},{33,97},{65,1},{97,33},{2,66}... | collective-permute-start | bytes 393224 | tf_op jit(solution)/shard_map/ppermute | solution.py:269
  18.5 3.0 %collective-permute-start.3 = (bf16[512,128]{1,0:T(8,128)(2,1)S(1)}, bf16[512,128]{1,0:T(8,128)(2,1)S(1)}, u32[]{:S(2)}, u32[]{:S(2)}) collective-permute-start(bf16[512,128]{1,0:T(8,128)(2,1)S(1)} %gather.1.own), channel_id=1, source_target_pairs={{0,32},{32,0},{64,96},{96,64},{1,33},{33,1},{65,97},{97,65},{2,34}... | collective-permute-start | bytes 393224 | tf_op jit(solution)/shard_map/ppermute | solution.py:268
  21.5 5.7 %collective-permute-start.2 = (bf16[512,128]{1,0:T(8,128)(2,1)S(1)}, bf16[512,128]{1,0:T(8,128)(2,1)S(1)}, u32[]{:S(2)}, u32[]{:S(2)}) collective-permute-start(bf16[512,128]{1,0:T(8,128)(2,1)S(1)} %collective-permute-done.1.vecs), channel_id=1, source_target_pairs={{0,32},{32,0},{64,96},{96,64},{1,33},{33,1},{65,97},{97,65},{2,34}... | collective-permute-start | bytes 393224 | tf_op jit(solution)/shard_map/ppermute | solution.py:270

commit v5 on v4

--- a/solution.py
+++ b/solution.py
@@ -108,24 +108,23 @@
     passages, slots = ids.shape
     tiles = slots // PER_TILE
     count = table.shape[0]
-    sublane = lax.broadcasted_iota(jnp.int32, (8, LANES), 0)
-
+    span = passages * SLAB
+    row = lax.broadcasted_iota(jnp.int32, (SLAB, LANES), 0)
+    fold = (
+        lax.broadcasted_iota(jnp.int32, (passages, span), 0)
+        == lax.broadcasted_iota(jnp.int32, (passages, span), 1) // SLAB
+    ).astype(jnp.float32).astype(jnp.bfloat16)
     for m in range(slots):
         j = (m % tiles) * PER_TILE + m // tiles
-        halves = []
-        for h in range(0, passages, 8):
-            held = jnp.zeros((8, LANES), jnp.float32)
-            for q in range(8):
-                local = ids[h + q, j] & (count - 1)
-                base = pl.multiple_of(local & ~(SLAB - 1), SLAB)
-                slab = table[pl.ds(base, SLAB), :].astype(jnp.float32)
-                within = local & (SLAB - 1)
-                half = jnp.where(within >= 8, slab[8:], slab[:8])
-                held = jnp.where(sublane == q, pltpu.roll(half, (q - within) & 7, 0), held)
-            halves.append(held)
+        kept = []
+        for p in range(passages):
+            local = ids[p, j] & (count - 1)
+            base = pl.multiple_of(local & ~(SLAB - 1), SLAB)
+            slab = table[pl.ds(base, SLAB), :].astype(jnp.float32)
+            kept.append(jnp.where(row == (local & (SLAB - 1)), slab, 0.0).astype(jnp.bfloat16))
+        centre = jnp.dot(fold, jnp.concatenate(kept, axis=0), preferred_element_type=jnp.float32)
         at = m * passages
-        raw = jnp.concatenate(halves, axis=0) + residual[at : at + passages, :]
-        out_ref[at : at + passages, :] = unit(raw)
+        out_ref[at : at + passages, :] = unit(centre + residual[at : at + passages, :])
 
 
 def decode(slot_centroid, lengths, slot_codes, codebook, centroids, sent):

time: 42 us -> 41.3 us (0.983)
  Pallas kernels: 7.71 us -> 7.02 us
    pallas_call x1, Pallas kernels: 2.38 us -> 1.7 us  [decode(): pl.pallas_call(gather_kernel, out_shape=jax.ShapeDtypeStruct((rows, featu...]
where the time goes in v5:
time: 41.3 us; the launch traced here: 41.1 us
  starting transfers between devices  13.2 us (32%)
  blocking collectives  12.8 us (31%)
  waiting for transfers between devices  7.86 us (19%)
  Pallas kernels  7.02 us (17%)
    all_to_all x1, blocking collectives, shards(): lax.all_to_all(table, 'wide', split_axis=0, concat_axis=0, tiled=True)  12.8 us
    all_to_all x1, starting transfers between devices, shards(): lax.all_to_all(sent, 'wide', split_axis=0, concat_axis=0, axis_index_grou...  7.15 us
    ppermute x1, starting transfers between devices, shards(): far = lax.ppermute(vecs, 'grp', [(i, i ^ 2) for i in range(4)])  3.96 us
    all_to_all x1, waiting for transfers between devices, shards(): lax.all_to_all(sent, 'wide', split_axis=0, concat_axis=0, axis_index_grou...  3.69 us
    ppermute x1, waiting for transfers between devices, shards(): far = lax.ppermute(vecs, 'grp', [(i, i ^ 2) for i in range(4)])  2.94 us
    ppermute x1, starting transfers between devices, shards(): lax.ppermute(plain, 'wide', [(i, i ^ PAIR) for i in range(owners)])  2.1 us
    pallas_call x1, Pallas kernels, decode(): pl.pallas_call(gather_kernel, out_shape=jax.ShapeDtypeStruct((rows, featu...  1.7 us
    pallas_call x1, Pallas kernels, shards(): pl.pallas_call(near_kernel, out_shape=best_shape, in_specs=[VMEM] * 4, ou...  1.26 us
  transfers between devices with their start and end apart: 5, of which 3 were waited for; matrix products, arithmetic and copies ran while one was open for 0% of the time, Pallas kernels for 6%

profile of v5, /device:TPU:0, one launch (start us, length us, event | category | flops | bytes accessed | tf_op | source)
XLA Modules:
  0.0 41.1 jit_solution(18392451482765597877)
XLA Ops:
  0.0 0.0 slice-start
  0.0 0.0 copy-start
  0.0 0.0 copy-start.1
  0.0 0.0 copy-start.5
  0.0 0.0 copy-start.2
  0.0 0.0 slice-start.1
  0.0 0.0 copy-start.3
  0.0 2.1 %collective-permute-start = (bf16[64,128]{1,0:T(8,128)(2,1)}, bf16[64,128]{1,0:T(8,128)(2,1)S(1)}, u32[]{:S(2)}, u32[]{:S(2)}) collective-permute-start(bf16[64,128]{1,0:T(8,128)(2,1)} %bitcast.14), channel_id=1, source_target_pairs={{0,4},{1,5},{2,6},{3,7},{4,0},{5,1},{6,2},{7,3},{8,12},{9,13},{10,... | collective-permute-start | bytes 49160 | tf_op jit(solution)/shard_map/ppermute | solution.py:258
  2.1 0.1 members.1
  2.2 0.0 copy-start.4
  2.2 0.0 copy-done
  2.2 0.0 copy-done.1
  2.2 0.0 copy-done.5
  2.2 0.6 %residual.1 = (f32[512,128]{1,0:T(8,128)S(1)}, s32[16,128]{1,0:T(8,128)S(1)}) custom-call(s32[16,1024]{1,0:T(8,128)S(1)} %copy-done, bf16[256,128]{1,0:T(8,128)(2,1)S(1)} %copy-done.1, s32[1,16]{1,0:T(1,128)S(1)} %bitcast.16), custom_call_target="tpu_custom_call" | custom-call | flops 16777216 | bytes 131072 | tf_op jit(solution)/shard_map/residual/pallas_call | solution.py:134
  2.8 1.2 %collective-permute-done.partner_ref = bf16[64,128]{1,0:T(8,128)(2,1)S(1)} collective-permute-done((bf16[64,128]{1,0:T(8,128)(2,1)}, bf16[64,128]{1,0:T(8,128)(2,1)S(1)}, u32[]{:S(2)}, u32[]{:S(2)}) %collective-permute-start) | collective-permute-done | bytes 16416 | tf_op jit(solution)/shard_map/ppermute | solution.py:258
  4.1 0.0 copy-done.2
  4.1 1.0 %spread.1 = bf16[16,128,128]{2,1,0:T(8,128)(2,1)} custom-call(bf16[64,128]{1,0:T(8,128)(2,1)S(1)} %bitcast.15, bf16[64,128]{1,0:T(8,128)(2,1)S(1)} %collective-permute-done.partner_ref), custom_call_target="tpu_custom_call" | custom-call | bytes 524288 | tf_op jit(solution)/shard_map/spread/pallas_call | solution.py:60
  5.0 0.0 slice-done
  5.0 0.0 slice-done.1
  5.0 0.0 copy-done.3
  5.0 1.7 %gather.1.own = bf16[512,128]{1,0:T(8,128)(2,1)S(1)} custom-call(s32[16,32]{1,0:T(8,128)S(1)} %copy-done.3, f32[512,128]{1,0:T(8,128)S(1)} %get-tuple-element.16.residual, bf16[32768,128]{1,0:T(8,128)(2,1)S(1)} %bitcast.8), custom_call_target="tpu_custom_call" | custom-call | flops 524288 | bytes 8388608 | tf_op jit(solution)/shard_map/gather/pallas_call | solution.py:147
  6.7 7.1 %all-to-all-start = ((bf16[16,128,128]{2,1,0:T(8,128)(2,1)}), bf16[16,128,128]{2,1,0:T(8,128)(2,1)S(1)}, u32[]{:S(2)}, u32[]{:S(2)}) async-start(bf16[16,128,128]{2,1,0:T(8,128)(2,1)} %spread.1), calls=%async_computation | async-start | bytes 1048576 | tf_op jit(solution)/shard_map/all_to_all | solution.py:262
  13.9 4.0 %collective-permute-start.1 = (bf16[512,128]{1,0:T(8,128)(2,1)S(1)}, bf16[512,128]{1,0:T(8,128)(2,1)S(1)}, u32[]{:S(2)}, u32[]{:S(2)}) collective-permute-start(bf16[512,128]{1,0:T(8,128)(2,1)S(1)} %gather.1.own), channel_id=1, source_target_pairs={{0,64},{32,96},{64,0},{96,32},{1,65},{33,97},{65,1},{97,33},{2,66}... | collective-permute-start | bytes 393224 | tf_op jit(solution)/shard_map/ppermute | solution.py:268
  17.9 0.0 collective-permute-start.3
  17.9 2.9 %collective-permute-done.1.vecs = bf16[512,128]{1,0:T(8,128)(2,1)S(1)} collective-permute-done((bf16[512,128]{1,0:T(8,128)(2,1)S(1)}, bf16[512,128]{1,0:T(8,128)(2,1)S(1)}, u32[]{:S(2)}, u32[]{:S(2)}) %collective-permute-start.1) | collective-permute-done | bytes 131104 | tf_op jit(solution)/shard_map/ppermute | solution.py:268
  20.8 0.0 collective-permute-start.2
  20.8 0.0 collective-permute-done.3.other
  20.8 3.7 %all-to-all-done = bf16[16,128,128]{2,1,0:T(8,128)(2,1)S(1)} async-done(((bf16[16,128,128]{2,1,0:T(8,128)(2,1)}), bf16[16,128,128]{2,1,0:T(8,128)(2,1)S(1)}, u32[]{:S(2)}, u32[]{:S(2)}) %all-to-all-start) | async-done | bytes 524320 | tf_op jit(solution)/shard_map/all_to_all | solution.py:262
  24.5 1.3 %score_near.1.before = f32[16,2048]{1,0:T(8,128)S(1)} custom-call(s32[16,128]{1,0:T(8,128)S(1)} %get-tuple-element.14.live, bf16[2048,128]{1,0:T(8,128)(2,1)S(1)} %bitcast.9, bf16[512,128]{1,0:T(8,128)(2,1)S(1)} %gather.1.own, bf16[512,128]{1,0:T(8,128)(2,1)S(1)} %collective-permute-done.3.other), custom_call_target="tpu_custom_call" | custom-call | flops 536870912 | bytes 786432 | tf_op jit(solution)/shard_map/score_near/pallas_call | solution.py:272
  25.8 0.7 %score_far.1.before = f32[16,2048]{1,0:T(8,128)S(1)} custom-call(s32[16,128]{1,0:T(8,128)S(1)} %get-tuple-element.14.live, bf16[2048,128]{1,0:T(8,128)(2,1)S(1)} %bitcast.10, bf16[512,128]{1,0:T(8,128)(2,1)S(1)} %collective-permute-done.1.vecs, f32[16,2048]{1,0:T(8,128)S(1)} %score_near.1.before), custom_call_target="tpu_custom_call" | custom-call | flops 268435456 | bytes 655360 | tf_op jit(solution)/shard_map/score_far/pallas_call | solution.py:282
  26.5 0.0 collective-permute-done.2.vecs
  26.5 1.0 %score_last.1 = f32[32,128]{1,0:T(8,128)S(1)} custom-call(s32[16,128]{1,0:T(8,128)S(1)} %get-tuple-element.14.live, bf16[2048,128]{1,0:T(8,128)(2,1)S(1)} %bitcast.11, bf16[512,128]{1,0:T(8,128)(2,1)S(1)} %collective-permute-done.2.vecs, f32[16,2048]{1,0:T(8,128)S(1)} %score_far.1.before, bf16[2,32,2048]{2,1,0:T(8,128)(2,1)S(1)} %members.1), custom_call_target="tpu_custom_call" | custom-call | flops 268435456 | bytes 655360 | tf_op jit(solution)/shard_map/score_last/pallas_call | solution.py:292
  27.5 12.8 %all_to_all.16 = f32[32,1,128]{2,1,0:T(1,128)S(1)} all-to-all(f32[32,1,128]{2,1,0:T(1,128)S(1)} %bitcast.12), channel_id=1, replica_groups=mesh['grp'=4,'wide'=32] {'wide'}, dimensions={0} | all-to-all | bytes 32768 | tf_op jit(solution)/shard_map/all_to_all | solution.py:302
  40.4 0.0 copy-done.4
  40.4 0.7 %pick.1 = f32[2,256]{1,0:T(2,128)} custom-call(f32[32,128]{1,0:T(8,128)S(1)} %bitcast.13, s32[2,256]{1,0:T(2,128)S(1)} %copy-done.4), custom_call_target="tpu_custom_call" | custom-call | flops 32768 | bytes 16384 | tf_op jit(solution)/shard_map/pick/pallas_call | solution.py:323
  (1 shorter events, 0.0 us)
Async XLA Ops:
  0.0 5.0 %slice-start = ((s8[8388608]{0:T(1024)(128)(4,1)}), s8[4194304]{0:T(1024)(128)(4,1)S(1)}, s32[]{:S(2)}) async-start(s8[8388608]{0:T(1024)(128)(4,1)} %bitcast.7), calls=%async_computation.2 | async-start | bytes 8388608
  0.0 2.2 %copy-start = (s32[16,1024]{1,0:T(8,128)S(1)}, s32[16,1024]{1,0:T(8,128)}, u32[]{:S(2)}) copy-start(s32[16,1024]{1,0:T(8,128)} %codes) | copy-start | bytes 196612
  0.0 2.2 %copy-start.1 = (bf16[256,128]{1,0:T(8,128)(2,1)S(1)}, bf16[256,128]{1,0:T(8,128)(2,1)}, u32[]{:S(2)}) copy-start(bf16[256,128]{1,0:T(8,128)(2,1)} %book.1) | copy-start | bytes 196612
  0.0 2.2 %copy-start.5 = (s32[16]{0:T(128)S(1)}, s32[16]{0:T(128)}, u32[]{:S(2)}) copy-start(s32[16]{0:T(128)} %param.12) | copy-start | bytes 196
  0.0 4.1 %copy-start.2 = (bf16[2,32,128]{2,1,0:T(8,128)(2,1)S(1)}, bf16[2,32,128]{2,1,0:T(8,128)(2,1)}, u32[]{:S(2)}) copy-start(bf16[2,32,128]{2,1,0:T(8,128)(2,1)} %param.7) | copy-start | bytes 49156
  0.0 5.0 %slice-start.1 = ((s8[8388608]{0:T(1024)(128)(4,1)}), s8[4194304]{0:T(1024)(128)(4,1)S(1)}, s32[]{:S(2)}) async-start(s8[8388608]{0:T(1024)(128)(4,1)} %bitcast.7), calls=%async_computation.3 | async-start | bytes 8388608
  0.0 5.0 %copy-start.3 = (s32[16,32]{1,0:T(8,128)S(1)}, s32[16,32]{1,0:T(8,128)}, u32[]{:S(2)}) copy-start(s32[16,32]{1,0:T(8,128)} %ids.1) | copy-start | bytes 6148
  0.0 4.0 %collective-permute-start = (bf16[64,128]{1,0:T(8,128)(2,1)}, bf16[64,128]{1,0:T(8,128)(2,1)S(1)}, u32[]{:S(2)}, u32[]{:S(2)}) collective-permute-start(bf16[64,128]{1,0:T(8,128)(2,1)} %bitcast.14), channel_id=1, source_target_pairs={{0,4},{1,5},{2,6},{3,7},{4,0},{5,1},{6,2},{7,3},{8,12},{9,13},{10,... | collective-permute-start | bytes 49160 | tf_op jit(solution)/shard_map/ppermute | solution.py:258
  2.2 38.2 %copy-start.4 = (s32[2,256]{1,0:T(2,128)S(1)}, s32[2,256]{1,0:T(2,128)}, u32[]{:S(2)}) copy-start(s32[2,256]{1,0:T(2,128)} %candidates_ref.1) | copy-start | bytes 6148
  6.7 17.8 %all-to-all-start = ((bf16[16,128,128]{2,1,0:T(8,128)(2,1)}), bf16[16,128,128]{2,1,0:T(8,128)(2,1)S(1)}, u32[]{:S(2)}, u32[]{:S(2)}) async-start(bf16[16,128,128]{2,1,0:T(8,128)(2,1)} %spread.1), calls=%async_computation | async-start | bytes 1048576 | tf_op jit(solution)/shard_map/all_to_all | solution.py:262
  13.9 6.9 %collective-permute-start.1 = (bf16[512,128]{1,0:T(8,128)(2,1)S(1)}, bf16[512,128]{1,0:T(8,128)(2,1)S(1)}, u32[]{:S(2)}, u32[]{:S(2)}) collective-permute-start(bf16[512,128]{1,0:T(8,128)(2,1)S(1)} %gather.1.own), channel_id=1, source_target_pairs={{0,64},{32,96},{64,0},{96,32},{1,65},{33,97},{65,1},{97,33},{2,66}... | collective-permute-start | bytes 393224 | tf_op jit(solution)/shard_map/ppermute | solution.py:268
  17.9 3.0 %collective-permute-start.3 = (bf16[512,128]{1,0:T(8,128)(2,1)S(1)}, bf16[512,128]{1,0:T(8,128)(2,1)S(1)}, u32[]{:S(2)}, u32[]{:S(2)}) collective-permute-start(bf16[512,128]{1,0:T(8,128)(2,1)S(1)} %gather.1.own), channel_id=1, source_target_pairs={{0,32},{32,0},{64,96},{96,64},{1,33},{33,1},{65,97},{97,65},{2,34}... | collective-permute-start | bytes 393224 | tf_op jit(solution)/shard_map/ppermute | solution.py:267
  20.8 5.7 %collective-permute-start.2 = (bf16[512,128]{1,0:T(8,128)(2,1)S(1)}, bf16[512,128]{1,0:T(8,128)(2,1)S(1)}, u32[]{:S(2)}, u32[]{:S(2)}) collective-permute-start(bf16[512,128]{1,0:T(8,128)(2,1)S(1)} %collective-permute-done.1.vecs), channel_id=1, source_target_pairs={{0,32},{32,0},{64,96},{96,64},{1,33},{33,1},{65,97},{97,65},{2,34}... | collective-permute-start | bytes 393224 | tf_op jit(solution)/shard_map/ppermute | solution.py:269

commit v6 on v5

--- a/solution.py
+++ b/solution.py
@@ -13,6 +13,8 @@
 PIECES = 4
 LOWEST = -1e30
 PAIR = 4
+TURN = 3
+UPPER = 2
 NT = (((1,), (1,)), ((), ()))
 VMEM = pl.BlockSpec(memory_space=pltpu.VMEM)
 ANY = pl.BlockSpec(memory_space=pl.ANY)
@@ -23,20 +25,23 @@
     return (values * scale).astype(jnp.bfloat16)
 
 
-def members_kernel(query_len, out_ref):
-    own, owners, count = out_ref.shape
+def members_kernel(query_len, owners, out_ref):
+    rows, count = out_ref.shape
     query = lax.broadcasted_iota(jnp.int32, (owners, count), 1) // query_len
     owner = lax.broadcasted_iota(jnp.int32, (owners, count), 0)
-    pair = (owner // (2 * PAIR)) * PAIR + owner % PAIR
-    place = pair * 2 + (owner // PAIR) % 2
+    upper = (owner & UPPER) // UPPER
+    lower = jnp.where(upper == 1, owner ^ TURN, owner)
+    place = ((owner // 8) * 2 + (lower & 1)) * 4 + ((owner & PAIR) // PAIR) * 2 + upper
+    own = rows // owners
     for q in range(own):
-        out_ref[q] = (query == place * own + q).astype(jnp.float32).astype(jnp.bfloat16)
+        here = (query == place * own + q).astype(jnp.float32).astype(jnp.bfloat16)
+        out_ref[q * owners : (q + 1) * owners, :] = here
 
 
 def members_of(own, owners, query_len):
     return pl.pallas_call(
-        functools.partial(members_kernel, query_len),
-        out_shape=jax.ShapeDtypeStruct((own, owners, owners * own * query_len), jnp.bfloat16),
+        functools.partial(members_kernel, query_len, owners),
+        out_shape=jax.ShapeDtypeStruct((own * owners, owners * own * query_len), jnp.bfloat16),
         out_specs=VMEM,
         compiler_params=params(2),
         cost_estimate=pl.CostEstimate(flops=20000000000, bytes_accessed=1000, transcendentals=0),
@@ -44,28 +49,31 @@
     )()
 
 
-def spread_kernel(queries_ref, partner_ref, out_ref):
-    rows = queries_ref.shape[0]
-    low = (lax.axis_index("wide") & PAIR) == 0
-    own = unit(queries_ref[...].astype(jnp.float32))
-    partner = unit(partner_ref[...].astype(jnp.float32))
-    first, second = jnp.where(low, own, partner), jnp.where(low, partner, own)
-    for i in range(out_ref.shape[0]):
-        out_ref[i, 0:rows, :] = first
-        out_ref[i, rows : 2 * rows, :] = second
-
-
-def spread(queries, partner, count):
-    rows, feature = queries.shape
+def spread_kernel(own_ref, turned_ref, paired_ref, both_ref, after_ref, out_ref):
+    rows = own_ref.shape[0]
+    index = lax.axis_index("wide")
+    at = ((index & PAIR) // PAIR) * 2 + (index & UPPER) // UPPER
+    held = [unit(ref[...].astype(jnp.float32)) for ref in (own_ref, turned_ref, paired_ref, both_ref)]
+    for place in range(4):
+        step = jnp.bitwise_xor(at, place)
+        value = held[3]
+        for i in range(3):
+            value = jnp.where(step == i, held[i], value)
+        for i in range(out_ref.shape[0]):
+            out_ref[i, place * rows : (place + 1) * rows, :] = value
+
+
+def spread(pieces, after, count):
+    rows, feature = pieces[0].shape
     return pl.pallas_call(
         spread_kernel,
-        out_shape=jax.ShapeDtypeStruct((count, 2 * rows, feature), queries.dtype),
-        in_specs=[VMEM, VMEM],
+        out_shape=jax.ShapeDtypeStruct((count, 4 * rows, feature), pieces[0].dtype),
+        in_specs=[VMEM] * 4 + [ANY],
         out_specs=VMEM,
         compiler_params=params(4),
-        cost_estimate=pl.CostEstimate(flops=0, bytes_accessed=count * rows * feature * 4, transcendentals=0),
+        cost_estimate=pl.CostEstimate(flops=0, bytes_accessed=count * rows * feature * 8, transcendentals=0),
         name="spread",
-    )(queries, partner)
+    )(*pieces, after)
 
 
 def residual_rows(codes, codebook, store):
@@ -127,7 +135,7 @@
         out_ref[at : at + passages, :] = unit(centre + residual[at : at + passages, :])
 
 
-def decode(slot_centroid, lengths, slot_codes, codebook, centroids, sent):
+def decode(slot_centroid, lengths, slot_codes, codebook, centroids):
     passages, slots = slot_centroid.shape
     rows, feature = passages * slots, codebook.shape[1]
     smem = pl.BlockSpec(memory_space=pltpu.SMEM)
@@ -143,7 +151,6 @@
         cost_estimate=pl.CostEstimate(flops=rows * 256 * feature, bytes_accessed=rows * 256, transcendentals=0),
         name="residual",
     )(slot_codes, codebook, lengths.reshape(1, passages))
-    residual, sent = lax.optimization_barrier((residual, sent))
     vecs = pl.pallas_call(
         gather_kernel,
         out_shape=jax.ShapeDtypeStruct((rows, feature), jnp.bfloat16),
@@ -155,8 +162,7 @@
         ),
         name="gather",
     )(slot_centroid, residual, centroids)
-    vecs, sent = lax.optimization_barrier((vecs, sent))
-    return vecs, live, sent
+    return vecs, live
 
 
 def maxima(live, tokens, blocks, scratch, store):
@@ -228,10 +234,12 @@
             whole[i * passages : (i + 1) * passages, k : k + best.shape[1]] = part
 
     maxima(live[...], tokens, [(begin[3], vecs)], scratch, store)
-    for q in range(members.shape[0]):
-        sums = lax.dot_general(members[q], whole[...], NT, preferred_element_type=jnp.float32)
-        total = sums[:, 2 * passages : 3 * passages] + sums[:, passages : 2 * passages]
-        out_ref[:, q * passages : (q + 1) * passages] = total + sums[:, :passages]
+    sums = lax.dot_general(members[...], whole[...], NT, preferred_element_type=jnp.float32)
+    total = sums[:, 2 * passages : 3 * passages] + sums[:, passages : 2 * passages]
+    total = total + sums[:, :passages]
+    owners = out_ref.shape[0]
+    for q in range(members.shape[0] // owners):
+        out_ref[:, q * passages : (q + 1) * passages] = total[q * owners : (q + 1) * owners]
 
 
 def params(mebibytes):
@@ -255,10 +263,14 @@
     plain = queries.reshape(own * query_len, feature)
     members = members_of(own, owners, query_len)
     members, slot_codes = lax.optimization_barrier((members, slot_codes))
-    partner = lax.ppermute(plain, "wide", [(i, i ^ PAIR) for i in range(owners)])
-    sent = spread(plain, partner, owners // 2)
-    vecs, live, sent = decode(slot_centroid, lengths, slot_codes, codebook, centroids, sent)
-    groups = [[i + z for i in range(owners) if not i & PAIR] for z in (0, PAIR)]
+    pieces = [plain] + [
+        lax.ppermute(plain, "wide", [(i, i ^ step) for i in range(owners)])
+        for step in (TURN, PAIR, TURN ^ PAIR)
+    ]
+    vecs, live = decode(slot_centroid, lengths, slot_codes, codebook, centroids)
+    sent = spread(pieces, vecs, owners // 4)
+    base = [i for i in range(owners) if not i & (PAIR | UPPER)]
+    groups = [[i ^ step for i in base] for step in (0, TURN, PAIR, TURN ^ PAIR)]
     gathered = lax.all_to_all(
         sent, "wide", split_axis=0, concat_axis=0, axis_index_groups=groups, tiled=True
     ).reshape(tokens, feature)

time: 41.3 us -> 41.1 us (level)
  waiting for transfers between devices: 7.86 us -> 8.68 us
  blocking collectives: 12.8 us -> 12 us
    ppermute x1 -> x3, starting transfers between devices: 2.1 us -> 4.86 us  [shards(): lax.ppermute(plain, 'wide', [(i, i ^ step) for i in range(owners)])]
    all_to_all x1, starting transfers between devices: 7.15 us -> 4.47 us  [shards(): lax.all_to_all(sent, 'wide', split_axis=0, concat_axis=0, axis_index_grou...]
    ppermute x1 -> x3, waiting for transfers between devices: 1.22 us -> 3.58 us  [shards(): lax.ppermute(plain, 'wide', [(i, i ^ step) for i in range(owners)])]
    all_to_all x1, waiting for transfers between devices: 3.69 us -> 2.15 us  [shards(): lax.all_to_all(sent, 'wide', split_axis=0, concat_axis=0, axis_index_grou...]
    all_to_all x1, blocking collectives: 12.8 us -> 12 us  [shards(): lax.all_to_all(table, 'wide', split_axis=0, concat_axis=0, tiled=True)]
  transfers between devices with their start and end apart: 5 -> 7, of which waited for: 3 -> 3; matrix products, arithmetic and copies ran while one was open for 0% -> 0% of each run, Pallas kernels for 6% -> 11%
where the time goes in v6:
time: 41.1 us; the launch traced here: 40.9 us
  starting transfers between devices  12.9 us (31%)
  blocking collectives  12 us (29%)
  waiting for transfers between devices  8.68 us (21%)
  Pallas kernels  7.11 us (17%)
    all_to_all x1, blocking collectives, shards(): lax.all_to_all(table, 'wide', split_axis=0, concat_axis=0, tiled=True)  12 us
    ppermute x3, starting transfers between devices, shards(): lax.ppermute(plain, 'wide', [(i, i ^ step) for i in range(owners)])  4.86 us
    all_to_all x1, starting transfers between devices, shards(): lax.all_to_all(sent, 'wide', split_axis=0, concat_axis=0, axis_index_grou...  4.47 us
    ppermute x1, starting transfers between devices, shards(): far = lax.ppermute(vecs, 'grp', [(i, i ^ 2) for i in range(4)])  3.58 us
    ppermute x3, waiting for transfers between devices, shards(): lax.ppermute(plain, 'wide', [(i, i ^ step) for i in range(owners)])  3.58 us
    ppermute x1, waiting for transfers between devices, shards(): far = lax.ppermute(vecs, 'grp', [(i, i ^ 2) for i in range(4)])  2.94 us
    all_to_all x1, waiting for transfers between devices, shards(): lax.all_to_all(sent, 'wide', split_axis=0, concat_axis=0, axis_index_grou...  2.15 us
    pallas_call x1, Pallas kernels, decode(): pl.pallas_call(gather_kernel, out_shape=jax.ShapeDtypeStruct((rows, featu...  1.7 us
  transfers between devices with their start and end apart: 7, of which 3 were waited for; matrix products, arithmetic and copies ran while one was open for 0% of the time, Pallas kernels for 11%

profile of v6, /device:TPU:0, one launch (start us, length us, event | category | flops | bytes accessed | tf_op | source)
XLA Modules:
  0.0 40.9 jit_solution(2872950184348481477)
XLA Ops:
  0.0 0.0 slice-start
  0.0 0.0 copy-start
  0.0 0.0 copy-start.1
  0.0 0.0 copy-start.5
  0.0 0.0 slice-start.1
  0.0 0.0 copy-start.3
  0.0 2.9 %collective-permute-start = (bf16[64,128]{1,0:T(8,128)(2,1)}, bf16[64,128]{1,0:T(8,128)(2,1)S(1)}, u32[]{:S(2)}, u32[]{:S(2)}) collective-permute-start(bf16[64,128]{1,0:T(8,128)(2,1)} %bitcast.14), channel_id=1, source_target_pairs={{0,3},{1,2},{2,1},{3,0},{4,7},{5,6},{6,5},{7,4},{8,11},{9,10},{10,... | collective-permute-start | bytes 49160 | tf_op jit(solution)/shard_map/ppermute | solution.py:267
  3.0 1.9 %collective-permute-start.1 = (bf16[64,128]{1,0:T(8,128)(2,1)}, bf16[64,128]{1,0:T(8,128)(2,1)S(1)}, u32[]{:S(2)}, u32[]{:S(2)}) collective-permute-start(bf16[64,128]{1,0:T(8,128)(2,1)} %bitcast.15), channel_id=1, source_target_pairs={{0,4},{1,5},{2,6},{3,7},{4,0},{5,1},{6,2},{7,3},{8,12},{9,13},{10,... | collective-permute-start | bytes 49160 | tf_op jit(solution)/shard_map/ppermute | solution.py:267
  4.9 0.0 collective-permute-start.2
  4.9 0.1 members.1
  4.9 0.0 copy-start.2
  5.0 0.0 copy-start.4
  5.0 0.0 copy-done
  5.0 0.0 copy-done.1
  5.0 0.0 copy-done.5
  5.0 0.6 %residual.1 = (f32[512,128]{1,0:T(8,128)S(1)}, s32[16,128]{1,0:T(8,128)S(1)}) custom-call(s32[16,1024]{1,0:T(8,128)S(1)} %copy-done, bf16[256,128]{1,0:T(8,128)(2,1)S(1)} %copy-done.1, s32[1,16]{1,0:T(1,128)S(1)} %bitcast.18), custom_call_target="tpu_custom_call" | custom-call | flops 16777216 | bytes 131072 | tf_op jit(solution)/shard_map/residual/pallas_call | solution.py:142
  5.6 0.0 slice-done
  5.6 0.0 slice-done.1
  5.6 0.0 copy-done.3
  5.6 1.7 %gather.1.after_ref.own = bf16[512,128]{1,0:T(8,128)(2,1)S(1)} custom-call(s32[16,32]{1,0:T(8,128)S(1)} %copy-done.3, f32[512,128]{1,0:T(8,128)S(1)} %get-tuple-element.11.residual, bf16[32768,128]{1,0:T(8,128)(2,1)S(1)} %bitcast.8), custom_call_target="tpu_custom_call" | custom-call | flops 524288 | bytes 8388608 | tf_op jit(solution)/shard_map/gather/pallas_call | solution.py:154
  7.3 0.0 collective-permute-done.turned_ref
  7.4 0.0 collective-permute-done.1.paired_ref
  7.4 3.6 %collective-permute-done.2.both_ref = bf16[64,128]{1,0:T(8,128)(2,1)S(1)} collective-permute-done((bf16[64,128]{1,0:T(8,128)(2,1)}, bf16[64,128]{1,0:T(8,128)(2,1)S(1)}, u32[]{:S(2)}, u32[]{:S(2)}) %collective-permute-start.2) | collective-permute-done | bytes 16416 | tf_op jit(solution)/shard_map/ppermute | solution.py:267
  10.9 0.0 copy-done.2
  10.9 1.0 %spread.1 = bf16[8,256,128]{2,1,0:T(8,128)(2,1)} custom-call(bf16[64,128]{1,0:T(8,128)(2,1)S(1)} %bitcast.17, bf16[64,128]{1,0:T(8,128)(2,1)S(1)} %collective-permute-done.turned_ref, bf16[64,128]{1,0:T(8,128)(2,1)S(1)} %collective-permute-done.1.paired_ref, bf16[64,128]{1,0:T(8,128)(2,1)S(1)} %collective-permute-done.2.both_ref, ...), custom_call_target="tpu_custom_call" | custom-call | bytes 524288 | tf_op jit(solution)/shard_map/spread/pallas_call | solution.py:68
  11.9 4.5 %all-to-all-start = ((bf16[8,256,128]{2,1,0:T(8,128)(2,1)}), bf16[8,256,128]{2,1,0:T(8,128)(2,1)S(1)}, u32[]{:S(2)}, u32[]{:S(2)}) async-start(bf16[8,256,128]{2,1,0:T(8,128)(2,1)} %spread.1), calls=%async_computation | async-start | bytes 1048576 | tf_op jit(solution)/shard_map/all_to_all | solution.py:274
  16.4 3.6 %collective-permute-start.3 = (bf16[512,128]{1,0:T(8,128)(2,1)S(1)}, bf16[512,128]{1,0:T(8,128)(2,1)S(1)}, u32[]{:S(2)}, u32[]{:S(2)}) collective-permute-start(bf16[512,128]{1,0:T(8,128)(2,1)S(1)} %gather.1.after_ref.own), channel_id=1, source_target_pairs={{0,64},{32,96},{64,0},{96,32},{1,65},{33,97},{65,1},{97,33},{2,66}... | collective-permute-start | bytes 393224 | tf_op jit(solution)/shard_map/ppermute | solution.py:280
  20.0 0.0 collective-permute-start.5
  20.0 2.9 %collective-permute-done.3.vecs = bf16[512,128]{1,0:T(8,128)(2,1)S(1)} collective-permute-done((bf16[512,128]{1,0:T(8,128)(2,1)S(1)}, bf16[512,128]{1,0:T(8,128)(2,1)S(1)}, u32[]{:S(2)}, u32[]{:S(2)}) %collective-permute-start.3) | collective-permute-done | bytes 131104 | tf_op jit(solution)/shard_map/ppermute | solution.py:280
  22.9 0.0 collective-permute-start.4
  22.9 0.0 collective-permute-done.5.other
  22.9 2.2 %all-to-all-done = bf16[8,256,128]{2,1,0:T(8,128)(2,1)S(1)} async-done(((bf16[8,256,128]{2,1,0:T(8,128)(2,1)}), bf16[8,256,128]{2,1,0:T(8,128)(2,1)S(1)}, u32[]{:S(2)}, u32[]{:S(2)}) %all-to-all-start) | async-done | bytes 524320 | tf_op jit(solution)/shard_map/all_to_all | solution.py:274
  25.1 1.3 %score_near.1.before = f32[16,2048]{1,0:T(8,128)S(1)} custom-call(s32[16,128]{1,0:T(8,128)S(1)} %get-tuple-element.10.live, bf16[2048,128]{1,0:T(8,128)(2,1)S(1)} %bitcast.9, bf16[512,128]{1,0:T(8,128)(2,1)S(1)} %gather.1.after_ref.own, bf16[512,128]{1,0:T(8,128)(2,1)S(1)} %collective-permute-done.5.other), custom_call_target="tpu_custom_call" | custom-call | flops 536870912 | bytes 786432 | tf_op jit(solution)/shard_map/score_near/pallas_call | solution.py:284
  26.4 0.7 %score_far.1.before = f32[16,2048]{1,0:T(8,128)S(1)} custom-call(s32[16,128]{1,0:T(8,128)S(1)} %get-tuple-element.10.live, bf16[2048,128]{1,0:T(8,128)(2,1)S(1)} %bitcast.10, bf16[512,128]{1,0:T(8,128)(2,1)S(1)} %collective-permute-done.3.vecs, f32[16,2048]{1,0:T(8,128)S(1)} %score_near.1.before), custom_call_target="tpu_custom_call" | custom-call | flops 268435456 | bytes 655360 | tf_op jit(solution)/shard_map/score_far/pallas_call | solution.py:294
  27.1 0.0 collective-permute-done.4.vecs
  27.1 1.1 %score_last.1 = f32[32,128]{1,0:T(8,128)S(1)} custom-call(s32[16,128]{1,0:T(8,128)S(1)} %get-tuple-element.10.live, bf16[2048,128]{1,0:T(8,128)(2,1)S(1)} %bitcast.11, bf16[512,128]{1,0:T(8,128)(2,1)S(1)} %collective-permute-done.4.vecs, f32[16,2048]{1,0:T(8,128)S(1)} %score_far.1.before, bf16[64,2048]{1,0:T(8,128)(2,1)S(1)} %members.1), custom_call_target="tpu_custom_call" | custom-call | flops 268435456 | bytes 655360 | tf_op jit(solution)/shard_map/score_last/pallas_call | solution.py:304
  28.2 12.0 %all_to_all.16 = f32[32,1,128]{2,1,0:T(1,128)S(1)} all-to-all(f32[32,1,128]{2,1,0:T(1,128)S(1)} %bitcast.12), channel_id=1, replica_groups=mesh['grp'=4,'wide'=32] {'wide'}, dimensions={0} | all-to-all | bytes 32768 | tf_op jit(solution)/shard_map/all_to_all | solution.py:314
  40.2 0.0 copy-done.4
  40.2 0.7 %pick.1 = f32[2,256]{1,0:T(2,128)} custom-call(f32[32,128]{1,0:T(8,128)S(1)} %bitcast.13, s32[2,256]{1,0:T(2,128)S(1)} %copy-done.4), custom_call_target="tpu_custom_call" | custom-call | flops 32768 | bytes 16384 | tf_op jit(solution)/shard_map/pick/pallas_call | solution.py:335
  (1 shorter events, 0.0 us)
Async XLA Ops:
  0.0 5.6 %slice-start = ((s8[8388608]{0:T(1024)(128)(4,1)}), s8[4194304]{0:T(1024)(128)(4,1)S(1)}, s32[]{:S(2)}) async-start(s8[8388608]{0:T(1024)(128)(4,1)} %bitcast.7), calls=%async_computation.2 | async-start | bytes 8388608
  0.0 5.0 %copy-start = (s32[16,1024]{1,0:T(8,128)S(1)}, s32[16,1024]{1,0:T(8,128)}, u32[]{:S(2)}) copy-start(s32[16,1024]{1,0:T(8,128)} %codes) | copy-start | bytes 196612
  0.0 5.0 %copy-start.1 = (bf16[256,128]{1,0:T(8,128)(2,1)S(1)}, bf16[256,128]{1,0:T(8,128)(2,1)}, u32[]{:S(2)}) copy-start(bf16[256,128]{1,0:T(8,128)(2,1)} %book.1) | copy-start | bytes 196612
  0.0 5.0 %copy-start.5 = (s32[16]{0:T(128)S(1)}, s32[16]{0:T(128)}, u32[]{:S(2)}) copy-start(s32[16]{0:T(128)} %param.12) | copy-start | bytes 196
  0.0 5.6 %slice-start.1 = ((s8[8388608]{0:T(1024)(128)(4,1)}), s8[4194304]{0:T(1024)(128)(4,1)S(1)}, s32[]{:S(2)}) async-start(s8[8388608]{0:T(1024)(128)(4,1)} %bitcast.7), calls=%async_computation.3 | async-start | bytes 8388608
  0.0 5.6 %copy-start.3 = (s32[16,32]{1,0:T(8,128)S(1)}, s32[16,32]{1,0:T(8,128)}, u32[]{:S(2)}) copy-start(s32[16,32]{1,0:T(8,128)} %ids.1) | copy-start | bytes 6148
  0.0 7.3 %collective-permute-start = (bf16[64,128]{1,0:T(8,128)(2,1)}, bf16[64,128]{1,0:T(8,128)(2,1)S(1)}, u32[]{:S(2)}, u32[]{:S(2)}) collective-permute-start(bf16[64,128]{1,0:T(8,128)(2,1)} %bitcast.14), channel_id=1, source_target_pairs={{0,3},{1,2},{2,1},{3,0},{4,7},{5,6},{6,5},{7,4},{8,11},{9,10},{10,... | collective-permute-start | bytes 49160 | tf_op jit(solution)/shard_map/ppermute | solution.py:267
  3.0 4.4 %collective-permute-start.1 = (bf16[64,128]{1,0:T(8,128)(2,1)}, bf16[64,128]{1,0:T(8,128)(2,1)S(1)}, u32[]{:S(2)}, u32[]{:S(2)}) collective-permute-start(bf16[64,128]{1,0:T(8,128)(2,1)} %bitcast.15), channel_id=1, source_target_pairs={{0,4},{1,5},{2,6},{3,7},{4,0},{5,1},{6,2},{7,3},{8,12},{9,13},{10,... | collective-permute-start | bytes 49160 | tf_op jit(solution)/shard_map/ppermute | solution.py:267
  4.9 6.1 %collective-permute-start.2 = (bf16[64,128]{1,0:T(8,128)(2,1)}, bf16[64,128]{1,0:T(8,128)(2,1)S(1)}, u32[]{:S(2)}, u32[]{:S(2)}) collective-permute-start(bf16[64,128]{1,0:T(8,128)(2,1)} %bitcast.16), channel_id=1, source_target_pairs={{0,7},{1,6},{2,5},{3,4},{4,3},{5,2},{6,1},{7,0},{8,15},{9,14},{10,... | collective-permute-start | bytes 49160 | tf_op jit(solution)/shard_map/ppermute | solution.py:267
  4.9 6.0 %copy-start.2 = (bf16[2,32,128]{2,1,0:T(8,128)(2,1)S(1)}, bf16[2,32,128]{2,1,0:T(8,128)(2,1)}, u32[]{:S(2)}) copy-start(bf16[2,32,128]{2,1,0:T(8,128)(2,1)} %param.7) | copy-start | bytes 49156
  5.0 35.2 %copy-start.4 = (s32[2,256]{1,0:T(2,128)S(1)}, s32[2,256]{1,0:T(2,128)}, u32[]{:S(2)}) copy-start(s32[2,256]{1,0:T(2,128)} %candidates_ref.1) | copy-start | bytes 6148
  11.9 13.2 %all-to-all-start = ((bf16[8,256,128]{2,1,0:T(8,128)(2,1)}), bf16[8,256,128]{2,1,0:T(8,128)(2,1)S(1)}, u32[]{:S(2)}, u32[]{:S(2)}) async-start(bf16[8,256,128]{2,1,0:T(8,128)(2,1)} %spread.1), calls=%async_computation | async-start | bytes 1048576 | tf_op jit(solution)/shard_map/all_to_all | solution.py:274
  16.4 6.5 %collective-permute-start.3 = (bf16[512,128]{1,0:T(8,128)(2,1)S(1)}, bf16[512,128]{1,0:T(8,128)(2,1)S(1)}, u32[]{:S(2)}, u32[]{:S(2)}) collective-permute-start(bf16[512,128]{1,0:T(8,128)(2,1)S(1)} %gather.1.after_ref.own), channel_id=1, source_target_pairs={{0,64},{32,96},{64,0},{96,32},{1,65},{33,97},{65,1},{97,33},{2,66}... | collective-permute-start | bytes 393224 | tf_op jit(solution)/shard_map/ppermute | solution.py:280
  20.0 3.0 %collective-permute-start.5 = (bf16[512,128]{1,0:T(8,128)(2,1)S(1)}, bf16[512,128]{1,0:T(8,128)(2,1)S(1)}, u32[]{:S(2)}, u32[]{:S(2)}) collective-permute-start(bf16[512,128]{1,0:T(8,128)(2,1)S(1)} %gather.1.after_ref.own), channel_id=1, source_target_pairs={{0,32},{32,0},{64,96},{96,64},{1,33},{33,1},{65,97},{97,65},{2,34}... | collective-permute-start | bytes 393224 | tf_op jit(solution)/shard_map/ppermute | solution.py:279
  22.9 4.2 %collective-permute-start.4 = (bf16[512,128]{1,0:T(8,128)(2,1)S(1)}, bf16[512,128]{1,0:T(8,128)(2,1)S(1)}, u32[]{:S(2)}, u32[]{:S(2)}) collective-permute-start(bf16[512,128]{1,0:T(8,128)(2,1)S(1)} %collective-permute-done.3.vecs), channel_id=1, source_target_pairs={{0,32},{32,0},{64,96},{96,64},{1,33},{33,1},{65,97},{97,65},{2,34}... | collective-permute-start | bytes 393224 | tf_op jit(solution)/shard_map/ppermute | solution.py:281

commit v7 on v6

--- a/solution.py
+++ b/solution.py
@@ -202,22 +202,14 @@
     return [jnp.bitwise_xor(own, s) * slots for s in range(4)]
 
 
-def near_kernel(live, tokens, own, other, best_out, scratch):
+def first_kernel(live, tokens, own, other, far, best_out, scratch):
     begin = begins(own.shape[0] // live.shape[0])
 
     def store(k, best):
         best_out[:, k : k + best.shape[1]] = best
 
-    maxima(live[...], tokens, [(begin[0], own), (begin[1], other)], scratch, store)
-
-
-def far_kernel(live, tokens, vecs, before, best_out, scratch):
-    begin = begins(vecs.shape[0] // live.shape[0])
-
-    def store(k, best):
-        best_out[:, k : k + best.shape[1]] = jnp.maximum(best, before[:, k : k + best.shape[1]])
-
-    maxima(live[...], tokens, [(begin[2], vecs)], scratch, store)
+    blocks = list(zip(begin[:3], (own, other, far)))
+    maxima(live[...], tokens, blocks, scratch, store)
 
 
 def last_kernel(live, tokens, vecs, before, members, out_ref, scratch, whole):
@@ -282,25 +274,15 @@
     best_shape = jax.ShapeDtypeStruct((passages, tokens), jnp.float32)
     block = pltpu.VMEM((rows, feature), jnp.bfloat16)
     best = pl.pallas_call(
-        near_kernel,
+        first_kernel,
         out_shape=best_shape,
-        in_specs=[VMEM] * 4,
-        out_specs=VMEM,
-        scratch_shapes=[pltpu.VMEM((2 * rows, feature), jnp.bfloat16)],
+        in_specs=[VMEM] * 5,
+        out_specs=VMEM,
+        scratch_shapes=[pltpu.VMEM((3 * rows, feature), jnp.bfloat16)],
         compiler_params=params(24),
-        cost_estimate=cost(tokens, 2 * rows, feature),
-        name="score_near",
-    )(live, gathered, vecs, other)
-    best = pl.pallas_call(
-        far_kernel,
-        out_shape=best_shape,
-        in_specs=[VMEM] * 4,
-        out_specs=VMEM,
-        scratch_shapes=[block],
-        compiler_params=params(24),
-        cost_estimate=cost(tokens, rows, feature),
-        name="score_far",
-    )(live, gathered, far, best)
+        cost_estimate=cost(tokens, 3 * rows, feature),
+        name="score_first",
+    )(live, gathered, vecs, other, far)
     table = pl.pallas_call(
         last_kernel,
         out_shape=jax.ShapeDtypeStruct((owners, LANES), jnp.float32),

time: 41.1 us -> 40.9 us (level)
    pallas_call x2 -> x1, Pallas kernels: 1.98 us -> 1.81 us  [shards(): pl.pallas_call(first_kernel, out_shape=best_shape, in_specs=[VMEM] * 5, o...]
  transfers between devices with their start and end apart: 7 -> 7, of which waited for: 3 -> 3; matrix products, arithmetic and copies ran while one was open for 0% -> 0% of each run, Pallas kernels for 11% -> 10%
where the time goes in v7:
time: 40.9 us; the launch traced here: 40.7 us
  starting transfers between devices  12.9 us (32%)
  blocking collectives  12 us (29%)
  waiting for transfers between devices  8.68 us (21%)
  Pallas kernels  6.94 us (17%)
    all_to_all x1, blocking collectives, shards(): lax.all_to_all(table, 'wide', split_axis=0, concat_axis=0, tiled=True)  12 us
    ppermute x3, starting transfers between devices, shards(): lax.ppermute(plain, 'wide', [(i, i ^ step) for i in range(owners)])  4.86 us
    all_to_all x1, starting transfers between devices, shards(): lax.all_to_all(sent, 'wide', split_axis=0, concat_axis=0, axis_index_grou...  4.47 us
    ppermute x1, starting transfers between devices, shards(): far = lax.ppermute(vecs, 'grp', [(i, i ^ 2) for i in range(4)])  3.58 us
    ppermute x3, waiting for transfers between devices, shards(): lax.ppermute(plain, 'wide', [(i, i ^ step) for i in range(owners)])  3.58 us
    ppermute x1, waiting for transfers between devices, shards(): far = lax.ppermute(vecs, 'grp', [(i, i ^ 2) for i in range(4)])  2.94 us
    all_to_all x1, waiting for transfers between devices, shards(): lax.all_to_all(sent, 'wide', split_axis=0, concat_axis=0, axis_index_grou...  2.15 us
    pallas_call x1, Pallas kernels, shards(): pl.pallas_call(first_kernel, out_shape=best_shape, in_specs=[VMEM] * 5, o...  1.81 us
  transfers between devices with their start and end apart: 7, of which 3 were waited for; matrix products, arithmetic and copies ran while one was open for 0% of the time, Pallas kernels for 10%

profile of v7, /device:TPU:0, one launch (start us, length us, event | category | flops | bytes accessed | tf_op | source)
XLA Modules:
  0.0 40.7 jit_solution(16645703347591326105)
XLA Ops:
  0.0 0.0 slice-start
  0.0 0.0 copy-start
  0.0 0.0 copy-start.1
  0.0 0.0 copy-start.5
  0.0 0.0 slice-start.1
  0.0 0.0 copy-start.3
  0.0 2.9 %collective-permute-start = (bf16[64,128]{1,0:T(8,128)(2,1)}, bf16[64,128]{1,0:T(8,128)(2,1)S(1)}, u32[]{:S(2)}, u32[]{:S(2)}) collective-permute-start(bf16[64,128]{1,0:T(8,128)(2,1)} %bitcast.13), channel_id=1, source_target_pairs={{0,3},{1,2},{2,1},{3,0},{4,7},{5,6},{6,5},{7,4},{8,11},{9,10},{10,... | collective-permute-start | bytes 49160 | tf_op jit(solution)/shard_map/ppermute | solution.py:259
  3.0 1.9 %collective-permute-start.1 = (bf16[64,128]{1,0:T(8,128)(2,1)}, bf16[64,128]{1,0:T(8,128)(2,1)S(1)}, u32[]{:S(2)}, u32[]{:S(2)}) collective-permute-start(bf16[64,128]{1,0:T(8,128)(2,1)} %bitcast.14), channel_id=1, source_target_pairs={{0,4},{1,5},{2,6},{3,7},{4,0},{5,1},{6,2},{7,3},{8,12},{9,13},{10,... | collective-permute-start | bytes 49160 | tf_op jit(solution)/shard_map/ppermute | solution.py:259
  4.9 0.0 collective-permute-start.2
  4.9 0.1 members.1
  4.9 0.0 copy-start.2
  5.0 0.0 copy-start.4
  5.0 0.0 copy-done
  5.0 0.0 copy-done.1
  5.0 0.0 copy-done.5
  5.0 0.6 %residual.1 = (f32[512,128]{1,0:T(8,128)S(1)}, s32[16,128]{1,0:T(8,128)S(1)}) custom-call(s32[16,1024]{1,0:T(8,128)S(1)} %copy-done, bf16[256,128]{1,0:T(8,128)(2,1)S(1)} %copy-done.1, s32[1,16]{1,0:T(1,128)S(1)} %bitcast.17), custom_call_target="tpu_custom_call" | custom-call | flops 16777216 | bytes 131072 | tf_op jit(solution)/shard_map/residual/pallas_call | solution.py:142
  5.6 0.0 slice-done
  5.6 0.0 slice-done.1
  5.6 0.0 copy-done.3
  5.6 1.7 %gather.1.after_ref.own = bf16[512,128]{1,0:T(8,128)(2,1)S(1)} custom-call(s32[16,32]{1,0:T(8,128)S(1)} %copy-done.3, f32[512,128]{1,0:T(8,128)S(1)} %get-tuple-element.11.residual, bf16[32768,128]{1,0:T(8,128)(2,1)S(1)} %bitcast.8), custom_call_target="tpu_custom_call" | custom-call | flops 524288 | bytes 8388608 | tf_op jit(solution)/shard_map/gather/pallas_call | solution.py:154
  7.3 0.0 collective-permute-done.turned_ref
  7.4 0.0 collective-permute-done.1.paired_ref
  7.4 3.6 %collective-permute-done.2.both_ref = bf16[64,128]{1,0:T(8,128)(2,1)S(1)} collective-permute-done((bf16[64,128]{1,0:T(8,128)(2,1)}, bf16[64,128]{1,0:T(8,128)(2,1)S(1)}, u32[]{:S(2)}, u32[]{:S(2)}) %collective-permute-start.2) | collective-permute-done | bytes 16416 | tf_op jit(solution)/shard_map/ppermute | solution.py:259
  10.9 0.0 copy-done.2
  10.9 1.0 %spread.1 = bf16[8,256,128]{2,1,0:T(8,128)(2,1)} custom-call(bf16[64,128]{1,0:T(8,128)(2,1)S(1)} %bitcast.16, bf16[64,128]{1,0:T(8,128)(2,1)S(1)} %collective-permute-done.turned_ref, bf16[64,128]{1,0:T(8,128)(2,1)S(1)} %collective-permute-done.1.paired_ref, bf16[64,128]{1,0:T(8,128)(2,1)S(1)} %collective-permute-done.2.both_ref, ...), custom_call_target="tpu_custom_call" | custom-call | bytes 524288 | tf_op jit(solution)/shard_map/spread/pallas_call | solution.py:68
  11.9 4.5 %all-to-all-start = ((bf16[8,256,128]{2,1,0:T(8,128)(2,1)}), bf16[8,256,128]{2,1,0:T(8,128)(2,1)S(1)}, u32[]{:S(2)}, u32[]{:S(2)}) async-start(bf16[8,256,128]{2,1,0:T(8,128)(2,1)} %spread.1), calls=%async_computation | async-start | bytes 1048576 | tf_op jit(solution)/shard_map/all_to_all | solution.py:266
  16.4 3.6 %collective-permute-start.3 = (bf16[512,128]{1,0:T(8,128)(2,1)S(1)}, bf16[512,128]{1,0:T(8,128)(2,1)S(1)}, u32[]{:S(2)}, u32[]{:S(2)}) collective-permute-start(bf16[512,128]{1,0:T(8,128)(2,1)S(1)} %gather.1.after_ref.own), channel_id=1, source_target_pairs={{0,64},{32,96},{64,0},{96,32},{1,65},{33,97},{65,1},{97,33},{2,66}... | collective-permute-start | bytes 393224 | tf_op jit(solution)/shard_map/ppermute | solution.py:272
  20.0 0.0 collective-permute-start.5
  20.0 2.9 %collective-permute-done.3.far = bf16[512,128]{1,0:T(8,128)(2,1)S(1)} collective-permute-done((bf16[512,128]{1,0:T(8,128)(2,1)S(1)}, bf16[512,128]{1,0:T(8,128)(2,1)S(1)}, u32[]{:S(2)}, u32[]{:S(2)}) %collective-permute-start.3) | collective-permute-done | bytes 131104 | tf_op jit(solution)/shard_map/ppermute | solution.py:272
  22.9 0.0 collective-permute-start.4
  22.9 0.0 collective-permute-done.5.other
  22.9 2.2 %all-to-all-done = bf16[8,256,128]{2,1,0:T(8,128)(2,1)S(1)} async-done(((bf16[8,256,128]{2,1,0:T(8,128)(2,1)}), bf16[8,256,128]{2,1,0:T(8,128)(2,1)S(1)}, u32[]{:S(2)}, u32[]{:S(2)}) %all-to-all-start) | async-done | bytes 524320 | tf_op jit(solution)/shard_map/all_to_all | solution.py:266
  25.1 1.8 %score_first.1.before = f32[16,2048]{1,0:T(8,128)S(1)} custom-call(s32[16,128]{1,0:T(8,128)S(1)} %get-tuple-element.10.live, bf16[2048,128]{1,0:T(8,128)(2,1)S(1)} %bitcast.9, bf16[512,128]{1,0:T(8,128)(2,1)S(1)} %gather.1.after_ref.own, bf16[512,128]{1,0:T(8,128)(2,1)S(1)} %collective-permute-done.5.other, bf16[512,128]{1,0:T(8,128)(2,1)S(1)} %collective-permute-done.3.far), custom_call_target="tpu_custom_call" | custom-call | flops 805306368 | bytes 917504 | tf_op jit(solution)/shard_map/score_first/pallas_call | solution.py:276
  26.9 0.0 collective-permute-done.4.vecs
  26.9 1.1 %score_last.1 = f32[32,128]{1,0:T(8,128)S(1)} custom-call(s32[16,128]{1,0:T(8,128)S(1)} %get-tuple-element.10.live, bf16[2048,128]{1,0:T(8,128)(2,1)S(1)} %bitcast.10, bf16[512,128]{1,0:T(8,128)(2,1)S(1)} %collective-permute-done.4.vecs, f32[16,2048]{1,0:T(8,128)S(1)} %score_first.1.before, bf16[64,2048]{1,0:T(8,128)(2,1)S(1)} %members.1), custom_call_target="tpu_custom_call" | custom-call | flops 268435456 | bytes 655360 | tf_op jit(solution)/shard_map/score_last/pallas_call | solution.py:286
  28.0 12.0 %all_to_all.16 = f32[32,1,128]{2,1,0:T(1,128)S(1)} all-to-all(f32[32,1,128]{2,1,0:T(1,128)S(1)} %bitcast.11), channel_id=1, replica_groups=mesh['grp'=4,'wide'=32] {'wide'}, dimensions={0} | all-to-all | bytes 32768 | tf_op jit(solution)/shard_map/all_to_all | solution.py:296
  40.0 0.0 copy-done.4
  40.0 0.7 %pick.1 = f32[2,256]{1,0:T(2,128)} custom-call(f32[32,128]{1,0:T(8,128)S(1)} %bitcast.12, s32[2,256]{1,0:T(2,128)S(1)} %copy-done.4), custom_call_target="tpu_custom_call" | custom-call | flops 32768 | bytes 16384 | tf_op jit(solution)/shard_map/pick/pallas_call | solution.py:317
  (1 shorter events, 0.0 us)
Async XLA Ops:
  0.0 5.6 %slice-start = ((s8[8388608]{0:T(1024)(128)(4,1)}), s8[4194304]{0:T(1024)(128)(4,1)S(1)}, s32[]{:S(2)}) async-start(s8[8388608]{0:T(1024)(128)(4,1)} %bitcast.7), calls=%async_computation.2 | async-start | bytes 8388608
  0.0 5.0 %copy-start = (s32[16,1024]{1,0:T(8,128)S(1)}, s32[16,1024]{1,0:T(8,128)}, u32[]{:S(2)}) copy-start(s32[16,1024]{1,0:T(8,128)} %codes) | copy-start | bytes 196612
  0.0 5.0 %copy-start.1 = (bf16[256,128]{1,0:T(8,128)(2,1)S(1)}, bf16[256,128]{1,0:T(8,128)(2,1)}, u32[]{:S(2)}) copy-start(bf16[256,128]{1,0:T(8,128)(2,1)} %book.1) | copy-start | bytes 196612
  0.0 5.0 %copy-start.5 = (s32[16]{0:T(128)S(1)}, s32[16]{0:T(128)}, u32[]{:S(2)}) copy-start(s32[16]{0:T(128)} %param.12) | copy-start | bytes 196
  0.0 5.6 %slice-start.1 = ((s8[8388608]{0:T(1024)(128)(4,1)}), s8[4194304]{0:T(1024)(128)(4,1)S(1)}, s32[]{:S(2)}) async-start(s8[8388608]{0:T(1024)(128)(4,1)} %bitcast.7), calls=%async_computation.3 | async-start | bytes 8388608
  0.0 5.6 %copy-start.3 = (s32[16,32]{1,0:T(8,128)S(1)}, s32[16,32]{1,0:T(8,128)}, u32[]{:S(2)}) copy-start(s32[16,32]{1,0:T(8,128)} %ids.1) | copy-start | bytes 6148
  0.0 7.3 %collective-permute-start = (bf16[64,128]{1,0:T(8,128)(2,1)}, bf16[64,128]{1,0:T(8,128)(2,1)S(1)}, u32[]{:S(2)}, u32[]{:S(2)}) collective-permute-start(bf16[64,128]{1,0:T(8,128)(2,1)} %bitcast.13), channel_id=1, source_target_pairs={{0,3},{1,2},{2,1},{3,0},{4,7},{5,6},{6,5},{7,4},{8,11},{9,10},{10,... | collective-permute-start | bytes 49160 | tf_op jit(solution)/shard_map/ppermute | solution.py:259
  3.0 4.4 %collective-permute-start.1 = (bf16[64,128]{1,0:T(8,128)(2,1)}, bf16[64,128]{1,0:T(8,128)(2,1)S(1)}, u32[]{:S(2)}, u32[]{:S(2)}) collective-permute-start(bf16[64,128]{1,0:T(8,128)(2,1)} %bitcast.14), channel_id=1, source_target_pairs={{0,4},{1,5},{2,6},{3,7},{4,0},{5,1},{6,2},{7,3},{8,12},{9,13},{10,... | collective-permute-start | bytes 49160 | tf_op jit(solution)/shard_map/ppermute | solution.py:259
  4.9 6.1 %collective-permute-start.2 = (bf16[64,128]{1,0:T(8,128)(2,1)}, bf16[64,128]{1,0:T(8,128)(2,1)S(1)}, u32[]{:S(2)}, u32[]{:S(2)}) collective-permute-start(bf16[64,128]{1,0:T(8,128)(2,1)} %bitcast.15), channel_id=1, source_target_pairs={{0,7},{1,6},{2,5},{3,4},{4,3},{5,2},{6,1},{7,0},{8,15},{9,14},{10,... | collective-permute-start | bytes 49160 | tf_op jit(solution)/shard_map/ppermute | solution.py:259
  4.9 6.0 %copy-start.2 = (bf16[2,32,128]{2,1,0:T(8,128)(2,1)S(1)}, bf16[2,32,128]{2,1,0:T(8,128)(2,1)}, u32[]{:S(2)}) copy-start(bf16[2,32,128]{2,1,0:T(8,128)(2,1)} %param.7) | copy-start | bytes 49156
  5.0 35.1 %copy-start.4 = (s32[2,256]{1,0:T(2,128)S(1)}, s32[2,256]{1,0:T(2,128)}, u32[]{:S(2)}) copy-start(s32[2,256]{1,0:T(2,128)} %candidates_ref.1) | copy-start | bytes 6148
  11.9 13.2 %all-to-all-start = ((bf16[8,256,128]{2,1,0:T(8,128)(2,1)}), bf16[8,256,128]{2,1,0:T(8,128)(2,1)S(1)}, u32[]{:S(2)}, u32[]{:S(2)}) async-start(bf16[8,256,128]{2,1,0:T(8,128)(2,1)} %spread.1), calls=%async_computation | async-start | bytes 1048576 | tf_op jit(solution)/shard_map/all_to_all | solution.py:266
  16.4 6.5 %collective-permute-start.3 = (bf16[512,128]{1,0:T(8,128)(2,1)S(1)}, bf16[512,128]{1,0:T(8,128)(2,1)S(1)}, u32[]{:S(2)}, u32[]{:S(2)}) collective-permute-start(bf16[512,128]{1,0:T(8,128)(2,1)S(1)} %gather.1.after_ref.own), channel_id=1, source_target_pairs={{0,64},{32,96},{64,0},{96,32},{1,65},{33,97},{65,1},{97,33},{2,66}... | collective-permute-start | bytes 393224 | tf_op jit(solution)/shard_map/ppermute | solution.py:272
  20.0 3.0 %collective-permute-start.5 = (bf16[512,128]{1,0:T(8,128)(2,1)S(1)}, bf16[512,128]{1,0:T(8,128)(2,1)S(1)}, u32[]{:S(2)}, u32[]{:S(2)}) collective-permute-start(bf16[512,128]{1,0:T(8,128)(2,1)S(1)} %gather.1.after_ref.own), channel_id=1, source_target_pairs={{0,32},{32,0},{64,96},{96,64},{1,33},{33,1},{65,97},{97,65},{2,34}... | collective-permute-start | bytes 393224 | tf_op jit(solution)/shard_map/ppermute | solution.py:271
  22.9 4.0 %collective-permute-start.4 = (bf16[512,128]{1,0:T(8,128)(2,1)S(1)}, bf16[512,128]{1,0:T(8,128)(2,1)S(1)}, u32[]{:S(2)}, u32[]{:S(2)}) collective-permute-start(bf16[512,128]{1,0:T(8,128)(2,1)S(1)} %collective-permute-done.3.far), channel_id=1, source_target_pairs={{0,32},{32,0},{64,96},{96,64},{1,33},{33,1},{65,97},{97,65},{2,34}... | collective-permute-start | bytes 393224 | tf_op jit(solution)/shard_map/ppermute | solution.py:273

commit v8 on v7

--- a/solution.py
+++ b/solution.py
@@ -117,7 +117,8 @@
     tiles = slots // PER_TILE
     count = table.shape[0]
     span = passages * SLAB
-    row = lax.broadcasted_iota(jnp.int32, (SLAB, LANES), 0)
+    row = lax.broadcasted_iota(jnp.int32, (SLAB, LANES), 0).astype(jnp.int16)
+    none = jnp.zeros((SLAB, LANES), jnp.bfloat16)
     fold = (
         lax.broadcasted_iota(jnp.int32, (passages, span), 0)
         == lax.broadcasted_iota(jnp.int32, (passages, span), 1) // SLAB
@@ -128,8 +129,8 @@
         for p in range(passages):
             local = ids[p, j] & (count - 1)
             base = pl.multiple_of(local & ~(SLAB - 1), SLAB)
-            slab = table[pl.ds(base, SLAB), :].astype(jnp.float32)
-            kept.append(jnp.where(row == (local & (SLAB - 1)), slab, 0.0).astype(jnp.bfloat16))
+            wanted = jnp.full((SLAB, LANES), local & (SLAB - 1), jnp.int32).astype(jnp.int16)
+            kept.append(jnp.where(row == wanted, table[pl.ds(base, SLAB), :], none))
         centre = jnp.dot(fold, jnp.concatenate(kept, axis=0), preferred_element_type=jnp.float32)
         at = m * passages
         out_ref[at : at + passages, :] = unit(centre + residual[at : at + passages, :])

time: 40.9 us -> 40.9 us (level)
  no operation moved by 1% of the time
where the time goes in v8:
time: 40.9 us; the launch traced here: 40.7 us
  starting transfers between devices  12.9 us (32%)
  blocking collectives  12 us (29%)
  waiting for transfers between devices  8.69 us (21%)
  Pallas kernels  6.92 us (17%)
    all_to_all x1, blocking collectives, shards(): lax.all_to_all(table, 'wide', split_axis=0, concat_axis=0, tiled=True)  12 us
    ppermute x3, starting transfers between devices, shards(): lax.ppermute(plain, 'wide', [(i, i ^ step) for i in range(owners)])  4.86 us
    all_to_all x1, starting transfers between devices, shards(): lax.all_to_all(sent, 'wide', split_axis=0, concat_axis=0, axis_index_grou...  4.47 us
    ppermute x3, waiting for transfers between devices, shards(): lax.ppermute(plain, 'wide', [(i, i ^ step) for i in range(owners)])  3.59 us
    ppermute x1, starting transfers between devices, shards(): far = lax.ppermute(vecs, 'grp', [(i, i ^ 2) for i in range(4)])  3.58 us
    ppermute x1, waiting for transfers between devices, shards(): far = lax.ppermute(vecs, 'grp', [(i, i ^ 2) for i in range(4)])  2.94 us
    all_to_all x1, waiting for transfers between devices, shards(): lax.all_to_all(sent, 'wide', split_axis=0, concat_axis=0, axis_index_grou...  2.15 us
    pallas_call x1, Pallas kernels, shards(): pl.pallas_call(first_kernel, out_shape=best_shape, in_specs=[VMEM] * 5, o...  1.81 us
  transfers between devices with their start and end apart: 7, of which 3 were waited for; matrix products, arithmetic and copies ran while one was open for 0% of the time, Pallas kernels for 10%

profile of v8, /device:TPU:0, one launch (start us, length us, event | category | flops | bytes accessed | tf_op | source)
XLA Modules:
  0.0 40.7 jit_solution(1991124930771377394)
XLA Ops:
  0.0 0.0 slice-start
  0.0 0.0 copy-start
  0.0 0.0 copy-start.1
  0.0 0.0 copy-start.5
  0.0 0.0 slice-start.1
  0.0 0.0 copy-start.3
  0.0 2.9 %collective-permute-start = (bf16[64,128]{1,0:T(8,128)(2,1)}, bf16[64,128]{1,0:T(8,128)(2,1)S(1)}, u32[]{:S(2)}, u32[]{:S(2)}) collective-permute-start(bf16[64,128]{1,0:T(8,128)(2,1)} %bitcast.13), channel_id=1, source_target_pairs={{0,3},{1,2},{2,1},{3,0},{4,7},{5,6},{6,5},{7,4},{8,11},{9,10},{10,... | collective-permute-start | bytes 49160 | tf_op jit(solution)/shard_map/ppermute | solution.py:260
  3.0 1.9 %collective-permute-start.1 = (bf16[64,128]{1,0:T(8,128)(2,1)}, bf16[64,128]{1,0:T(8,128)(2,1)S(1)}, u32[]{:S(2)}, u32[]{:S(2)}) collective-permute-start(bf16[64,128]{1,0:T(8,128)(2,1)} %bitcast.14), channel_id=1, source_target_pairs={{0,4},{1,5},{2,6},{3,7},{4,0},{5,1},{6,2},{7,3},{8,12},{9,13},{10,... | collective-permute-start | bytes 49160 | tf_op jit(solution)/shard_map/ppermute | solution.py:260
  4.9 0.0 collective-permute-start.2
  4.9 0.1 members.1
  4.9 0.0 copy-start.2
  5.0 0.0 copy-start.4
  5.0 0.0 copy-done
  5.0 0.0 copy-done.1
  5.0 0.0 copy-done.5
  5.0 0.6 %residual.1 = (f32[512,128]{1,0:T(8,128)S(1)}, s32[16,128]{1,0:T(8,128)S(1)}) custom-call(s32[16,1024]{1,0:T(8,128)S(1)} %copy-done, bf16[256,128]{1,0:T(8,128)(2,1)S(1)} %copy-done.1, s32[1,16]{1,0:T(1,128)S(1)} %bitcast.17), custom_call_target="tpu_custom_call" | custom-call | flops 16777216 | bytes 131072 | tf_op jit(solution)/shard_map/residual/pallas_call | solution.py:143
  5.6 0.0 slice-done
  5.6 0.0 slice-done.1
  5.6 0.0 copy-done.3
  5.6 1.7 %gather.1.after_ref.own = bf16[512,128]{1,0:T(8,128)(2,1)S(1)} custom-call(s32[16,32]{1,0:T(8,128)S(1)} %copy-done.3, f32[512,128]{1,0:T(8,128)S(1)} %get-tuple-element.11.residual, bf16[32768,128]{1,0:T(8,128)(2,1)S(1)} %bitcast.8), custom_call_target="tpu_custom_call" | custom-call | flops 524288 | bytes 8388608 | tf_op jit(solution)/shard_map/gather/pallas_call | solution.py:155
  7.3 0.0 collective-permute-done.turned_ref
  7.3 0.0 collective-permute-done.1.paired_ref
  7.3 3.6 %collective-permute-done.2.both_ref = bf16[64,128]{1,0:T(8,128)(2,1)S(1)} collective-permute-done((bf16[64,128]{1,0:T(8,128)(2,1)}, bf16[64,128]{1,0:T(8,128)(2,1)S(1)}, u32[]{:S(2)}, u32[]{:S(2)}) %collective-permute-start.2) | collective-permute-done | bytes 16416 | tf_op jit(solution)/shard_map/ppermute | solution.py:260
  10.9 0.0 copy-done.2
  10.9 1.0 %spread.1 = bf16[8,256,128]{2,1,0:T(8,128)(2,1)} custom-call(bf16[64,128]{1,0:T(8,128)(2,1)S(1)} %bitcast.16, bf16[64,128]{1,0:T(8,128)(2,1)S(1)} %collective-permute-done.turned_ref, bf16[64,128]{1,0:T(8,128)(2,1)S(1)} %collective-permute-done.1.paired_ref, bf16[64,128]{1,0:T(8,128)(2,1)S(1)} %collective-permute-done.2.both_ref, ...), custom_call_target="tpu_custom_call" | custom-call | bytes 524288 | tf_op jit(solution)/shard_map/spread/pallas_call | solution.py:68
  11.9 4.5 %all-to-all-start = ((bf16[8,256,128]{2,1,0:T(8,128)(2,1)}), bf16[8,256,128]{2,1,0:T(8,128)(2,1)S(1)}, u32[]{:S(2)}, u32[]{:S(2)}) async-start(bf16[8,256,128]{2,1,0:T(8,128)(2,1)} %spread.1), calls=%async_computation | async-start | bytes 1048576 | tf_op jit(solution)/shard_map/all_to_all | solution.py:267
  16.4 3.6 %collective-permute-start.3 = (bf16[512,128]{1,0:T(8,128)(2,1)S(1)}, bf16[512,128]{1,0:T(8,128)(2,1)S(1)}, u32[]{:S(2)}, u32[]{:S(2)}) collective-permute-start(bf16[512,128]{1,0:T(8,128)(2,1)S(1)} %gather.1.after_ref.own), channel_id=1, source_target_pairs={{0,64},{32,96},{64,0},{96,32},{1,65},{33,97},{65,1},{97,33},{2,66}... | collective-permute-start | bytes 393224 | tf_op jit(solution)/shard_map/ppermute | solution.py:273
  20.0 0.0 collective-permute-start.5
  20.0 2.9 %collective-permute-done.3.far = bf16[512,128]{1,0:T(8,128)(2,1)S(1)} collective-permute-done((bf16[512,128]{1,0:T(8,128)(2,1)S(1)}, bf16[512,128]{1,0:T(8,128)(2,1)S(1)}, u32[]{:S(2)}, u32[]{:S(2)}) %collective-permute-start.3) | collective-permute-done | bytes 131104 | tf_op jit(solution)/shard_map/ppermute | solution.py:273
  22.9 0.0 collective-permute-start.4
  22.9 0.0 collective-permute-done.5.other
  22.9 2.2 %all-to-all-done = bf16[8,256,128]{2,1,0:T(8,128)(2,1)S(1)} async-done(((bf16[8,256,128]{2,1,0:T(8,128)(2,1)}), bf16[8,256,128]{2,1,0:T(8,128)(2,1)S(1)}, u32[]{:S(2)}, u32[]{:S(2)}) %all-to-all-start) | async-done | bytes 524320 | tf_op jit(solution)/shard_map/all_to_all | solution.py:267
  25.1 1.8 %score_first.1.before = f32[16,2048]{1,0:T(8,128)S(1)} custom-call(s32[16,128]{1,0:T(8,128)S(1)} %get-tuple-element.10.live, bf16[2048,128]{1,0:T(8,128)(2,1)S(1)} %bitcast.9, bf16[512,128]{1,0:T(8,128)(2,1)S(1)} %gather.1.after_ref.own, bf16[512,128]{1,0:T(8,128)(2,1)S(1)} %collective-permute-done.5.other, bf16[512,128]{1,0:T(8,128)(2,1)S(1)} %collective-permute-done.3.far), custom_call_target="tpu_custom_call" | custom-call | flops 805306368 | bytes 917504 | tf_op jit(solution)/shard_map/score_first/pallas_call | solution.py:277
  26.9 0.0 collective-permute-done.4.vecs
  26.9 1.1 %score_last.1 = f32[32,128]{1,0:T(8,128)S(1)} custom-call(s32[16,128]{1,0:T(8,128)S(1)} %get-tuple-element.10.live, bf16[2048,128]{1,0:T(8,128)(2,1)S(1)} %bitcast.10, bf16[512,128]{1,0:T(8,128)(2,1)S(1)} %collective-permute-done.4.vecs, f32[16,2048]{1,0:T(8,128)S(1)} %score_first.1.before, bf16[64,2048]{1,0:T(8,128)(2,1)S(1)} %members.1), custom_call_target="tpu_custom_call" | custom-call | flops 268435456 | bytes 655360 | tf_op jit(solution)/shard_map/score_last/pallas_call | solution.py:287
  28.0 12.0 %all_to_all.16 = f32[32,1,128]{2,1,0:T(1,128)S(1)} all-to-all(f32[32,1,128]{2,1,0:T(1,128)S(1)} %bitcast.11), channel_id=1, replica_groups=mesh['grp'=4,'wide'=32] {'wide'}, dimensions={0} | all-to-all | bytes 32768 | tf_op jit(solution)/shard_map/all_to_all | solution.py:297
  40.0 0.0 copy-done.4
  40.0 0.7 %pick.1 = f32[2,256]{1,0:T(2,128)} custom-call(f32[32,128]{1,0:T(8,128)S(1)} %bitcast.12, s32[2,256]{1,0:T(2,128)S(1)} %copy-done.4), custom_call_target="tpu_custom_call" | custom-call | flops 32768 | bytes 16384 | tf_op jit(solution)/shard_map/pick/pallas_call | solution.py:318
  (1 shorter events, 0.0 us)
Async XLA Ops:
  0.0 5.6 %slice-start = ((s8[8388608]{0:T(1024)(128)(4,1)}), s8[4194304]{0:T(1024)(128)(4,1)S(1)}, s32[]{:S(2)}) async-start(s8[8388608]{0:T(1024)(128)(4,1)} %bitcast.7), calls=%async_computation.2 | async-start | bytes 8388608
  0.0 5.0 %copy-start = (s32[16,1024]{1,0:T(8,128)S(1)}, s32[16,1024]{1,0:T(8,128)}, u32[]{:S(2)}) copy-start(s32[16,1024]{1,0:T(8,128)} %codes) | copy-start | bytes 196612
  0.0 5.0 %copy-start.1 = (bf16[256,128]{1,0:T(8,128)(2,1)S(1)}, bf16[256,128]{1,0:T(8,128)(2,1)}, u32[]{:S(2)}) copy-start(bf16[256,128]{1,0:T(8,128)(2,1)} %book.1) | copy-start | bytes 196612
  0.0 5.0 %copy-start.5 = (s32[16]{0:T(128)S(1)}, s32[16]{0:T(128)}, u32[]{:S(2)}) copy-start(s32[16]{0:T(128)} %param.12) | copy-start | bytes 196
  0.0 5.6 %slice-start.1 = ((s8[8388608]{0:T(1024)(128)(4,1)}), s8[4194304]{0:T(1024)(128)(4,1)S(1)}, s32[]{:S(2)}) async-start(s8[8388608]{0:T(1024)(128)(4,1)} %bitcast.7), calls=%async_computation.3 | async-start | bytes 8388608
  0.0 5.6 %copy-start.3 = (s32[16,32]{1,0:T(8,128)S(1)}, s32[16,32]{1,0:T(8,128)}, u32[]{:S(2)}) copy-start(s32[16,32]{1,0:T(8,128)} %ids.1) | copy-start | bytes 6148
  0.0 7.3 %collective-permute-start = (bf16[64,128]{1,0:T(8,128)(2,1)}, bf16[64,128]{1,0:T(8,128)(2,1)S(1)}, u32[]{:S(2)}, u32[]{:S(2)}) collective-permute-start(bf16[64,128]{1,0:T(8,128)(2,1)} %bitcast.13), channel_id=1, source_target_pairs={{0,3},{1,2},{2,1},{3,0},{4,7},{5,6},{6,5},{7,4},{8,11},{9,10},{10,... | collective-permute-start | bytes 49160 | tf_op jit(solution)/shard_map/ppermute | solution.py:260
  3.0 4.4 %collective-permute-start.1 = (bf16[64,128]{1,0:T(8,128)(2,1)}, bf16[64,128]{1,0:T(8,128)(2,1)S(1)}, u32[]{:S(2)}, u32[]{:S(2)}) collective-permute-start(bf16[64,128]{1,0:T(8,128)(2,1)} %bitcast.14), channel_id=1, source_target_pairs={{0,4},{1,5},{2,6},{3,7},{4,0},{5,1},{6,2},{7,3},{8,12},{9,13},{10,... | collective-permute-start | bytes 49160 | tf_op jit(solution)/shard_map/ppermute | solution.py:260
  4.9 6.1 %collective-permute-start.2 = (bf16[64,128]{1,0:T(8,128)(2,1)}, bf16[64,128]{1,0:T(8,128)(2,1)S(1)}, u32[]{:S(2)}, u32[]{:S(2)}) collective-permute-start(bf16[64,128]{1,0:T(8,128)(2,1)} %bitcast.15), channel_id=1, source_target_pairs={{0,7},{1,6},{2,5},{3,4},{4,3},{5,2},{6,1},{7,0},{8,15},{9,14},{10,... | collective-permute-start | bytes 49160 | tf_op jit(solution)/shard_map/ppermute | solution.py:260
  4.9 6.0 %copy-start.2 = (bf16[2,32,128]{2,1,0:T(8,128)(2,1)S(1)}, bf16[2,32,128]{2,1,0:T(8,128)(2,1)}, u32[]{:S(2)}) copy-start(bf16[2,32,128]{2,1,0:T(8,128)(2,1)} %param.7) | copy-start | bytes 49156
  5.0 35.1 %copy-start.4 = (s32[2,256]{1,0:T(2,128)S(1)}, s32[2,256]{1,0:T(2,128)}, u32[]{:S(2)}) copy-start(s32[2,256]{1,0:T(2,128)} %candidates_ref.1) | copy-start | bytes 6148
  11.9 13.2 %all-to-all-start = ((bf16[8,256,128]{2,1,0:T(8,128)(2,1)}), bf16[8,256,128]{2,1,0:T(8,128)(2,1)S(1)}, u32[]{:S(2)}, u32[]{:S(2)}) async-start(bf16[8,256,128]{2,1,0:T(8,128)(2,1)} %spread.1), calls=%async_computation | async-start | bytes 1048576 | tf_op jit(solution)/shard_map/all_to_all | solution.py:267
  16.4 6.5 %collective-permute-start.3 = (bf16[512,128]{1,0:T(8,128)(2,1)S(1)}, bf16[512,128]{1,0:T(8,128)(2,1)S(1)}, u32[]{:S(2)}, u32[]{:S(2)}) collective-permute-start(bf16[512,128]{1,0:T(8,128)(2,1)S(1)} %gather.1.after_ref.own), channel_id=1, source_target_pairs={{0,64},{32,96},{64,0},{96,32},{1,65},{33,97},{65,1},{97,33},{2,66}... | collective-permute-start | bytes 393224 | tf_op jit(solution)/shard_map/ppermute | solution.py:273
  20.0 3.0 %collective-permute-start.5 = (bf16[512,128]{1,0:T(8,128)(2,1)S(1)}, bf16[512,128]{1,0:T(8,128)(2,1)S(1)}, u32[]{:S(2)}, u32[]{:S(2)}) collective-permute-start(bf16[512,128]{1,0:T(8,128)(2,1)S(1)} %gather.1.after_ref.own), channel_id=1, source_target_pairs={{0,32},{32,0},{64,96},{96,64},{1,33},{33,1},{65,97},{97,65},{2,34}... | collective-permute-start | bytes 393224 | tf_op jit(solution)/shard_map/ppermute | solution.py:272
  22.9 4.0 %collective-permute-start.4 = (bf16[512,128]{1,0:T(8,128)(2,1)S(1)}, bf16[512,128]{1,0:T(8,128)(2,1)S(1)}, u32[]{:S(2)}, u32[]{:S(2)}) collective-permute-start(bf16[512,128]{1,0:T(8,128)(2,1)S(1)} %collective-permute-done.3.far), channel_id=1, source_target_pairs={{0,32},{32,0},{64,96},{96,64},{1,33},{33,1},{65,97},{97,65},{2,34}... | collective-permute-start | bytes 393224 | tf_op jit(solution)/shard_map/ppermute | solution.py:274

commit v9 on v8

--- a/solution.py
+++ b/solution.py
@@ -181,7 +181,7 @@
             at = b * rows + m * passages
             scratch[at : at + passages, :] = held
 
-    chunk, span = 1024, 128
+    chunk, span = 2048, 128
     for k in range(0, tokens.shape[0], chunk):
         wanted = tokens[k : k + chunk, :]
         best = None

time: 40.9 us -> 41 us (level)
  no operation moved by 1% of the time
where the time goes in v9:
time: 41 us; the launch traced here: 40.7 us
  starting transfers between devices  12.9 us (31%)
  blocking collectives  12 us (29%)
  waiting for transfers between devices  8.69 us (21%)
  Pallas kernels  6.94 us (17%)
    all_to_all x1, blocking collectives, shards(): lax.all_to_all(table, 'wide', split_axis=0, concat_axis=0, tiled=True)  12 us
    ppermute x3, starting transfers between devices, shards(): lax.ppermute(plain, 'wide', [(i, i ^ step) for i in range(owners)])  4.86 us
    all_to_all x1, starting transfers between devices, shards(): lax.all_to_all(sent, 'wide', split_axis=0, concat_axis=0, axis_index_grou...  4.47 us
    ppermute x3, waiting for transfers between devices, shards(): lax.ppermute(plain, 'wide', [(i, i ^ step) for i in range(owners)])  3.59 us
    ppermute x1, starting transfers between devices, shards(): far = lax.ppermute(vecs, 'grp', [(i, i ^ 2) for i in range(4)])  3.58 us
    ppermute x1, waiting for transfers between devices, shards(): far = lax.ppermute(vecs, 'grp', [(i, i ^ 2) for i in range(4)])  2.94 us
    all_to_all x1, waiting for transfers between devices, shards(): lax.all_to_all(sent, 'wide', split_axis=0, concat_axis=0, axis_index_grou...  2.15 us
    pallas_call x1, Pallas kernels, shards(): pl.pallas_call(first_kernel, out_shape=best_shape, in_specs=[VMEM] * 5, o...  1.83 us
  transfers between devices with their start and end apart: 7, of which 3 were waited for; matrix products, arithmetic and copies ran while one was open for 0% of the time, Pallas kernels for 10%

profile of v9, /device:TPU:0, one launch (start us, length us, event | category | flops | bytes accessed | tf_op | source)
XLA Modules:
  0.0 40.7 jit_solution(2383618864424190357)
XLA Ops:
  0.0 0.0 slice-start
  0.0 0.0 copy-start
  0.0 0.0 copy-start.1
  0.0 0.0 copy-start.5
  0.0 0.0 slice-start.1
  0.0 0.0 copy-start.3
  0.0 2.9 %collective-permute-start = (bf16[64,128]{1,0:T(8,128)(2,1)}, bf16[64,128]{1,0:T(8,128)(2,1)S(1)}, u32[]{:S(2)}, u32[]{:S(2)}) collective-permute-start(bf16[64,128]{1,0:T(8,128)(2,1)} %bitcast.13), channel_id=1, source_target_pairs={{0,3},{1,2},{2,1},{3,0},{4,7},{5,6},{6,5},{7,4},{8,11},{9,10},{10,... | collective-permute-start | bytes 49160 | tf_op jit(solution)/shard_map/ppermute | solution.py:260
  3.0 1.9 %collective-permute-start.1 = (bf16[64,128]{1,0:T(8,128)(2,1)}, bf16[64,128]{1,0:T(8,128)(2,1)S(1)}, u32[]{:S(2)}, u32[]{:S(2)}) collective-permute-start(bf16[64,128]{1,0:T(8,128)(2,1)} %bitcast.14), channel_id=1, source_target_pairs={{0,4},{1,5},{2,6},{3,7},{4,0},{5,1},{6,2},{7,3},{8,12},{9,13},{10,... | collective-permute-start | bytes 49160 | tf_op jit(solution)/shard_map/ppermute | solution.py:260
  4.9 0.0 collective-permute-start.2
  4.9 0.1 members.1
  4.9 0.0 copy-start.2
  5.0 0.0 copy-start.4
  5.0 0.0 copy-done
  5.0 0.0 copy-done.1
  5.0 0.0 copy-done.5
  5.0 0.6 %residual.1 = (f32[512,128]{1,0:T(8,128)S(1)}, s32[16,128]{1,0:T(8,128)S(1)}) custom-call(s32[16,1024]{1,0:T(8,128)S(1)} %copy-done, bf16[256,128]{1,0:T(8,128)(2,1)S(1)} %copy-done.1, s32[1,16]{1,0:T(1,128)S(1)} %bitcast.17), custom_call_target="tpu_custom_call" | custom-call | flops 16777216 | bytes 131072 | tf_op jit(solution)/shard_map/residual/pallas_call | solution.py:143
  5.6 0.0 slice-done
  5.6 0.0 slice-done.1
  5.6 0.0 copy-done.3
  5.6 1.7 %gather.1.after_ref.own = bf16[512,128]{1,0:T(8,128)(2,1)S(1)} custom-call(s32[16,32]{1,0:T(8,128)S(1)} %copy-done.3, f32[512,128]{1,0:T(8,128)S(1)} %get-tuple-element.11.residual, bf16[32768,128]{1,0:T(8,128)(2,1)S(1)} %bitcast.8), custom_call_target="tpu_custom_call" | custom-call | flops 524288 | bytes 8388608 | tf_op jit(solution)/shard_map/gather/pallas_call | solution.py:155
  7.3 0.0 collective-permute-done.turned_ref
  7.3 0.0 collective-permute-done.1.paired_ref
  7.3 3.6 %collective-permute-done.2.both_ref = bf16[64,128]{1,0:T(8,128)(2,1)S(1)} collective-permute-done((bf16[64,128]{1,0:T(8,128)(2,1)}, bf16[64,128]{1,0:T(8,128)(2,1)S(1)}, u32[]{:S(2)}, u32[]{:S(2)}) %collective-permute-start.2) | collective-permute-done | bytes 16416 | tf_op jit(solution)/shard_map/ppermute | solution.py:260
  10.9 0.0 copy-done.2
  10.9 1.0 %spread.1 = bf16[8,256,128]{2,1,0:T(8,128)(2,1)} custom-call(bf16[64,128]{1,0:T(8,128)(2,1)S(1)} %bitcast.16, bf16[64,128]{1,0:T(8,128)(2,1)S(1)} %collective-permute-done.turned_ref, bf16[64,128]{1,0:T(8,128)(2,1)S(1)} %collective-permute-done.1.paired_ref, bf16[64,128]{1,0:T(8,128)(2,1)S(1)} %collective-permute-done.2.both_ref, ...), custom_call_target="tpu_custom_call" | custom-call | bytes 524288 | tf_op jit(solution)/shard_map/spread/pallas_call | solution.py:68
  11.9 4.5 %all-to-all-start = ((bf16[8,256,128]{2,1,0:T(8,128)(2,1)}), bf16[8,256,128]{2,1,0:T(8,128)(2,1)S(1)}, u32[]{:S(2)}, u32[]{:S(2)}) async-start(bf16[8,256,128]{2,1,0:T(8,128)(2,1)} %spread.1), calls=%async_computation | async-start | bytes 1048576 | tf_op jit(solution)/shard_map/all_to_all | solution.py:267
  16.4 3.6 %collective-permute-start.3 = (bf16[512,128]{1,0:T(8,128)(2,1)S(1)}, bf16[512,128]{1,0:T(8,128)(2,1)S(1)}, u32[]{:S(2)}, u32[]{:S(2)}) collective-permute-start(bf16[512,128]{1,0:T(8,128)(2,1)S(1)} %gather.1.after_ref.own), channel_id=1, source_target_pairs={{0,64},{32,96},{64,0},{96,32},{1,65},{33,97},{65,1},{97,33},{2,66}... | collective-permute-start | bytes 393224 | tf_op jit(solution)/shard_map/ppermute | solution.py:273
  20.0 0.0 collective-permute-start.5
  20.0 2.9 %collective-permute-done.3.far = bf16[512,128]{1,0:T(8,128)(2,1)S(1)} collective-permute-done((bf16[512,128]{1,0:T(8,128)(2,1)S(1)}, bf16[512,128]{1,0:T(8,128)(2,1)S(1)}, u32[]{:S(2)}, u32[]{:S(2)}) %collective-permute-start.3) | collective-permute-done | bytes 131104 | tf_op jit(solution)/shard_map/ppermute | solution.py:273
  22.9 0.0 collective-permute-start.4
  22.9 0.0 collective-permute-done.5.other
  22.9 2.2 %all-to-all-done = bf16[8,256,128]{2,1,0:T(8,128)(2,1)S(1)} async-done(((bf16[8,256,128]{2,1,0:T(8,128)(2,1)}), bf16[8,256,128]{2,1,0:T(8,128)(2,1)S(1)}, u32[]{:S(2)}, u32[]{:S(2)}) %all-to-all-start) | async-done | bytes 524320 | tf_op jit(solution)/shard_map/all_to_all | solution.py:267
  25.1 1.8 %score_first.1.before = f32[16,2048]{1,0:T(8,128)S(1)} custom-call(s32[16,128]{1,0:T(8,128)S(1)} %get-tuple-element.10.live, bf16[2048,128]{1,0:T(8,128)(2,1)S(1)} %bitcast.9, bf16[512,128]{1,0:T(8,128)(2,1)S(1)} %gather.1.after_ref.own, bf16[512,128]{1,0:T(8,128)(2,1)S(1)} %collective-permute-done.5.other, bf16[512,128]{1,0:T(8,128)(2,1)S(1)} %collective-permute-done.3.far), custom_call_target="tpu_custom_call" | custom-call | flops 805306368 | bytes 917504 | tf_op jit(solution)/shard_map/score_first/pallas_call | solution.py:277
  26.9 0.0 collective-permute-done.4.vecs
  26.9 1.1 %score_last.1 = f32[32,128]{1,0:T(8,128)S(1)} custom-call(s32[16,128]{1,0:T(8,128)S(1)} %get-tuple-element.10.live, bf16[2048,128]{1,0:T(8,128)(2,1)S(1)} %bitcast.10, bf16[512,128]{1,0:T(8,128)(2,1)S(1)} %collective-permute-done.4.vecs, f32[16,2048]{1,0:T(8,128)S(1)} %score_first.1.before, bf16[64,2048]{1,0:T(8,128)(2,1)S(1)} %members.1), custom_call_target="tpu_custom_call" | custom-call | flops 268435456 | bytes 655360 | tf_op jit(solution)/shard_map/score_last/pallas_call | solution.py:287
  28.0 12.0 %all_to_all.16 = f32[32,1,128]{2,1,0:T(1,128)S(1)} all-to-all(f32[32,1,128]{2,1,0:T(1,128)S(1)} %bitcast.11), channel_id=1, replica_groups=mesh['grp'=4,'wide'=32] {'wide'}, dimensions={0} | all-to-all | bytes 32768 | tf_op jit(solution)/shard_map/all_to_all | solution.py:297
  40.0 0.0 copy-done.4
  40.0 0.7 %pick.1 = f32[2,256]{1,0:T(2,128)} custom-call(f32[32,128]{1,0:T(8,128)S(1)} %bitcast.12, s32[2,256]{1,0:T(2,128)S(1)} %copy-done.4), custom_call_target="tpu_custom_call" | custom-call | flops 32768 | bytes 16384 | tf_op jit(solution)/shard_map/pick/pallas_call | solution.py:318
  (1 shorter events, 0.0 us)
Async XLA Ops:
  0.0 5.6 %slice-start = ((s8[8388608]{0:T(1024)(128)(4,1)}), s8[4194304]{0:T(1024)(128)(4,1)S(1)}, s32[]{:S(2)}) async-start(s8[8388608]{0:T(1024)(128)(4,1)} %bitcast.7), calls=%async_computation.2 | async-start | bytes 8388608
  0.0 5.0 %copy-start = (s32[16,1024]{1,0:T(8,128)S(1)}, s32[16,1024]{1,0:T(8,128)}, u32[]{:S(2)}) copy-start(s32[16,1024]{1,0:T(8,128)} %codes) | copy-start | bytes 196612
  0.0 5.0 %copy-start.1 = (bf16[256,128]{1,0:T(8,128)(2,1)S(1)}, bf16[256,128]{1,0:T(8,128)(2,1)}, u32[]{:S(2)}) copy-start(bf16[256,128]{1,0:T(8,128)(2,1)} %book.1) | copy-start | bytes 196612
  0.0 5.0 %copy-start.5 = (s32[16]{0:T(128)S(1)}, s32[16]{0:T(128)}, u32[]{:S(2)}) copy-start(s32[16]{0:T(128)} %param.12) | copy-start | bytes 196
  0.0 5.6 %slice-start.1 = ((s8[8388608]{0:T(1024)(128)(4,1)}), s8[4194304]{0:T(1024)(128)(4,1)S(1)}, s32[]{:S(2)}) async-start(s8[8388608]{0:T(1024)(128)(4,1)} %bitcast.7), calls=%async_computation.3 | async-start | bytes 8388608
  0.0 5.6 %copy-start.3 = (s32[16,32]{1,0:T(8,128)S(1)}, s32[16,32]{1,0:T(8,128)}, u32[]{:S(2)}) copy-start(s32[16,32]{1,0:T(8,128)} %ids.1) | copy-start | bytes 6148
  0.0 7.3 %collective-permute-start = (bf16[64,128]{1,0:T(8,128)(2,1)}, bf16[64,128]{1,0:T(8,128)(2,1)S(1)}, u32[]{:S(2)}, u32[]{:S(2)}) collective-permute-start(bf16[64,128]{1,0:T(8,128)(2,1)} %bitcast.13), channel_id=1, source_target_pairs={{0,3},{1,2},{2,1},{3,0},{4,7},{5,6},{6,5},{7,4},{8,11},{9,10},{10,... | collective-permute-start | bytes 49160 | tf_op jit(solution)/shard_map/ppermute | solution.py:260
  3.0 4.4 %collective-permute-start.1 = (bf16[64,128]{1,0:T(8,128)(2,1)}, bf16[64,128]{1,0:T(8,128)(2,1)S(1)}, u32[]{:S(2)}, u32[]{:S(2)}) collective-permute-start(bf16[64,128]{1,0:T(8,128)(2,1)} %bitcast.14), channel_id=1, source_target_pairs={{0,4},{1,5},{2,6},{3,7},{4,0},{5,1},{6,2},{7,3},{8,12},{9,13},{10,... | collective-permute-start | bytes 49160 | tf_op jit(solution)/shard_map/ppermute | solution.py:260
  4.9 6.1 %collective-permute-start.2 = (bf16[64,128]{1,0:T(8,128)(2,1)}, bf16[64,128]{1,0:T(8,128)(2,1)S(1)}, u32[]{:S(2)}, u32[]{:S(2)}) collective-permute-start(bf16[64,128]{1,0:T(8,128)(2,1)} %bitcast.15), channel_id=1, source_target_pairs={{0,7},{1,6},{2,5},{3,4},{4,3},{5,2},{6,1},{7,0},{8,15},{9,14},{10,... | collective-permute-start | bytes 49160 | tf_op jit(solution)/shard_map/ppermute | solution.py:260
  4.9 6.0 %copy-start.2 = (bf16[2,32,128]{2,1,0:T(8,128)(2,1)S(1)}, bf16[2,32,128]{2,1,0:T(8,128)(2,1)}, u32[]{:S(2)}) copy-start(bf16[2,32,128]{2,1,0:T(8,128)(2,1)} %param.7) | copy-start | bytes 49156
  5.0 35.1 %copy-start.4 = (s32[2,256]{1,0:T(2,128)S(1)}, s32[2,256]{1,0:T(2,128)}, u32[]{:S(2)}) copy-start(s32[2,256]{1,0:T(2,128)} %candidates_ref.1) | copy-start | bytes 6148
  11.9 13.2 %all-to-all-start = ((bf16[8,256,128]{2,1,0:T(8,128)(2,1)}), bf16[8,256,128]{2,1,0:T(8,128)(2,1)S(1)}, u32[]{:S(2)}, u32[]{:S(2)}) async-start(bf16[8,256,128]{2,1,0:T(8,128)(2,1)} %spread.1), calls=%async_computation | async-start | bytes 1048576 | tf_op jit(solution)/shard_map/all_to_all | solution.py:267
  16.4 6.5 %collective-permute-start.3 = (bf16[512,128]{1,0:T(8,128)(2,1)S(1)}, bf16[512,128]{1,0:T(8,128)(2,1)S(1)}, u32[]{:S(2)}, u32[]{:S(2)}) collective-permute-start(bf16[512,128]{1,0:T(8,128)(2,1)S(1)} %gather.1.after_ref.own), channel_id=1, source_target_pairs={{0,64},{32,96},{64,0},{96,32},{1,65},{33,97},{65,1},{97,33},{2,66}... | collective-permute-start | bytes 393224 | tf_op jit(solution)/shard_map/ppermute | solution.py:273
  20.0 3.0 %collective-permute-start.5 = (bf16[512,128]{1,0:T(8,128)(2,1)S(1)}, bf16[512,128]{1,0:T(8,128)(2,1)S(1)}, u32[]{:S(2)}, u32[]{:S(2)}) collective-permute-start(bf16[512,128]{1,0:T(8,128)(2,1)S(1)} %gather.1.after_ref.own), channel_id=1, source_target_pairs={{0,32},{32,0},{64,96},{96,64},{1,33},{33,1},{65,97},{97,65},{2,34}... | collective-permute-start | bytes 393224 | tf_op jit(solution)/shard_map/ppermute | solution.py:272
  22.9 4.0 %collective-permute-start.4 = (bf16[512,128]{1,0:T(8,128)(2,1)S(1)}, bf16[512,128]{1,0:T(8,128)(2,1)S(1)}, u32[]{:S(2)}, u32[]{:S(2)}) collective-permute-start(bf16[512,128]{1,0:T(8,128)(2,1)S(1)} %collective-permute-done.3.far), channel_id=1, source_target_pairs={{0,32},{32,0},{64,96},{96,64},{1,33},{33,1},{65,97},{97,65},{2,34}... | collective-permute-start | bytes 393224 | tf_op jit(solution)/shard_map/ppermute | solution.py:274
